TPU v7x, 512 devices: a whole 4x8x8 slice. The times are simulated.
512 devices in a mesh: rep: 8 (over x, core), row: 64 (over z, y).
Axes of the slice: x: 4, y: 8, z: 8, core: 2. Of those that a mesh axis runs over, the one named last changes fastest.
Arguments:
- weight: bfloat16 [8192, 384], P('row'), may hold values from -0.0625 to 0.0625
- first_moment: bfloat16 [8, 8192, 384], P('rep', 'row'), may hold values from -0.29882812 to 0.29882812
- second_moment: bfloat16 [8, 8192, 384], P('rep', 'row'), may hold values from 2.9921532e-05 to 0.0029907227
- token_ids: int32 [8, 4, 1024], P('rep'), may hold values from 0 to 1535
- shared_inputs: bfloat16 [1024, 8192], P(None, 'row'), may hold values from -6 to 6
- private_inputs: bfloat16 [8, 512, 8192], P('rep', None, 'row'), may hold values from -6 to 6
- shared_targets: bfloat16 [1024, 384], replicated, may hold values from -6 to 6
- private_targets: bfloat16 [8, 512, 384], P('rep'), may hold values from -6 to 6
Outputs:
- merged: float32 [8192, 384], P(('row', 'rep'))
All inputs are finite; a program needn't handle non-finite values.
Results may differ from a plain program's by a relative error of at most 0.0005.
The roundings to bfloat16 on the way count: a program that leaves them out, or rounds other values in their place, can miss the bound.
Values sent between devices are 32-bit elements; how exact they have to be, the bound alone decides.
No kernel may reach another device: no remote copies, remote signals or barrier semaphores. Data moves between devices by JAX's collectives and lax.ppermute only.
A program may use at most 64 MiB of HBM per device.

v0:
```python
import jax
import jax.numpy as jnp
from jax import lax
from jax.sharding import Mesh
from jax.sharding import PartitionSpec as P

ROW = ("row_0", "row_1")
REP = ("rep_0", "rep_1")
ROW_REP = ("row_0", "row_1", "rep_0", "rep_1")


learn_rate = 0.001
beta_one = 0.9
beta_two = 0.95
adam_eps = 1e-08
weight_decay = 0.1
norm_eps = 1e-06


def in_blocks(shard, dim, devices):
    before, after = (shard.shape[:dim], shard.shape[dim + 1 :])
    return jnp.moveaxis(shard.reshape(*before, devices, -1, *after), dim, 0)


def sent_and_summed(shard, axis, dim):
    tiles = in_blocks(shard, dim, lax.axis_size(axis))
    arrived = lax.all_to_all(tiles, axis, split_axis=0, concat_axis=0, tiled=True)
    return arrived.sum(axis=0)


def padded_to(lines, devices):
    spare = -lines.shape[0] % devices
    if not spare:
        return lines
    return jnp.concatenate([lines, jnp.zeros((spare, *lines.shape[1:]), lines.dtype)])


def from_everyone(shard, axis):
    copies = jnp.broadcast_to(shard, (lax.axis_size(axis), *shard.shape))
    return lax.all_to_all(copies, axis, split_axis=0, concat_axis=0, tiled=True)


def in_order(tiles, dim):
    dims = list(tiles.shape[1:])
    dims[dim] *= tiles.shape[0]
    return jnp.moveaxis(tiles, 0, dim).reshape(dims)


def gathered_copies(shard, axis, dim):
    tiles = from_everyone(shard, axis)
    return in_order(tiles, dim)


def nested_sum(shard, axes):
    lines = shard.reshape(-1, shard.shape[-1])
    own = sent_and_summed(padded_to(lines, lax.axis_size(axes)), axes, 0)
    whole = gathered_copies(own, axes, 0)
    return whole[: len(lines)].reshape(shard.shape)


def gathered_by_axis(shard, axes, dim):
    far, near = axes
    leading = from_everyone(shard, far)
    tiles = jnp.swapaxes(from_everyone(leading, near), 0, 1)
    return in_order(tiles.reshape(-1, *shard.shape), dim)


def one_axis_at_a_time(shard, axes):
    for axis in axes:
        shard = lax.psum(shard, axis)
    return shard


def combine_pair(lower_vec, upper_vec, cross_dot, lower_norm, upper_norm):
    lower_coef = 1.0 - cross_dot / (2.0 * (lower_norm + norm_eps))
    upper_coef = 1.0 - cross_dot / (2.0 * (upper_norm + norm_eps))
    return lower_coef * lower_vec + upper_coef * upper_vec


def local_training(
    weight,
    first_moment,
    second_moment,
    token_ids,
    shared_inputs,
    private_inputs,
    shared_targets,
    private_targets,
):
    input_table = jnp.concatenate([shared_inputs, private_inputs[0]], axis=0)
    target_table = jnp.concatenate([shared_targets, private_targets[0]], axis=0).astype(jnp.float32)
    weight_start = weight.astype(jnp.float32)
    moment_one = first_moment[0].astype(jnp.float32)
    moment_two = second_moment[0].astype(jnp.float32)
    update_sum = jnp.zeros(weight_start.shape, jnp.float32)
    tokens_count = token_ids.shape[2]
    for step_index in range(token_ids.shape[1]):
        chosen = token_ids[0, step_index]
        tok_rows = jnp.take(input_table, chosen, axis=0)
        targets = jnp.take(target_table, chosen, axis=0)
        weight_now = weight_start - learn_rate * update_sum
        weight_bf = weight_now.astype(jnp.bfloat16)
        partial_value = jnp.dot(tok_rows, weight_bf, preferred_element_type=jnp.float32)
        output = nested_sum(partial_value, ROW)
        residual = (output - targets).astype(jnp.bfloat16)
        gradient = (
            lax.dot_general(
                tok_rows, residual, (((0,), (0,)), ((), ())), preferred_element_type=jnp.float32
            )
            / tokens_count
        )
        moment_one = beta_one * moment_one + (1.0 - beta_one) * gradient
        moment_two = beta_two * moment_two + (1.0 - beta_two) * gradient * gradient
        direction = moment_one / (jnp.sqrt(moment_two) + adam_eps) + weight_decay * weight_now
        update_sum = update_sum + direction
    return update_sum


def on_device(
    weight,
    first_moment,
    second_moment,
    token_ids,
    shared_inputs,
    private_inputs,
    shared_targets,
    private_targets,
):
    update_sum = local_training(
        weight,
        first_moment,
        second_moment,
        token_ids,
        shared_inputs,
        private_inputs,
        shared_targets,
        private_targets,
    )
    replica_count = lax.axis_size(REP)
    level_count = replica_count.bit_length() - 1
    replica = lax.axis_index(REP)
    local_rows, columns = update_sum.shape
    block_rows = local_rows // replica_count
    gathered = gathered_by_axis(update_sum[None], ("rep_0", "rep_1"), 0)
    flat = gathered.reshape(replica_count, local_rows * columns)
    partial_gram = lax.dot_general(
        flat,
        flat,
        (((1,), (1,)), ((), ())),
        precision=lax.Precision.HIGHEST,
        preferred_element_type=jnp.float32,
    )
    gram = one_axis_at_a_time(partial_gram, ROW)
    mixing = jnp.eye(replica_count, dtype=jnp.float32)
    for tree_level in range(level_count):
        lower_rows = mixing[0::2]
        upper_rows = mixing[1::2]
        lower_image = jnp.dot(lower_rows, gram, precision=lax.Precision.HIGHEST)
        upper_image = jnp.dot(upper_rows, gram, precision=lax.Precision.HIGHEST)
        cross_dot = jnp.sum(lower_image * upper_rows, axis=1, keepdims=True)
        lower_norm = jnp.sum(lower_image * lower_rows, axis=1, keepdims=True)
        upper_norm = jnp.sum(upper_image * upper_rows, axis=1, keepdims=True)
        mixing = combine_pair(lower_rows, upper_rows, cross_dot, lower_norm, upper_norm)
    own_block = lax.dynamic_slice_in_dim(gathered, replica * block_rows, block_rows, 1)
    own_flat = own_block.reshape(replica_count, block_rows * columns)
    merged = jnp.dot(mixing, own_flat, precision=lax.Precision.HIGHEST)
    return merged.reshape(block_rows, columns)


def solution(mesh):
    torus = Mesh(mesh.devices.reshape(4, 2, 8, 8), ("rep_0", "rep_1", "row_0", "row_1"))
    placed = (
        P(ROW, None),
        P(REP, ROW, None),
        P(REP, ROW, None),
        P(REP, None, None),
        P(None, ROW),
        P(REP, None, ROW),
        P(),
        P(REP, None, None),
    )
    return jax.shard_map(
        on_device, mesh=torus, in_specs=placed, out_specs=P(ROW_REP, None), check_vma=False
    )
```

profile of v0, /device:TPU:1, one launch (start us, length us, event | category | flops | bytes accessed | tf_op | source)
XLA Modules:
  0.0 463.1 jit_solution(16146191925963480883)
XLA Ops:
  2.0 3.2 gather_fusion
  5.6 55.9 %all_to_all.53 = f32[64,16,384]{2,1,0:T(8,128)S(1)} all-to-all(f32[64,16,384]{2,1,0:T(8,128)S(1)} %bitcast.121), channel_id=1, replica_groups=mesh['rep_0'=4,'rep_1'=2,'row_0'=8,'row_1'=8] {'row_0','row_1'}, dimensions={0} | all-to-all | bytes 3145728 | tf_op jit(solution)/shard_map/all_to_all | solution.py:27
  62.9 8.8 %all-to-all-start.1 = ((f32[64,16,384]{2,1,0:T(8,128)}), f32[64,16,384]{2,1,0:T(8,128)}, u32[]{:S(2)}, u32[]{:S(2)}) async-start(f32[64,16,384]{2,1,0:T(8,128)} %broadcast_in_dim.46), calls=%async_computation.1 | async-start | bytes 3145728 | tf_op jit(solution)/shard_map/all_to_all | solution.py:40
  73.0 4.8 %gather_fusion.1 = f32[1024,384]{1,0:T(8,128)} fusion(f32[1536,384]{1,0:T(8,128)S(1)} %maximum_convert_fusion, s32[1024]{0:T(1024)S(1)} %fusion.25), kind=kCustom, calls=%fused_computation.1.clone | custom fusion | bytes 3149824 | tf_op jit(solution)/shard_map/jit(_take)/gather | solution.py:100
  81.0 27.0 %all-to-all-done.1 = f32[64,16,384]{2,1,0:T(8,128)} async-done(((f32[64,16,384]{2,1,0:T(8,128)}), f32[64,16,384]{2,1,0:T(8,128)}, u32[]{:S(2)}, u32[]{:S(2)}) %all-to-all-start.1) | async-done | bytes 1572896 | tf_op jit(solution)/shard_map/all_to_all | solution.py:40
  111.3 43.3 %all_to_all.54 = f32[64,16,384]{2,1,0:T(8,128)} all-to-all(f32[64,16,384]{2,1,0:T(8,128)S(1)} %bitcast.122), channel_id=1, replica_groups=mesh['rep_0'=4,'rep_1'=2,'row_0'=8,'row_1'=8] {'row_0','row_1'}, dimensions={0} | all-to-all | bytes 3145728 | tf_op jit(solution)/shard_map/all_to_all | solution.py:27
  157.5 10.7 %all-to-all-start.3 = ((f32[64,16,384]{2,1,0:T(8,128)}), f32[64,16,384]{2,1,0:T(8,128)}, u32[]{:S(2)}, u32[]{:S(2)}) async-start(f32[64,16,384]{2,1,0:T(8,128)} %broadcast_in_dim.47), calls=%async_computation.3 | async-start | bytes 3145728 | tf_op jit(solution)/shard_map/all_to_all | solution.py:40
  168.2 4.8 %gather_fusion.3 = f32[1024,384]{1,0:T(8,128)} fusion(f32[1536,384]{1,0:T(8,128)S(1)} %maximum_convert_fusion, s32[1024]{0:T(1024)S(1)} %fusion.26), kind=kCustom, calls=%fused_computation.5.clone | custom fusion | bytes 3149824 | tf_op jit(solution)/shard_map/jit(_take)/gather | solution.py:100
  176.1 26.7 %all-to-all-done.3 = f32[64,16,384]{2,1,0:T(8,128)} async-done(((f32[64,16,384]{2,1,0:T(8,128)}), f32[64,16,384]{2,1,0:T(8,128)}, u32[]{:S(2)}, u32[]{:S(2)}) %all-to-all-start.3) | async-done | bytes 1572896 | tf_op jit(solution)/shard_map/all_to_all | solution.py:40
  206.5 45.4 %all_to_all.55 = f32[64,16,384]{2,1,0:T(8,128)} all-to-all(f32[64,16,384]{2,1,0:T(8,128)S(1)} %bitcast.124), channel_id=1, replica_groups=mesh['rep_0'=4,'rep_1'=2,'row_0'=8,'row_1'=8] {'row_0','row_1'}, dimensions={0} | all-to-all | bytes 3145728 | tf_op jit(solution)/shard_map/all_to_all | solution.py:27
  254.7 12.2 %all-to-all-start.5 = ((f32[64,16,384]{2,1,0:T(8,128)}), f32[64,16,384]{2,1,0:T(8,128)}, u32[]{:S(2)}, u32[]{:S(2)}) async-start(f32[64,16,384]{2,1,0:T(8,128)} %broadcast_in_dim.48), calls=%async_computation.5 | async-start | bytes 3145728 | tf_op jit(solution)/shard_map/all_to_all | solution.py:40
  266.9 4.8 %gather_fusion.5 = f32[1024,384]{1,0:T(8,128)} fusion(f32[1536,384]{1,0:T(8,128)S(1)} %maximum_convert_fusion, s32[1024]{0:T(1024)S(1)} %fusion.27), kind=kCustom, calls=%fused_computation.6.clone | custom fusion | bytes 3149824 | tf_op jit(solution)/shard_map/jit(_take)/gather | solution.py:100
  271.6 4.3 gather_fusion.6
  276.0 25.4 %all-to-all-done.5 = f32[64,16,384]{2,1,0:T(8,128)} async-done(((f32[64,16,384]{2,1,0:T(8,128)}), f32[64,16,384]{2,1,0:T(8,128)}, u32[]{:S(2)}, u32[]{:S(2)}) %all-to-all-start.5) | async-done | bytes 1572896 | tf_op jit(solution)/shard_map/all_to_all | solution.py:40
  304.9 45.4 %all_to_all.56 = f32[64,16,384]{2,1,0:T(8,128)} all-to-all(f32[64,16,384]{2,1,0:T(8,128)S(1)} %bitcast.125), channel_id=1, replica_groups=mesh['rep_0'=4,'rep_1'=2,'row_0'=8,'row_1'=8] {'row_0','row_1'}, dimensions={0} | all-to-all | bytes 3145728 | tf_op jit(solution)/shard_map/all_to_all | solution.py:27
  353.1 11.7 %all-to-all-start.7 = ((f32[64,16,384]{2,1,0:T(8,128)}), f32[64,16,384]{2,1,0:T(8,128)}, u32[]{:S(2)}, u32[]{:S(2)}) async-start(f32[64,16,384]{2,1,0:T(8,128)} %broadcast_in_dim.49), calls=%async_computation.7 | async-start | bytes 3145728 | tf_op jit(solution)/shard_map/all_to_all | solution.py:40
  364.8 4.8 %gather_fusion.7 = f32[1024,384]{1,0:T(8,128)} fusion(f32[1536,384]{1,0:T(8,128)S(1)} %maximum_convert_fusion, s32[1024]{0:T(1024)S(1)} %fusion.28), kind=kCustom, calls=%fused_computation.7.clone | custom fusion | bytes 3149824 | tf_op jit(solution)/shard_map/jit(_take)/gather | solution.py:100
  369.6 29.8 %all-to-all-done.7 = f32[64,16,384]{2,1,0:T(8,128)} async-done(((f32[64,16,384]{2,1,0:T(8,128)}), f32[64,16,384]{2,1,0:T(8,128)}, u32[]{:S(2)}, u32[]{:S(2)}) %all-to-all-start.7) | async-done | bytes 1572896 | tf_op jit(solution)/shard_map/all_to_all | solution.py:40
  403.5 3.5 all-to-all-start.8
  407.1 8.2 %all-to-all-done.8 = f32[4,1,128,384]{3,2,1,0:T(8,128)S(1)} async-done(((f32[4,1,128,384]{3,2,1,0:T(8,128)}), f32[4,1,128,384]{3,2,1,0:T(8,128)S(1)}, u32[]{:S(2)}, u32[]{:S(2)}) %all-to-all-start.8) | async-done | bytes 786464 | tf_op jit(solution)/shard_map/all_to_all | solution.py:40
  415.4 12.7 %all_to_all.57 = f32[2,4,1,128,384]{4,3,1,2,0:T(8,128)S(1)} all-to-all(f32[2,4,1,128,384]{4,3,1,2,0:T(8,128)S(1)} %broadcast_in_dim.51), channel_id=1, replica_groups=mesh['rep_0'=4,'rep_1'=2,'row_0'=8,'row_1'=8] {'rep_1'}, dimensions={0} | all-to-all | bytes 3145728 | tf_op jit(solution)/shard_map/all_to_all | solution.py:40
  429.2 3.5 fusion.70
  432.7 12.1 %psum.14 = f32[8,8]{1,0:T(8,128)S(1)} all-reduce(f32[8,8]{1,0:T(8,128)S(1)} %fusion.70), channel_id=1, replica_groups=mesh['rep_0'=4,'rep_1'=2,'row_0'=8,'row_1'=8] {'row_0'}, use_global_device_ids=true, to_apply=%region_4.7 | all-reduce | flops 64 | bytes 512 | tf_op jit(solution)/shard_map/psum | solution.py:70
  444.8 11.9 %psum.15 = f32[8,8]{1,0:T(8,128)S(1)} all-reduce(f32[8,8]{1,0:T(8,128)S(1)} %psum.14), channel_id=1, replica_groups=mesh['rep_0'=4,'rep_1'=2,'row_0'=8,'row_1'=8] {'row_1'}, use_global_device_ids=true, to_apply=%region_5.8 | all-reduce | flops 64 | bytes 512 | tf_op jit(solution)/shard_map/psum | solution.py:70
  (98 shorter events, 39.3 us)
Async XLA Ops:
  0.9 4.3 copy-start
  62.9 8.8 %copy-start.10 = (bf16[1,512,384]{2,1,0:T(8,128)(2,1)S(1)}, bf16[1,512,384]{2,1,0:T(8,128)(2,1)}, u32[]{:S(2)}) copy-start(bf16[1,512,384]{2,1,0:T(8,128)(2,1)} %param.19) | copy-start | bytes 1179652
  62.9 45.1 %all-to-all-start.1 = ((f32[64,16,384]{2,1,0:T(8,128)}), f32[64,16,384]{2,1,0:T(8,128)}, u32[]{:S(2)}, u32[]{:S(2)}) async-start(f32[64,16,384]{2,1,0:T(8,128)} %broadcast_in_dim.46), calls=%async_computation.1 | async-start | bytes 3145728 | tf_op jit(solution)/shard_map/all_to_all | solution.py:40
  108.1 2.8 copy-start.1
  108.1 2.8 copy-start.4
  108.1 2.8 copy-start.7
  157.5 45.3 %all-to-all-start.3 = ((f32[64,16,384]{2,1,0:T(8,128)}), f32[64,16,384]{2,1,0:T(8,128)}, u32[]{:S(2)}, u32[]{:S(2)}) async-start(f32[64,16,384]{2,1,0:T(8,128)} %broadcast_in_dim.47), calls=%async_computation.3 | async-start | bytes 3145728 | tf_op jit(solution)/shard_map/all_to_all | solution.py:40
  202.8 2.2 copy-start.5
  202.8 2.2 copy-start.8
  205.0 0.9 copy-start.2
  205.6 0.8 copy-start.12
  205.7 0.8 copy-start.15
  254.7 46.6 %all-to-all-start.5 = ((f32[64,16,384]{2,1,0:T(8,128)}), f32[64,16,384]{2,1,0:T(8,128)}, u32[]{:S(2)}, u32[]{:S(2)}) async-start(f32[64,16,384]{2,1,0:T(8,128)} %broadcast_in_dim.48), calls=%async_computation.5 | async-start | bytes 3145728 | tf_op jit(solution)/shard_map/all_to_all | solution.py:40
  275.9 28.2 %copy-start.3 = (bf16[128,384]{1,0:T(8,128)(2,1)S(1)}, bf16[128,384]{1,0:T(8,128)(2,1)}, u32[]{:S(2)}) copy-start(bf16[128,384]{1,0:T(8,128)(2,1)} %param.12) | copy-start | bytes 294916
  275.9 28.2 %copy-start.6 = (bf16[1,128,384]{2,1,0:T(8,128)(2,1)S(1)}, bf16[1,128,384]{2,1,0:T(8,128)(2,1)}, u32[]{:S(2)}) copy-start(bf16[1,128,384]{2,1,0:T(8,128)(2,1)} %param.14) | copy-start | bytes 294916
  275.9 28.2 %copy-start.9 = (bf16[1,128,384]{2,1,0:T(8,128)(2,1)S(1)}, bf16[1,128,384]{2,1,0:T(8,128)(2,1)}, u32[]{:S(2)}) copy-start(bf16[1,128,384]{2,1,0:T(8,128)(2,1)} %param.13) | copy-start | bytes 294916
  275.9 28.2 %copy-start.11 = (bf16[1024,128]{1,0:T(8,128)(2,1)S(1)}, bf16[1024,128]{1,0:T(8,128)(2,1)}, u32[]{:S(2)}) copy-start(bf16[1024,128]{1,0:T(8,128)(2,1)} %gather_fusion.6) | copy-start | bytes 786436
  301.3 2.8 copy-start.13
  301.3 2.8 copy-start.16
  353.1 46.3 %all-to-all-start.7 = ((f32[64,16,384]{2,1,0:T(8,128)}), f32[64,16,384]{2,1,0:T(8,128)}, u32[]{:S(2)}, u32[]{:S(2)}) async-start(f32[64,16,384]{2,1,0:T(8,128)} %broadcast_in_dim.49), calls=%async_computation.7 | async-start | bytes 3145728 | tf_op jit(solution)/shard_map/all_to_all | solution.py:40
  369.6 32.0 %copy-start.14 = (f32[128,384]{1,0:T(8,128)S(1)}, f32[128,384]{1,0:T(8,128)}, u32[]{:S(2)}) copy-start(f32[128,384]{1,0:T(8,128)} %copy-done.12) | copy-start | bytes 589828
  369.6 32.0 %copy-start.17 = (f32[128,384]{1,0:T(8,128)S(1)}, f32[128,384]{1,0:T(8,128)}, u32[]{:S(2)}) copy-start(f32[128,384]{1,0:T(8,128)} %copy-done.15) | copy-start | bytes 589828
  369.6 32.0 %copy-start.19 = (f32[128,384]{1,0:T(8,128)S(1)}, f32[128,384]{1,0:T(8,128)}, u32[]{:S(2)}) copy-start(f32[128,384]{1,0:T(8,128)} %copy-done.18) | copy-start | bytes 589828
  403.5 11.8 %all-to-all-start.8 = ((f32[4,1,128,384]{3,2,1,0:T(8,128)}), f32[4,1,128,384]{3,2,1,0:T(8,128)S(1)}, u32[]{:S(2)}, u32[]{:S(2)}) async-start(f32[4,1,128,384]{3,2,1,0:T(8,128)} %broadcast_in_dim.50), calls=%async_computation.8 | async-start | bytes 1572864 | tf_op jit(solution)/shard_map/all_to_all | solution.py:40
  (1 other events, 0.7 us)
where the time goes:
time: 469 us; the launch traced here: 463 us
  blocking collectives  227 us (48%)
  waiting for transfers between devices  117 us (25%)
  starting transfers between devices  46.8 us (10%)
  local copies, waits for them, and re-layouts  42 us (9%)
  other arithmetic  15.9 us (3%)
  matrix products  11.5 us (2%)
    all_to_all x4, blocking collectives, sent_and_summed(): lax.all_to_all(tiles, axis, split_axis=0, concat_axis=0, tiled=True)  190 us
    all_to_all x5, waiting for transfers between devices, from_everyone(): return lax.all_to_all(copies, axis, split_axis=0, concat_axis=0, tiled=True)  117 us
    all_to_all x5, starting transfers between devices, from_everyone(): return lax.all_to_all(copies, axis, split_axis=0, concat_axis=0, tiled=True)  46.8 us
    psum x2, blocking collectives, one_axis_at_a_time(): shard = lax.psum(shard, axis)  24 us
    gather x4, local copies, waits for them, and re-layouts, local_training(): targets = jnp.take(target_table, chosen, axis=0)  19.1 us
    gather x4, local copies, waits for them, and re-layouts, local_training(): tok_rows = jnp.take(input_table, chosen, axis=0)  13.9 us
    all_to_all x1, blocking collectives, from_everyone(): return lax.all_to_all(copies, axis, split_axis=0, concat_axis=0, tiled=True)  12.7 us
  transfers between devices with their start and end apart: 5, of which 5 were waited for; matrix products, arithmetic and copies ran while one was open for 7% of the time, Pallas kernels for 0%

commit v1 on v0

v1 whole, which is shorter than its diff:
```python
import functools

import jax
import jax.numpy as jnp
from jax import lax
from jax.experimental import pallas as pl
from jax.experimental.pallas import tpu as pltpu
from jax.sharding import Mesh
from jax.sharding import PartitionSpec as P

CZY = ("core", "z", "y")
F32 = jnp.float32
BF16 = jnp.bfloat16

learn_rate = 0.001
beta_one = 0.9
beta_two = 0.95
adam_eps = 1e-08
weight_decay = 0.1
norm_eps = 1e-06

SIDE = 8
LANES = 128
COLS = 48
HALF = COLS // 2
TILE = COLS + HALF
POOL = 1024
TABLE = 1536
STEPS = 4
TOKENS = 1024
REPLICAS = 8
PAIRS = [(i, j) for i in range(REPLICAS) for j in range(i, REPLICAS)]
VMEM = 48 * 1024 * 1024


def position(core, z, y):
    return (core * SIDE + z) * SIDE + y


SUM_GROUPS = [[position(0, z, y) for z in range(SIDE)] for y in range(SIDE)] + [
    [position(1, z, y) for y in range(SIDE)] for z in range(SIDE)
]
GATHER_GROUPS = [[position(0, z, y) for y in range(SIDE)] for z in range(SIDE)] + [
    [position(1, z, y) for z in range(SIDE)] for y in range(SIDE)
]


def exchange(blocks, axes, groups=None):
    return lax.all_to_all(
        blocks, axes, split_axis=0, concat_axis=0, tiled=True, axis_index_groups=groups
    )


def kernel_call(body, out_shapes, *operands):
    return pl.pallas_call(
        body,
        out_shape=out_shapes,
        compiler_params=pltpu.CompilerParams(vmem_limit_bytes=VMEM),
    )(*operands)


def shaped(*dims, dtype=F32):
    return jax.ShapeDtypeStruct(dims, dtype)


def store_output(out_ref, output):
    for j in range(SIDE):
        out_ref[j, :COLS, :] = output[:, j * LANES : (j + 1) * LANES]
        private = POOL + (j // 2) * LANES
        line = (j % 2) * HALF
        out_ref[j, COLS:, :] = output[line : line + HALF, private : private + LANES]


def states_kernel(w_ref, m_ref, v_ref, out_ref):
    for part, ref in enumerate((w_ref, m_ref, v_ref)):
        turned = ref[...].astype(F32).T.reshape(SIDE, COLS, LANES)
        out_ref[:, part * COLS : (part + 1) * COLS, :] = turned


def first_kernel(x_ref, w_ref, table_ref, out_ref, total):
    step = pl.program_id(0)
    block = jnp.concatenate([x_ref[0], x_ref[1]], axis=1).astype(BF16)
    table_ref[...] = block
    weights = jnp.concatenate([w_ref[0], w_ref[1]], axis=1).astype(BF16)
    part = lax.dot_general(
        weights, block, (((1,), (1,)), ((), ())), preferred_element_type=F32
    )

    @pl.when(step == 0)
    def _():
        total[...] = part

    @pl.when(step > 0)
    def _():
        total[...] += part

    @pl.when(step == pl.num_programs(0) - 1)
    def _():
        store_output(out_ref, total[...])


def first_output(gathered, states):
    return pl.pallas_call(
        first_kernel,
        grid=(SIDE // 2,),
        in_specs=[
            pl.BlockSpec((2, TABLE, LANES), lambda i: (i, 0, 0)),
            pl.BlockSpec((2, COLS, LANES), lambda i: (i, 0, 0)),
        ],
        out_specs=[
            pl.BlockSpec((TABLE, 2 * LANES), lambda i: (0, i)),
            pl.BlockSpec((SIDE, TILE, LANES), lambda i: (0, 0, 0)),
        ],
        out_shape=[shaped(TABLE, SIDE * LANES, dtype=BF16), shaped(SIDE, TILE, LANES)],
        scratch_shapes=[pltpu.VMEM((COLS, TABLE), F32)],
        compiler_params=pltpu.CompilerParams(vmem_limit_bytes=VMEM),
    )(gathered, states)


def error_kernel(step, parts_ref, target_ref, count_ref, out_ref):
    output = parts_ref[0]
    for j in range(1, SIDE):
        output = output + parts_ref[j]
    error = (output - target_ref[...]).astype(BF16).astype(F32)
    weighted = error * count_ref[step]
    for j in range(SIDE):
        out_ref[j] = weighted


def step_kernel(first, last, error_ref, table_ref, w_ref, states_ref, *rest):
    if last:
        (total_out,) = rest
        new_states = None
    else:
        new_states, output_ref = rest
    error = jnp.concatenate(
        [error_ref[j, :COLS, :] for j in range(SIDE)]
        + [
            jnp.concatenate([error_ref[2 * k, COLS:, :], error_ref[2 * k + 1, COLS:, :]], axis=0)
            for k in range(SIDE // 2)
        ],
        axis=1,
    )
    high = error.astype(BF16)
    low = (error - high.astype(F32)).astype(BF16)
    both = jnp.concatenate([high, low], axis=0)
    wide = 2 * LANES
    updated = []
    for k in range(SIDE // 2):
        product = jnp.dot(both, table_ref[:, k * wide : (k + 1) * wide], preferred_element_type=F32)
        gradients = (product[:COLS] + product[COLS:]) * (1.0 / TOKENS)
        for half in range(2):
            j = 2 * k + half
            gradient = gradients[:, half * LANES : (half + 1) * LANES]
            weight_start = w_ref[j, :COLS, :]
            if first:
                weight_now = weight_start
            else:
                update_sum = states_ref[j, 2 * COLS :, :]
                weight_now = weight_start - learn_rate * update_sum
            base = COLS if first else 0
            moment_one = states_ref[j, base : base + COLS, :]
            moment_two = states_ref[j, base + COLS : base + 2 * COLS, :]
            moment_one = beta_one * moment_one + (1.0 - beta_one) * gradient
            moment_two = beta_two * moment_two + (1.0 - beta_two) * gradient * gradient
            direction = (
                moment_one / (jnp.sqrt(moment_two) + adam_eps) + weight_decay * weight_now
            )
            update_sum = direction if first else update_sum + direction
            if last:
                total_out[j] = update_sum
            else:
                new_states[j, :COLS, :] = moment_one
                new_states[j, COLS : 2 * COLS, :] = moment_two
                new_states[j, 2 * COLS :, :] = update_sum
                updated.append((weight_start - learn_rate * update_sum).astype(BF16))
    if last:
        return
    weights = jnp.concatenate(updated, axis=1)
    output = jnp.concatenate(
        [
            lax.dot_general(
                weights,
                table_ref[row : row + wide, :],
                (((1,), (1,)), ((), ())),
                preferred_element_type=F32,
            )
            for row in range(0, TABLE, wide)
        ],
        axis=1,
    )
    store_output(output_ref, output)


def turn_kernel(parts_ref, out_ref):
    turned = parts_ref[...].reshape(SIDE * COLS, LANES).T
    out_ref[...] = turned.reshape(REPLICAS, LANES // REPLICAS, SIDE * COLS)


def gram_kernel(updates_ref, out_ref):
    updates = [updates_ref[r] for r in range(REPLICAS)]
    lines = []
    for i, j in PAIRS:
        product = updates[i] * updates[j]
        lines.append(jnp.sum(product, axis=0, keepdims=True))
    while len(lines) % 8:
        lines.append(jnp.zeros_like(lines[0]))
    sums = jnp.sum(jnp.concatenate(lines, axis=0), axis=1, keepdims=True)
    spread = jnp.broadcast_to(sums, (len(lines), LANES))
    line = lax.broadcasted_iota(jnp.int32, spread.shape, 0)
    lane = lax.broadcasted_iota(jnp.int32, spread.shape, 1)
    packed = jnp.sum(jnp.where(line == lane, spread, 0.0), axis=0, keepdims=True)
    for j in range(REPLICAS):
        out_ref[j] = packed


def gram_sum_kernel(parts_ref, out_ref):
    packed = jnp.sum(parts_ref[...], axis=0)
    for j in range(SIDE * SIDE):
        out_ref[j] = packed


def merge_kernel(parts_ref, updates_ref, out_ref):
    packed = jnp.sum(parts_ref[...], axis=0)
    lane = lax.broadcasted_iota(jnp.int32, packed.shape, 1)
    gram = {}
    for place, (i, j) in enumerate(PAIRS):
        value = jnp.sum(jnp.where(lane == place, packed, 0.0), axis=1, keepdims=True)
        gram[i, j] = value
        gram[j, i] = value
    members = [[r] for r in range(REPLICAS)]
    while len(members) > 1:
        merged = []
        for lower, upper in zip(members[0::2], members[1::2]):
            cross_dot = sum(gram[i, j] for i in lower for j in upper)
            lower_norm = sum(gram[i, j] for i in lower for j in lower)
            upper_norm = sum(gram[i, j] for i in upper for j in upper)
            lower_coef = 1.0 - cross_dot / (2.0 * (lower_norm + norm_eps))
            upper_coef = 1.0 - cross_dot / (2.0 * (upper_norm + norm_eps))
            scale = {**{i: lower_coef for i in lower}, **{i: upper_coef for i in upper}}
            merged.append((lower + upper, scale))
        factor = {i: scale[i] for _, scale in merged for i in scale}
        gram = {(i, j): factor[i] * factor[j] * value for (i, j), value in gram.items()}
        total = factor if len(merged) * 2 == REPLICAS else {i: total[i] * factor[i] for i in total}
        members = [group for group, _ in merged]
    result = total[0] * updates_ref[0]
    for r in range(1, REPLICAS):
        result = result + total[r] * updates_ref[r]
    out_ref[...] = result


def own_targets(shared_targets, private_targets, sum_place, gather_place):
    rows = lax.dynamic_slice_in_dim(shared_targets, sum_place * LANES, LANES, 0)
    shared = lax.dynamic_slice_in_dim(rows.astype(F32).T, gather_place * COLS, COLS, 0)
    rows = lax.dynamic_slice_in_dim(private_targets, (sum_place // 2) * LANES, LANES, 0)
    line = gather_place * COLS + (sum_place % 2) * HALF
    private = lax.dynamic_slice_in_dim(rows.astype(F32).T, line, HALF, 0)
    return jnp.concatenate([shared, private], axis=0)


def own_counts(token_ids, sum_place):
    lane = lax.iota(jnp.int32, LANES)
    counts = []
    for start, lines in (
        (sum_place * LANES, COLS),
        (POOL + (sum_place // 2) * LANES, HALF),
    ):
        hits = (token_ids[:, :, None] == (start + lane)[None, None, :]).astype(F32)
        count = jnp.sum(hits, axis=1)
        counts.append(jnp.broadcast_to(count[:, None, :], (STEPS, lines, LANES)))
    return jnp.concatenate(counts, axis=1)


def on_device(
    weight,
    first_moment,
    second_moment,
    token_ids,
    shared_inputs,
    private_inputs,
    shared_targets,
    private_targets,
):
    core = lax.axis_index("core")
    z = lax.axis_index("z")
    y = lax.axis_index("y")
    sum_place = jnp.where(core == 0, z, y)
    gather_place = jnp.where(core == 0, y, z)

    slices = jnp.concatenate([shared_inputs, private_inputs[0]], axis=0).astype(F32)
    gathered = lax.all_gather(
        slices, CZY, axis=0, tiled=True, axis_index_groups=GATHER_GROUPS
    ).reshape(SIDE, TABLE, LANES)

    states = kernel_call(
        states_kernel, shaped(SIDE, 3 * COLS, LANES), weight, first_moment[0], second_moment[0]
    )
    start = exchange(states, CZY, GATHER_GROUPS)
    targets = own_targets(shared_targets, private_targets[0], sum_place, gather_place)
    counts = own_counts(token_ids[0], sum_place)

    table, parts = first_output(gathered, start)
    states = start
    for step in range(STEPS):
        parts = exchange(parts, CZY, SUM_GROUPS)
        error = kernel_call(
            functools.partial(error_kernel, step), shaped(SIDE, TILE, LANES), parts, targets, counts
        )
        error = exchange(error, CZY, SUM_GROUPS)
        last = step == STEPS - 1
        body = functools.partial(step_kernel, step == 0, last)
        if last:
            updates = kernel_call(body, shaped(SIDE, COLS, LANES), error, table, start, states)
        else:
            states, parts = kernel_call(
                body,
                [shaped(SIDE, 3 * COLS, LANES), shaped(SIDE, TILE, LANES)],
                error,
                table,
                start,
                states,
            )

    updates = exchange(updates, CZY, GATHER_GROUPS)
    turned = kernel_call(turn_kernel, shaped(REPLICAS, LANES // REPLICAS, SIDE * COLS), updates)
    updates = exchange(turned, ("x", "core"))
    gram = kernel_call(gram_kernel, shaped(REPLICAS, 1, LANES), updates)
    gram = exchange(gram, ("x", "core"))
    gram = kernel_call(gram_sum_kernel, shaped(SIDE * SIDE, 1, LANES), gram)
    gram = exchange(gram, ("z", "y"))
    return kernel_call(
        merge_kernel, shaped(LANES // REPLICAS, SIDE * COLS), gram, updates
    )


def solution(mesh):
    torus = Mesh(mesh.devices.reshape(4, 2, SIDE, SIDE), ("x", "core", "z", "y"))
    row = ("z", "y")
    rep = ("x", "core")
    placed = (
        P(row, None),
        P(rep, row, None),
        P(rep, row, None),
        P(rep, None, None),
        P(None, row),
        P(rep, None, row),
        P(),
        P(rep, None, None),
    )
    return jax.shard_map(
        on_device,
        mesh=torus,
        in_specs=placed,
        out_specs=P((*row, *rep), None),
        check_vma=False,
    )
```

time: 469 us -> 248 us (0.53); the launches traced: 463 us -> 247 us
  blocking collectives: 227 us -> 144 us
  waiting for transfers between devices: 117 us -> 49 us
  local copies, waits for them, and re-layouts: 42 us -> 6.47 us
  starting transfers between devices: 46.8 us -> 17.4 us
  Pallas kernels: 0 us -> 13.2 us
  other arithmetic: 15.9 us -> 3.85 us
  matrix products: 11.5 us -> 0 us
  between operations: 3.08 us -> 13.5 us
    all_to_all x5 -> x2, waiting for transfers between devices: 117 us -> 20.5 us  [exchange(): lax.all_to_all(blocks, axes, split_axis=0, concat_axis=0, tiled=True, axi...]
    all_to_all x5 -> x11, blocking collectives: 203 us -> 144 us  [exchange(): lax.all_to_all(blocks, axes, split_axis=0, concat_axis=0, tiled=True, axi...]
    gather x8 -> x0, local copies, waits for them, and re-layouts: 32.9 us -> none  [the longest x4 19.1 us: local_training(): targets = jnp.take(target_table, chosen, axis=0)]
    all_to_all x5 -> x2, starting transfers between devices: 46.8 us -> 17.4 us  [exchange(): lax.all_to_all(blocks, axes, split_axis=0, concat_axis=0, tiled=True, axi...]
    all_gather x0 -> x1, waiting for transfers between devices: none -> 28.5 us  [on_device(): lax.all_gather(slices, CZY, axis=0, tiled=True, axis_index_groups=GATHER_...]
    psum x2 -> x0, blocking collectives: 24 us -> none  [one_axis_at_a_time(): shard = lax.psum(shard, axis)]
    pallas_call x0 -> x14, Pallas kernels: none -> 13.2 us  [the longest x13 8.04 us: kernel_call(): pl.pallas_call(body, out_shape=out_shapes, compiler_params=pltpu.Compiler...]
    dot_general x16 -> x0, matrix products: 11.5 us -> none  [the longest x1 3.54 us: on_device(): lax.dot_general(flat, flat, (((1,), (1,)), ((), ())), precision=lax.Preci...]
  transfers between devices with their start and end apart: 5 -> 3, of which waited for: 5 -> 3; matrix products, arithmetic and copies ran while one was open for 7% -> 1% of each run, Pallas kernels for 0% -> 0%
where the time goes in v1:
time: 248 us; the launch traced here: 247 us
  blocking collectives  144 us (58%)
  waiting for transfers between devices  49 us (20%)
  starting transfers between devices  17.4 us (7%)
  between operations  13.5 us (5%)
  Pallas kernels  13.2 us (5%)
  local copies, waits for them, and re-layouts  6.47 us (3%)
  other arithmetic  3.85 us (2%)
    all_to_all x11, blocking collectives, exchange(): lax.all_to_all(blocks, axes, split_axis=0, concat_axis=0, tiled=True, axi...  144 us
    all_gather x1, waiting for transfers between devices, on_device(): lax.all_gather(slices, CZY, axis=0, tiled=True, axis_index_groups=GATHER_...  28.5 us
    all_to_all x2, waiting for transfers between devices, exchange(): lax.all_to_all(blocks, axes, split_axis=0, concat_axis=0, tiled=True, axi...  20.5 us
    all_to_all x2, starting transfers between devices, exchange(): lax.all_to_all(blocks, axes, split_axis=0, concat_axis=0, tiled=True, axi...  17.4 us
    pallas_call x13, Pallas kernels, kernel_call(): pl.pallas_call(body, out_shape=out_shapes, compiler_params=pltpu.Compiler...  8.04 us
    unnamed x17, local copies, waits for them, and re-layouts  6.29 us
    pallas_call x1, Pallas kernels, first_output(): pl.pallas_call(first_kernel, grid=(SIDE // 2,), in_specs=[pl.BlockSpec((2...  5.18 us
  transfers between devices with their start and end apart: 3, of which 3 were waited for; matrix products, arithmetic and copies ran while one was open for 1% of the time, Pallas kernels for 0%

profile of v1, /device:TPU:1, one launch (start us, length us, event | category | flops | bytes accessed | tf_op | source)
XLA Modules:
  0.0 247.3 jit_solution(10852374512159985236)
XLA Ops:
  6.5 2.0 maximum_convert_fusion
  11.3 1.0 shard_map.82
  12.3 10.9 %all-to-all-start = ((f32[8,144,128]{2,1,0:T(8,128)}), f32[8,144,128]{2,1,0:T(8,128)S(1)}, u32[]{:S(2)}, u32[]{:S(2)}) async-start(f32[8,144,128]{2,1,0:T(8,128)} %shard_map.82), calls=%async_computation | async-start | bytes 1179648 | tf_op jit(solution)/shard_map/all_to_all | solution.py:49
  23.4 12.7 %all-to-all-done.w_ref.states_ref = f32[8,144,128]{2,1,0:T(8,128)S(1)} async-done(((f32[8,144,128]{2,1,0:T(8,128)}), f32[8,144,128]{2,1,0:T(8,128)S(1)}, u32[]{:S(2)}, u32[]{:S(2)}) %all-to-all-start) | async-done | bytes 589856 | tf_op jit(solution)/shard_map/all_to_all | solution.py:49
  36.1 28.5 %all-gather.2.cloned.1.call-done = f32[12288,128]{1,0:T(8,128)} async-done(((f32[1536,128]{1,0:T(8,128)}), f32[12288,128]{1,0:T(8,128)}) %all-gather.2.cloned.1.call-update) | async-done | bytes 6291472 | tf_op jit(solution)/shard_map/all_gather | solution.py:291
  64.6 5.2 %shard_map.83 = (bf16[1536,1024]{1,0:T(8,128)(2,1)S(1)}, f32[8,72,128]{2,1,0:T(8,128)}) custom-call(f32[8,1536,128]{2,1,0:T(8,128)} %bitcast.12, f32[8,144,128]{2,1,0:T(8,128)S(1)} %all-to-all-done.w_ref.states_ref), custom_call_target="tpu_custom_call" | custom-call | tf_op jit(solution)/shard_map/pallas_call | solution.py:103
  69.8 1.6 copy-done.1
  71.4 6.5 %all-to-all-start.1 = ((f32[8,72,128]{2,1,0:T(8,128)}), f32[8,72,128]{2,1,0:T(8,128)S(1)}, u32[]{:S(2)}, u32[]{:S(2)}) async-start(f32[8,72,128]{2,1,0:T(8,128)} %get-tuple-element.13), calls=%async_computation.1 | async-start | bytes 589824 | tf_op jit(solution)/shard_map/all_to_all | solution.py:49
  79.8 7.8 %all-to-all-done.1.parts_ref = f32[8,72,128]{2,1,0:T(8,128)S(1)} async-done(((f32[8,72,128]{2,1,0:T(8,128)}), f32[8,72,128]{2,1,0:T(8,128)S(1)}, u32[]{:S(2)}, u32[]{:S(2)}) %all-to-all-start.1) | async-done | bytes 294944 | tf_op jit(solution)/shard_map/all_to_all | solution.py:49
  87.7 12.1 %all_to_all.65.error_ref = f32[8,72,128]{2,1,0:T(8,128)S(1)} all-to-all(f32[8,72,128]{2,1,0:T(8,128)S(1)} %shard_map.84), channel_id=1, replica_groups={{0,8,16,24,32,40,48,56},{1,9,17,25,33,41,49,57},{2,10,18,26,34,42,50,58..., dimensions={0} | all-to-all | bytes 589824 | tf_op jit(solution)/shard_map/all_to_all | solution.py:49
  99.7 1.9 copy-done.2
  101.6 1.6 shard_map.85
  103.3 12.1 %all_to_all.66.parts_ref = f32[8,72,128]{2,1,0:T(8,128)S(1)} all-to-all(f32[8,72,128]{2,1,0:T(8,128)S(1)} %get-tuple-element.15), channel_id=1, replica_groups={{0,8,16,24,32,40,48,56},{1,9,17,25,33,41,49,57},{2,10,18,26,34,42,50,58..., dimensions={0} | all-to-all | bytes 589824 | tf_op jit(solution)/shard_map/all_to_all | solution.py:49
  115.3 12.1 %all_to_all.67.error_ref = f32[8,72,128]{2,1,0:T(8,128)S(1)} all-to-all(f32[8,72,128]{2,1,0:T(8,128)S(1)} %shard_map.86), channel_id=1, replica_groups={{0,8,16,24,32,40,48,56},{1,9,17,25,33,41,49,57},{2,10,18,26,34,42,50,58..., dimensions={0} | all-to-all | bytes 589824 | tf_op jit(solution)/shard_map/all_to_all | solution.py:49
  127.4 1.6 shard_map.87
  129.1 12.1 %all_to_all.68.parts_ref = f32[8,72,128]{2,1,0:T(8,128)S(1)} all-to-all(f32[8,72,128]{2,1,0:T(8,128)S(1)} %get-tuple-element.17), channel_id=1, replica_groups={{0,8,16,24,32,40,48,56},{1,9,17,25,33,41,49,57},{2,10,18,26,34,42,50,58..., dimensions={0} | all-to-all | bytes 589824 | tf_op jit(solution)/shard_map/all_to_all | solution.py:49
  141.1 12.1 %all_to_all.69.error_ref = f32[8,72,128]{2,1,0:T(8,128)S(1)} all-to-all(f32[8,72,128]{2,1,0:T(8,128)S(1)} %shard_map.88), channel_id=1, replica_groups={{0,8,16,24,32,40,48,56},{1,9,17,25,33,41,49,57},{2,10,18,26,34,42,50,58..., dimensions={0} | all-to-all | bytes 589824 | tf_op jit(solution)/shard_map/all_to_all | solution.py:49
  153.2 1.7 shard_map.89
  154.9 12.1 %all_to_all.70.parts_ref = f32[8,72,128]{2,1,0:T(8,128)S(1)} all-to-all(f32[8,72,128]{2,1,0:T(8,128)S(1)} %get-tuple-element.19), channel_id=1, replica_groups={{0,8,16,24,32,40,48,56},{1,9,17,25,33,41,49,57},{2,10,18,26,34,42,50,58..., dimensions={0} | all-to-all | bytes 589824 | tf_op jit(solution)/shard_map/all_to_all | solution.py:49
  167.0 12.1 %all_to_all.71.error_ref = f32[8,72,128]{2,1,0:T(8,128)S(1)} all-to-all(f32[8,72,128]{2,1,0:T(8,128)S(1)} %shard_map.90), channel_id=1, replica_groups={{0,8,16,24,32,40,48,56},{1,9,17,25,33,41,49,57},{2,10,18,26,34,42,50,58..., dimensions={0} | all-to-all | bytes 589824 | tf_op jit(solution)/shard_map/all_to_all | solution.py:49
  179.8 12.3 %all_to_all.72.parts_ref = f32[8,48,128]{2,1,0:T(8,128)S(1)} all-to-all(f32[8,48,128]{2,1,0:T(8,128)S(1)} %shard_map.91), channel_id=1, replica_groups={{0,1,2,3,4,5,6,7},{8,9,10,11,12,13,14,15},{16,17,18,19,20,21,22,23},{24..., dimensions={0} | all-to-all | bytes 393216 | tf_op jit(solution)/shard_map/all_to_all | solution.py:49
  192.3 24.7 %all_to_all.73.updates_ref = f32[8,16,384]{2,1,0:T(8,128)S(1)} all-to-all(f32[8,16,384]{2,1,0:T(8,128)S(1)} %shard_map.92), channel_id=1, replica_groups=mesh['x'=4,'core'=2,'z'=8,'y'=8] {'x','core'}, dimensions={0} | all-to-all | bytes 393216 | tf_op jit(solution)/shard_map/all_to_all | solution.py:49
  217.1 7.9 %all_to_all.74.parts_ref = f32[8,1,128]{2,1,0:T(1,128)S(1)} all-to-all(f32[8,1,128]{2,1,0:T(1,128)S(1)} %shard_map.93), channel_id=1, replica_groups=mesh['x'=4,'core'=2,'z'=8,'y'=8] {'x','core'}, dimensions={0} | all-to-all | bytes 8192 | tf_op jit(solution)/shard_map/all_to_all | solution.py:49
  225.0 14.6 %all_to_all.75.parts_ref = f32[64,1,128]{2,1,0:T(1,128)S(1)} all-to-all(f32[64,1,128]{2,1,0:T(1,128)S(1)} %shard_map.94), channel_id=1, replica_groups=mesh['x'=4,'core'=2,'z'=8,'y'=8] {'z','y'}, dimensions={0} | all-to-all | bytes 65536 | tf_op jit(solution)/shard_map/all_to_all | solution.py:49
  (37 shorter events, 6.9 us)
Async XLA Ops:
  6.5 16.6 %copy-start = (bf16[1024,384]{1,0:T(8,128)(2,1)S(1)}, bf16[1024,384]{1,0:T(8,128)(2,1)}, u32[]{:S(2)}) copy-start(bf16[1024,384]{1,0:T(8,128)(2,1)} %param.14) | copy-start | bytes 2359300
  6.5 58.0 %all-gather.2.cloned.1.call-start = ((), (), s32[]{:S(2)}) async-start(), calls=%async_computation.13 | async-start | bytes 7077888 | tf_op jit(solution)/shard_map/all_gather | solution.py:291
  8.6 0.9 copy-start.4
  9.5 0.9 copy-start.5
  10.4 0.9 copy-start.6
  12.3 23.8 %all-to-all-start = ((f32[8,144,128]{2,1,0:T(8,128)}), f32[8,144,128]{2,1,0:T(8,128)S(1)}, u32[]{:S(2)}, u32[]{:S(2)}) async-start(f32[8,144,128]{2,1,0:T(8,128)} %shard_map.82), calls=%async_computation | async-start | bytes 1179648 | tf_op jit(solution)/shard_map/all_to_all | solution.py:49
  64.6 14.4 %copy-start.7 = (s32[1,4,1024]{2,1,0:T(4,128)S(1)}, s32[1,4,1024]{2,1,0:T(4,128)}, u32[]{:S(2)}) copy-start(s32[1,4,1024]{2,1,0:T(4,128)} %param.11) | copy-start | bytes 49156
  69.8 1.6 copy-start.1
  71.4 16.2 %all-to-all-start.1 = ((f32[8,72,128]{2,1,0:T(8,128)}), f32[8,72,128]{2,1,0:T(8,128)S(1)}, u32[]{:S(2)}, u32[]{:S(2)}) async-start(f32[8,72,128]{2,1,0:T(8,128)} %get-tuple-element.13), calls=%async_computation.1 | async-start | bytes 589824 | tf_op jit(solution)/shard_map/all_to_all | solution.py:49
  99.7 1.9 copy-start.2
  101.6 25.8 %copy-start.3 = (bf16[1536,1024]{1,0:T(8,128)(2,1)S(1)}, bf16[1536,1024]{1,0:T(8,128)(2,1)}, u32[]{:S(2)}) copy-start(bf16[1536,1024]{1,0:T(8,128)(2,1)} %copy-done.1) | copy-start | bytes 9437188
Sparse Core Ops, SparseCore 0:
  9.4 55.0 all-gather.1

commit v2 on v1

--- a/solution.py
+++ b/solution.py
@@ -30,7 +30,9 @@
 TOKENS = 1024
 REPLICAS = 8
 PAIRS = [(i, j) for i in range(REPLICAS) for j in range(i, REPLICAS)]
-VMEM = 48 * 1024 * 1024
+MIB = 1024 * 1024
+WIDE = 2 * LANES
+OFFSETS = (0, 4, -1, 1, -2, 2, -3, 3)
 
 
 def position(core, z, y):
@@ -45,17 +47,26 @@
 ]
 
 
+UP = [(group[i], group[(i + 1) % SIDE]) for group in GATHER_GROUPS for i in range(SIDE)]
+DOWN = [(group[i], group[(i - 1) % SIDE]) for group in GATHER_GROUPS for i in range(SIDE)]
+
+
 def exchange(blocks, axes, groups=None):
     return lax.all_to_all(
         blocks, axes, split_axis=0, concat_axis=0, tiled=True, axis_index_groups=groups
     )
 
 
-def kernel_call(body, out_shapes, *operands):
+def kernel_call(body, out_shapes, *operands, room=12):
+    in_specs = [
+        pl.BlockSpec(memory_space=pltpu.SMEM if operand.dtype == jnp.int32 else pltpu.VMEM)
+        for operand in operands
+    ]
     return pl.pallas_call(
         body,
+        in_specs=in_specs,
         out_shape=out_shapes,
-        compiler_params=pltpu.CompilerParams(vmem_limit_bytes=VMEM),
+        compiler_params=pltpu.CompilerParams(vmem_limit_bytes=room * MIB),
     )(*operands)
 
 
@@ -77,60 +88,98 @@
         out_ref[:, part * COLS : (part + 1) * COLS, :] = turned
 
 
-def first_kernel(x_ref, w_ref, table_ref, out_ref, total):
-    step = pl.program_id(0)
-    block = jnp.concatenate([x_ref[0], x_ref[1]], axis=1).astype(BF16)
-    table_ref[...] = block
-    weights = jnp.concatenate([w_ref[0], w_ref[1]], axis=1).astype(BF16)
-    part = lax.dot_general(
-        weights, block, (((1,), (1,)), ((), ())), preferred_element_type=F32
-    )
-
-    @pl.when(step == 0)
-    def _():
-        total[...] = part
-
-    @pl.when(step > 0)
-    def _():
-        total[...] += part
-
-    @pl.when(step == pl.num_programs(0) - 1)
-    def _():
-        store_output(out_ref, total[...])
-
-
-def first_output(gathered, states):
+def widen_kernel(shared_ref, private_ref, out_ref, shared, private, arrived):
+    copies = [
+        pltpu.make_async_copy(shared_ref, shared, arrived.at[0]),
+        pltpu.make_async_copy(private_ref, private, arrived.at[1]),
+    ]
+    for copy in copies:
+        copy.start()
+    copies[0].wait()
+    out_ref[:POOL, :] = shared[...].astype(F32)
+    copies[1].wait()
+    out_ref[POOL:, :] = private[...].astype(F32)
+
+
+def widened(shared_inputs, private_inputs):
     return pl.pallas_call(
-        first_kernel,
-        grid=(SIDE // 2,),
-        in_specs=[
-            pl.BlockSpec((2, TABLE, LANES), lambda i: (i, 0, 0)),
-            pl.BlockSpec((2, COLS, LANES), lambda i: (i, 0, 0)),
+        widen_kernel,
+        in_specs=[pl.BlockSpec(memory_space=pltpu.HBM)] * 2,
+        out_shape=shaped(TABLE, LANES),
+        scratch_shapes=[
+            pltpu.VMEM((POOL, LANES), BF16),
+            pltpu.VMEM((TABLE - POOL, LANES), BF16),
+            pltpu.SemaphoreType.DMA((2,)),
         ],
-        out_specs=[
-            pl.BlockSpec((TABLE, 2 * LANES), lambda i: (0, i)),
-            pl.BlockSpec((SIDE, TILE, LANES), lambda i: (0, 0, 0)),
+        compiler_params=pltpu.CompilerParams(vmem_limit_bytes=4 * MIB),
+    )(shared_inputs, private_inputs)
+
+
+def narrow_kernel(*refs):
+    *blocks, out_ref = refs
+    for k, block in enumerate(blocks):
+        out_ref[:, k * LANES : (k + 1) * LANES] = block[...].astype(BF16)
+
+
+def narrowed(*blocks):
+    return kernel_call(narrow_kernel, shaped(TABLE, len(blocks) * LANES, dtype=BF16), *blocks)
+
+
+def turned_product(weights, table_rows):
+    return lax.dot_general(
+        weights, table_rows, (((1,), (1,)), ((), ())), preferred_element_type=F32
+    )
+
+
+def early_kernel(
+    place_ref, start_ref, target_ref, count_ref, own_ref, *refs
+):
+    pairs, (states_ref, constant_ref, part_ref) = refs[:3], refs[3:]
+    place = place_ref[0]
+    for k, offset in enumerate(OFFSETS):
+        states_ref[k] = start_ref[lax.rem(place + (offset + SIDE), SIDE)]
+    constant_ref[:STEPS] = count_ref[...]
+    constant_ref[STEPS] = target_ref[...]
+    weights = [states_ref[k, :COLS, :].astype(BF16) for k in range(SIDE)]
+    for row in range(0, TABLE, WIDE):
+        rows = slice(row, row + WIDE)
+        part = turned_product(weights[0], own_ref[rows, :])
+        for k, pair in enumerate(pairs):
+            both = jnp.concatenate(weights[2 * k + 2 : 2 * k + 4], axis=1)
+            part = part + turned_product(both, pair[rows, :])
+        part_ref[:, rows] = part
+
+
+def late_kernel(states_ref, own_ref, opposite_ref, part_ref, table_ref, out_ref):
+    table_ref[:, :LANES] = own_ref[...]
+    table_ref[:, LANES:] = opposite_ref[...].astype(BF16)
+    weights = states_ref[1, :COLS, :].astype(BF16)
+    output = jnp.concatenate(
+        [
+            part_ref[:, row : row + WIDE]
+            + turned_product(weights, table_ref[row : row + WIDE, LANES:])
+            for row in range(0, TABLE, WIDE)
         ],
-        out_shape=[shaped(TABLE, SIDE * LANES, dtype=BF16), shaped(SIDE, TILE, LANES)],
-        scratch_shapes=[pltpu.VMEM((COLS, TABLE), F32)],
-        compiler_params=pltpu.CompilerParams(vmem_limit_bytes=VMEM),
-    )(gathered, states)
-
-
-def error_kernel(step, parts_ref, target_ref, count_ref, out_ref):
+        axis=1,
+    )
+    store_output(out_ref, output)
+
+
+def error_kernel(step, parts_ref, constant_ref, out_ref):
     output = parts_ref[0]
     for j in range(1, SIDE):
         output = output + parts_ref[j]
-    error = (output - target_ref[...]).astype(BF16).astype(F32)
-    weighted = error * count_ref[step]
+    error = (output - constant_ref[STEPS]).astype(BF16).astype(F32)
+    weighted = error * constant_ref[step]
     for j in range(SIDE):
         out_ref[j] = weighted
 
 
-def step_kernel(first, last, error_ref, table_ref, w_ref, states_ref, *rest):
+def step_kernel(first, last, place_ref, error_ref, *refs):
+    tables, (w_ref, states_ref, *rest) = refs[: SIDE // 2], refs[SIDE // 2 :]
     if last:
         (total_out,) = rest
-        new_states = None
+        place = place_ref[0]
     else:
         new_states, output_ref = rest
     error = jnp.concatenate(
@@ -144,10 +193,9 @@
     high = error.astype(BF16)
     low = (error - high.astype(F32)).astype(BF16)
     both = jnp.concatenate([high, low], axis=0)
-    wide = 2 * LANES
     updated = []
     for k in range(SIDE // 2):
-        product = jnp.dot(both, table_ref[:, k * wide : (k + 1) * wide], preferred_element_type=F32)
+        product = jnp.dot(both, tables[k][...], preferred_element_type=F32)
         gradients = (product[:COLS] + product[COLS:]) * (1.0 / TOKENS)
         for half in range(2):
             j = 2 * k + half
@@ -168,7 +216,7 @@
             )
             update_sum = direction if first else update_sum + direction
             if last:
-                total_out[j] = update_sum
+                total_out[lax.rem(place + (OFFSETS[j] + SIDE), SIDE)] = update_sum
             else:
                 new_states[j, :COLS, :] = moment_one
                 new_states[j, COLS : 2 * COLS, :] = moment_two
@@ -177,19 +225,12 @@
     if last:
         return
     weights = jnp.concatenate(updated, axis=1)
-    output = jnp.concatenate(
-        [
-            lax.dot_general(
-                weights,
-                table_ref[row : row + wide, :],
-                (((1,), (1,)), ((), ())),
-                preferred_element_type=F32,
-            )
-            for row in range(0, TABLE, wide)
-        ],
-        axis=1,
-    )
-    store_output(output_ref, output)
+    output = []
+    for row in range(0, TABLE, WIDE):
+        rows = slice(row, row + WIDE)
+        table_rows = jnp.concatenate([table[rows, :] for table in tables], axis=1)
+        output.append(turned_product(weights, table_rows))
+    store_output(output_ref, jnp.concatenate(output, axis=1))
 
 
 def turn_kernel(parts_ref, out_ref):
@@ -287,38 +328,62 @@
     sum_place = jnp.where(core == 0, z, y)
     gather_place = jnp.where(core == 0, y, z)
 
-    slices = jnp.concatenate([shared_inputs, private_inputs[0]], axis=0).astype(F32)
-    gathered = lax.all_gather(
-        slices, CZY, axis=0, tiled=True, axis_index_groups=GATHER_GROUPS
-    ).reshape(SIDE, TABLE, LANES)
-
-    states = kernel_call(
+    own = widened(shared_inputs, private_inputs[0])
+    tables = [narrowed(own)]
+    upward = downward = own
+    for hop in range(3):
+        if hop >= 1:
+            upward, tables[hop - 1] = lax.optimization_barrier((upward, tables[hop - 1]))
+        upward = lax.ppermute(upward, CZY, UP)
+        downward = lax.ppermute(downward, CZY, DOWN)
+        tables.append(narrowed(upward, downward))
+    opposite, tables[2] = lax.optimization_barrier((upward, tables[2]))
+    opposite = lax.ppermute(opposite, CZY, UP)
+
+    start = kernel_call(
         states_kernel, shaped(SIDE, 3 * COLS, LANES), weight, first_moment[0], second_moment[0]
     )
-    start = exchange(states, CZY, GATHER_GROUPS)
+    start = exchange(start, CZY, GATHER_GROUPS)
     targets = own_targets(shared_targets, private_targets[0], sum_place, gather_place)
     counts = own_counts(token_ids[0], sum_place)
-
-    table, parts = first_output(gathered, start)
+    place = gather_place.astype(jnp.int32).reshape(1)
+
+    start, constants, part = kernel_call(
+        early_kernel,
+        [
+            shaped(SIDE, 3 * COLS, LANES),
+            shaped(STEPS + 1, TILE, LANES),
+            shaped(COLS, TABLE),
+        ],
+        place,
+        start,
+        targets,
+        counts,
+        *tables,
+    )
+    tables[0], parts = kernel_call(
+        late_kernel,
+        [shaped(TABLE, WIDE, dtype=BF16), shaped(SIDE, TILE, LANES)],
+        start,
+        tables[0],
+        opposite,
+        part,
+    )
     states = start
     for step in range(STEPS):
         parts = exchange(parts, CZY, SUM_GROUPS)
         error = kernel_call(
-            functools.partial(error_kernel, step), shaped(SIDE, TILE, LANES), parts, targets, counts
+            functools.partial(error_kernel, step), shaped(SIDE, TILE, LANES), parts, constants
         )
         error = exchange(error, CZY, SUM_GROUPS)
         last = step == STEPS - 1
         body = functools.partial(step_kernel, step == 0, last)
+        operands = (place, error, *tables, start, states)
         if last:
-            updates = kernel_call(body, shaped(SIDE, COLS, LANES), error, table, start, states)
+            updates = kernel_call(body, shaped(SIDE, COLS, LANES), *operands)
         else:
             states, parts = kernel_call(
-                body,
-                [shaped(SIDE, 3 * COLS, LANES), shaped(SIDE, TILE, LANES)],
-                error,
-                table,
-                start,
-                states,
+                body, [shaped(SIDE, 3 * COLS, LANES), shaped(SIDE, TILE, LANES)], *operands
             )
 
     updates = exchange(updates, CZY, GATHER_GROUPS)

time: 248 us -> 241 us (0.972)
  waiting for transfers between devices: 49 us -> 16.9 us
  blocking collectives: 144 us -> 164 us
  starting transfers between devices: 17.4 us -> 32.4 us
  between operations: 13.5 us -> 0.35 us
    all_gather x1 -> x0, waiting for transfers between devices: 28.5 us -> none  [on_device(): lax.all_gather(slices, CZY, axis=0, tiled=True, axis_index_groups=GATHER_...]
    ppermute x0 -> x7, starting transfers between devices: none -> 28.2 us  [the longest x3 17.6 us: on_device(): downward = lax.ppermute(downward, CZY, DOWN)]
    all_to_all x2 -> x1, waiting for transfers between devices: 20.5 us -> 0.01 us  [exchange(): lax.all_to_all(blocks, axes, split_axis=0, concat_axis=0, tiled=True, axi...]
    all_to_all x11 -> x12, blocking collectives: 144 us -> 164 us  [exchange(): lax.all_to_all(blocks, axes, split_axis=0, concat_axis=0, tiled=True, axi...]
    ppermute x0 -> x7, waiting for transfers between devices: none -> 16.9 us  [the longest x3 16.3 us: on_device(): upward = lax.ppermute(upward, CZY, UP)]
    all_to_all x2 -> x1, starting transfers between devices: 17.4 us -> 4.19 us  [exchange(): lax.all_to_all(blocks, axes, split_axis=0, concat_axis=0, tiled=True, axi...]
    pallas_call x14 -> x20, Pallas kernels: 13.2 us -> 14.3 us  [the longest x19 14.1 us: kernel_call(): pl.pallas_call(body, in_specs=in_specs, out_shape=out_shapes, compiler_pa...]
  transfers between devices with their start and end apart: 3 -> 8, of which waited for: 3 -> 4; matrix products, arithmetic and copies ran while one was open for 1% -> 4% of each run, Pallas kernels for 0% -> 2%
where the time goes in v2:
time: 241 us; the launch traced here: 240 us
  blocking collectives  164 us (68%)
  starting transfers between devices  32.4 us (13%)
  waiting for transfers between devices  16.9 us (7%)
  Pallas kernels  14.3 us (6%)
  local copies, waits for them, and re-layouts  6.69 us (3%)
  other arithmetic  5.46 us (2%)
    all_to_all x12, blocking collectives, exchange(): lax.all_to_all(blocks, axes, split_axis=0, concat_axis=0, tiled=True, axi...  164 us
    ppermute x3, starting transfers between devices, on_device(): downward = lax.ppermute(downward, CZY, DOWN)  17.6 us
    ppermute x3, waiting for transfers between devices, on_device(): upward = lax.ppermute(upward, CZY, UP)  16.3 us
    pallas_call x19, Pallas kernels, kernel_call(): pl.pallas_call(body, in_specs=in_specs, out_shape=out_shapes, compiler_pa...  14.1 us
    ppermute x3, starting transfers between devices, on_device(): upward = lax.ppermute(upward, CZY, UP)  8.65 us
    unnamed x17, local copies, waits for them, and re-layouts  5.08 us
  transfers between devices with their start and end apart: 8, of which 4 were waited for; matrix products, arithmetic and copies ran while one was open for 4% of the time, Pallas kernels for 2%

profile of v2, /device:TPU:1, one launch (start us, length us, event | category | flops | bytes accessed | tf_op | source)
XLA Modules:
  0.0 240.1 jit_solution(2502985425087174658)
XLA Ops:
  2.2 4.8 %collective-permute-start = (f32[1536,128]{1,0:T(8,128)S(1)}, f32[1536,128]{1,0:T(8,128)S(1)}, u32[]{:S(2)}, u32[]{:S(2)}) collective-permute-start(f32[1536,128]{1,0:T(8,128)S(1)} %shard_map.83.refs_0_), channel_id=1, source_target_pairs={{0,1},{1,2},{2,3},{3,4},{4,5},{5,6},{6,7},{7,0},{8,9},{9,10},{10,1... | collective-permute-start | bytes 2359304 | tf_op jit(solution)/shard_map/ppermute | solution.py:337
  7.0 8.6 %collective-permute-start.2 = (f32[1536,128]{1,0:T(8,128)S(1)}, f32[1536,128]{1,0:T(8,128)S(1)}, u32[]{:S(2)}, u32[]{:S(2)}) collective-permute-start(f32[1536,128]{1,0:T(8,128)S(1)} %shard_map.83.refs_0_), channel_id=1, source_target_pairs={{0,7},{1,0},{2,1},{3,2},{4,3},{5,4},{6,5},{7,6},{8,15},{9,8},{10,9... | collective-permute-start | bytes 2359304 | tf_op jit(solution)/shard_map/ppermute | solution.py:338
  15.7 7.6 %collective-permute-done.refs_0_ = f32[1536,128]{1,0:T(8,128)S(1)} collective-permute-done((f32[1536,128]{1,0:T(8,128)S(1)}, f32[1536,128]{1,0:T(8,128)S(1)}, u32[]{:S(2)}, u32[]{:S(2)}) %collective-permute-start) | collective-permute-done | bytes 786464 | tf_op jit(solution)/shard_map/ppermute | solution.py:337
  23.4 1.9 collective-permute-start.1
  25.3 4.6 %collective-permute-start.4 = (f32[1536,128]{1,0:T(8,128)S(1)}, f32[1536,128]{1,0:T(8,128)S(1)}, u32[]{:S(2)}, u32[]{:S(2)}) collective-permute-start(f32[1536,128]{1,0:T(8,128)S(1)} %collective-permute-done.2.refs_1_), channel_id=1, source_target_pairs={{0,7},{1,0},{2,1},{3,2},{4,3},{5,4},{6,5},{7,6},{8,15},{9,8},{10,9... | collective-permute-start | bytes 2359304 | tf_op jit(solution)/shard_map/ppermute | solution.py:338
  30.0 7.7 %collective-permute-done.1.refs_0_ = f32[1536,128]{1,0:T(8,128)} collective-permute-done((f32[1536,128]{1,0:T(8,128)S(1)}, f32[1536,128]{1,0:T(8,128)}, u32[]{:S(2)}, u32[]{:S(2)}) %collective-permute-start.1) | collective-permute-done | bytes 786464 | tf_op jit(solution)/shard_map/ppermute | solution.py:337
  37.7 1.9 collective-permute-start.3
  40.6 4.2 %all-to-all-start = ((f32[8,144,128]{2,1,0:T(8,128)}), f32[8,144,128]{2,1,0:T(8,128)}, u32[]{:S(2)}, u32[]{:S(2)}) async-start(f32[8,144,128]{2,1,0:T(8,128)} %shard_map.82), calls=%async_computation | async-start | bytes 1179648 | tf_op jit(solution)/shard_map/all_to_all | solution.py:55
  46.5 4.4 %collective-permute-start.5 = (f32[1536,128]{1,0:T(8,128)S(1)}, f32[1536,128]{1,0:T(8,128)}, u32[]{:S(2)}, u32[]{:S(2)}) collective-permute-start(f32[1536,128]{1,0:T(8,128)S(1)} %collective-permute-done.4.refs_1_), channel_id=1, source_target_pairs={{0,7},{1,0},{2,1},{3,2},{4,3},{5,4},{6,5},{7,6},{8,15},{9,8},{10,9... | collective-permute-start | bytes 2359304 | tf_op jit(solution)/shard_map/ppermute | solution.py:338
  53.1 1.9 collective-permute-start.6
  59.4 1.9 convert_reduce_fusion.1
  65.8 2.0 shard_map.88
  69.3 16.3 %all_to_all.65.parts_ref = f32[8,72,128]{2,1,0:T(8,128)S(1)} all-to-all(f32[8,72,128]{2,1,0:T(8,128)S(1)} %get-tuple-element.30), channel_id=1, replica_groups={{0,8,16,24,32,40,48,56},{1,9,17,25,33,41,49,57},{2,10,18,26,34,42,50,58..., dimensions={0} | all-to-all | bytes 589824 | tf_op jit(solution)/shard_map/all_to_all | solution.py:55
  85.6 12.1 %all_to_all.66.error_ref = f32[8,72,128]{2,1,0:T(8,128)S(1)} all-to-all(f32[8,72,128]{2,1,0:T(8,128)S(1)} %shard_map.90), channel_id=1, replica_groups={{0,8,16,24,32,40,48,56},{1,9,17,25,33,41,49,57},{2,10,18,26,34,42,50,58..., dimensions={0} | all-to-all | bytes 589824 | tf_op jit(solution)/shard_map/all_to_all | solution.py:55
  99.2 12.1 %all_to_all.67.parts_ref = f32[8,72,128]{2,1,0:T(8,128)S(1)} all-to-all(f32[8,72,128]{2,1,0:T(8,128)S(1)} %get-tuple-element.33), channel_id=1, replica_groups={{0,8,16,24,32,40,48,56},{1,9,17,25,33,41,49,57},{2,10,18,26,34,42,50,58..., dimensions={0} | all-to-all | bytes 589824 | tf_op jit(solution)/shard_map/all_to_all | solution.py:55
  111.3 12.1 %all_to_all.68.error_ref = f32[8,72,128]{2,1,0:T(8,128)S(1)} all-to-all(f32[8,72,128]{2,1,0:T(8,128)S(1)} %shard_map.92), channel_id=1, replica_groups={{0,8,16,24,32,40,48,56},{1,9,17,25,33,41,49,57},{2,10,18,26,34,42,50,58..., dimensions={0} | all-to-all | bytes 589824 | tf_op jit(solution)/shard_map/all_to_all | solution.py:55
  124.9 12.1 %all_to_all.69.parts_ref = f32[8,72,128]{2,1,0:T(8,128)S(1)} all-to-all(f32[8,72,128]{2,1,0:T(8,128)S(1)} %get-tuple-element.35), channel_id=1, replica_groups={{0,8,16,24,32,40,48,56},{1,9,17,25,33,41,49,57},{2,10,18,26,34,42,50,58..., dimensions={0} | all-to-all | bytes 589824 | tf_op jit(solution)/shard_map/all_to_all | solution.py:55
  137.0 12.1 %all_to_all.70.error_ref = f32[8,72,128]{2,1,0:T(8,128)S(1)} all-to-all(f32[8,72,128]{2,1,0:T(8,128)S(1)} %shard_map.94), channel_id=1, replica_groups={{0,8,16,24,32,40,48,56},{1,9,17,25,33,41,49,57},{2,10,18,26,34,42,50,58..., dimensions={0} | all-to-all | bytes 589824 | tf_op jit(solution)/shard_map/all_to_all | solution.py:55
  150.6 12.1 %all_to_all.71.parts_ref = f32[8,72,128]{2,1,0:T(8,128)S(1)} all-to-all(f32[8,72,128]{2,1,0:T(8,128)S(1)} %get-tuple-element.37), channel_id=1, replica_groups={{0,8,16,24,32,40,48,56},{1,9,17,25,33,41,49,57},{2,10,18,26,34,42,50,58..., dimensions={0} | all-to-all | bytes 589824 | tf_op jit(solution)/shard_map/all_to_all | solution.py:55
  162.7 12.1 %all_to_all.72.error_ref = f32[8,72,128]{2,1,0:T(8,128)S(1)} all-to-all(f32[8,72,128]{2,1,0:T(8,128)S(1)} %shard_map.96), channel_id=1, replica_groups={{0,8,16,24,32,40,48,56},{1,9,17,25,33,41,49,57},{2,10,18,26,34,42,50,58..., dimensions={0} | all-to-all | bytes 589824 | tf_op jit(solution)/shard_map/all_to_all | solution.py:55
  175.5 14.8 %all_to_all.73.parts_ref = f32[8,48,128]{2,1,0:T(8,128)S(1)} all-to-all(f32[8,48,128]{2,1,0:T(8,128)S(1)} %shard_map.97), channel_id=1, replica_groups={{0,1,2,3,4,5,6,7},{8,9,10,11,12,13,14,15},{16,17,18,19,20,21,22,23},{24..., dimensions={0} | all-to-all | bytes 393216 | tf_op jit(solution)/shard_map/all_to_all | solution.py:55
  190.5 26.0 %all_to_all.74.updates_ref = f32[8,16,384]{2,1,0:T(8,128)S(1)} all-to-all(f32[8,16,384]{2,1,0:T(8,128)S(1)} %shard_map.98), channel_id=1, replica_groups=mesh['x'=4,'core'=2,'z'=8,'y'=8] {'x','core'}, dimensions={0} | all-to-all | bytes 393216 | tf_op jit(solution)/shard_map/all_to_all | solution.py:55
  216.7 7.9 %all_to_all.75.parts_ref = f32[8,1,128]{2,1,0:T(1,128)S(1)} all-to-all(f32[8,1,128]{2,1,0:T(1,128)S(1)} %shard_map.99), channel_id=1, replica_groups=mesh['x'=4,'core'=2,'z'=8,'y'=8] {'x','core'}, dimensions={0} | all-to-all | bytes 8192 | tf_op jit(solution)/shard_map/all_to_all | solution.py:55
  224.6 14.6 %all_to_all.76.parts_ref = f32[64,1,128]{2,1,0:T(1,128)S(1)} all-to-all(f32[64,1,128]{2,1,0:T(1,128)S(1)} %shard_map.100), channel_id=1, replica_groups=mesh['x'=4,'core'=2,'z'=8,'y'=8] {'z','y'}, dimensions={0} | all-to-all | bytes 65536 | tf_op jit(solution)/shard_map/all_to_all | solution.py:55
  (52 shorter events, 24.1 us)
Async XLA Ops:
  0.0 46.4 %copy-start = (bf16[1024,384]{1,0:T(8,128)(2,1)S(1)}, bf16[1024,384]{1,0:T(8,128)(2,1)}, u32[]{:S(2)}) copy-start(bf16[1024,384]{1,0:T(8,128)(2,1)} %param.14) | copy-start | bytes 2359300
  0.0 1.0 copy-start.2
  1.0 0.9 copy-start.4
  2.2 21.2 %collective-permute-start = (f32[1536,128]{1,0:T(8,128)S(1)}, f32[1536,128]{1,0:T(8,128)S(1)}, u32[]{:S(2)}, u32[]{:S(2)}) collective-permute-start(f32[1536,128]{1,0:T(8,128)S(1)} %shard_map.83.refs_0_), channel_id=1, source_target_pairs={{0,1},{1,2},{2,3},{3,4},{4,5},{5,6},{6,7},{7,0},{8,9},{9,10},{10,1... | collective-permute-start | bytes 2359304 | tf_op jit(solution)/shard_map/ppermute | solution.py:337
  7.0 18.2 %collective-permute-start.2 = (f32[1536,128]{1,0:T(8,128)S(1)}, f32[1536,128]{1,0:T(8,128)S(1)}, u32[]{:S(2)}, u32[]{:S(2)}) collective-permute-start(f32[1536,128]{1,0:T(8,128)S(1)} %shard_map.83.refs_0_), channel_id=1, source_target_pairs={{0,7},{1,0},{2,1},{3,2},{4,3},{5,4},{6,5},{7,6},{8,15},{9,8},{10,9... | collective-permute-start | bytes 2359304 | tf_op jit(solution)/shard_map/ppermute | solution.py:338
  15.7 23.9 %copy-start.5 = (bf16[128,384]{1,0:T(8,128)(2,1)S(1)}, bf16[128,384]{1,0:T(8,128)(2,1)}, u32[]{:S(2)}) copy-start(bf16[128,384]{1,0:T(8,128)(2,1)} %w_ref.1) | copy-start | bytes 294916
  15.7 23.9 %copy-start.6 = (bf16[1,128,384]{2,1,0:T(8,128)(2,1)S(1)}, bf16[1,128,384]{2,1,0:T(8,128)(2,1)}, u32[]{:S(2)}) copy-start(bf16[1,128,384]{2,1,0:T(8,128)(2,1)} %param.9) | copy-start | bytes 294916
  15.7 23.9 %copy-start.7 = (bf16[1,128,384]{2,1,0:T(8,128)(2,1)S(1)}, bf16[1,128,384]{2,1,0:T(8,128)(2,1)}, u32[]{:S(2)}) copy-start(bf16[1,128,384]{2,1,0:T(8,128)(2,1)} %param.10) | copy-start | bytes 294916
  23.4 14.3 %collective-permute-start.1 = (f32[1536,128]{1,0:T(8,128)S(1)}, f32[1536,128]{1,0:T(8,128)}, u32[]{:S(2)}, u32[]{:S(2)}) collective-permute-start(f32[1536,128]{1,0:T(8,128)S(1)} %collective-permute-done.refs_0_), channel_id=1, source_target_pairs={{0,1},{1,2},{2,3},{3,4},{4,5},{5,6},{6,7},{7,0},{8,9},{9,10},{10,1... | collective-permute-start | bytes 2359304 | tf_op jit(solution)/shard_map/ppermute | solution.py:337
  25.3 21.2 %collective-permute-start.4 = (f32[1536,128]{1,0:T(8,128)S(1)}, f32[1536,128]{1,0:T(8,128)S(1)}, u32[]{:S(2)}, u32[]{:S(2)}) collective-permute-start(f32[1536,128]{1,0:T(8,128)S(1)} %collective-permute-done.2.refs_1_), channel_id=1, source_target_pairs={{0,7},{1,0},{2,1},{3,2},{4,3},{5,4},{6,5},{7,6},{8,15},{9,8},{10,9... | collective-permute-start | bytes 2359304 | tf_op jit(solution)/shard_map/ppermute | solution.py:338
  37.7 15.4 %collective-permute-start.3 = (f32[1536,128]{1,0:T(8,128)}, f32[1536,128]{1,0:T(8,128)}, u32[]{:S(2)}, u32[]{:S(2)}) collective-permute-start(f32[1536,128]{1,0:T(8,128)} %collective-permute-done.1.refs_0_), channel_id=1, source_target_pairs={{0,1},{1,2},{2,3},{3,4},{4,5},{5,6},{6,7},{7,0},{8,9},{9,10},{10,1... | collective-permute-start | bytes 2359304 | tf_op jit(solution)/shard_map/ppermute | solution.py:337
  40.6 23.4 %all-to-all-start = ((f32[8,144,128]{2,1,0:T(8,128)}), f32[8,144,128]{2,1,0:T(8,128)}, u32[]{:S(2)}, u32[]{:S(2)}) async-start(f32[8,144,128]{2,1,0:T(8,128)} %shard_map.82), calls=%async_computation | async-start | bytes 1179648 | tf_op jit(solution)/shard_map/all_to_all | solution.py:55
  46.5 16.1 %collective-permute-start.5 = (f32[1536,128]{1,0:T(8,128)S(1)}, f32[1536,128]{1,0:T(8,128)}, u32[]{:S(2)}, u32[]{:S(2)}) collective-permute-start(f32[1536,128]{1,0:T(8,128)S(1)} %collective-permute-done.4.refs_1_), channel_id=1, source_target_pairs={{0,7},{1,0},{2,1},{3,2},{4,3},{5,4},{6,5},{7,6},{8,15},{9,8},{10,9... | collective-permute-start | bytes 2359304 | tf_op jit(solution)/shard_map/ppermute | solution.py:338
  53.1 14.7 %collective-permute-start.6 = (f32[1536,128]{1,0:T(8,128)}, f32[1536,128]{1,0:T(8,128)}, u32[]{:S(2)}, u32[]{:S(2)}) collective-permute-start(f32[1536,128]{1,0:T(8,128)} %collective-permute-done.3.refs_0_), channel_id=1, source_target_pairs={{0,1},{1,2},{2,3},{3,4},{4,5},{5,6},{6,7},{7,0},{8,9},{9,10},{10,1... | collective-permute-start | bytes 2359304 | tf_op jit(solution)/shard_map/ppermute | solution.py:341
  64.1 0.9 copy-start.1
  65.0 0.8 copy-start.3

commit v3 on v2

--- a/solution.py
+++ b/solution.py
@@ -49,6 +49,7 @@
 
 UP = [(group[i], group[(i + 1) % SIDE]) for group in GATHER_GROUPS for i in range(SIDE)]
 DOWN = [(group[i], group[(i - 1) % SIDE]) for group in GATHER_GROUPS for i in range(SIDE)]
+ACROSS = [(group[i], group[(i + 4) % SIDE]) for group in GATHER_GROUPS for i in range(SIDE)]
 
 
 def exchange(blocks, axes, groups=None):
@@ -134,7 +135,7 @@
 def early_kernel(
     place_ref, start_ref, target_ref, count_ref, own_ref, *refs
 ):
-    pairs, (states_ref, constant_ref, part_ref) = refs[:3], refs[3:]
+    pairs, (states_ref, constant_ref, part_ref) = refs[:2], refs[2:]
     place = place_ref[0]
     for k, offset in enumerate(OFFSETS):
         states_ref[k] = start_ref[lax.rem(place + (offset + SIDE), SIDE)]
@@ -150,19 +151,20 @@
         part_ref[:, rows] = part
 
 
-def late_kernel(states_ref, own_ref, opposite_ref, part_ref, table_ref, out_ref):
-    table_ref[:, :LANES] = own_ref[...]
-    table_ref[:, LANES:] = opposite_ref[...].astype(BF16)
-    weights = states_ref[1, :COLS, :].astype(BF16)
-    output = jnp.concatenate(
-        [
-            part_ref[:, row : row + WIDE]
-            + turned_product(weights, table_ref[row : row + WIDE, LANES:])
-            for row in range(0, TABLE, WIDE)
-        ],
-        axis=1,
-    )
-    store_output(out_ref, output)
+def late_kernel(
+    states_ref, upward_ref, downward_ref, opposite_ref, part_ref, pair_ref, single_ref, out_ref
+):
+    pair_ref[:, :LANES] = upward_ref[...].astype(BF16)
+    pair_ref[:, LANES:] = downward_ref[...].astype(BF16)
+    single_ref[...] = opposite_ref[...].astype(BF16)
+    weights = jnp.concatenate([states_ref[k, :COLS, :] for k in (6, 7)], axis=1).astype(BF16)
+    single = states_ref[1, :COLS, :].astype(BF16)
+    output = []
+    for row in range(0, TABLE, WIDE):
+        rows = slice(row, row + WIDE)
+        part = part_ref[:, rows] + turned_product(weights, pair_ref[rows, :])
+        output.append(part + turned_product(single, single_ref[rows, :]))
+    store_output(out_ref, jnp.concatenate(output, axis=1))
 
 
 def error_kernel(step, parts_ref, constant_ref, out_ref):
@@ -176,7 +178,8 @@
 
 
 def step_kernel(first, last, place_ref, error_ref, *refs):
-    tables, (w_ref, states_ref, *rest) = refs[: SIDE // 2], refs[SIDE // 2 :]
+    own, opposite, *pairs = refs[:5]
+    w_ref, states_ref, *rest = refs[5:]
     if last:
         (total_out,) = rest
         place = place_ref[0]
@@ -195,7 +198,11 @@
     both = jnp.concatenate([high, low], axis=0)
     updated = []
     for k in range(SIDE // 2):
-        product = jnp.dot(both, tables[k][...], preferred_element_type=F32)
+        if k == 0:
+            columns = jnp.concatenate([own[...], opposite[...]], axis=1)
+        else:
+            columns = pairs[k - 1][...]
+        product = jnp.dot(both, columns, preferred_element_type=F32)
         gradients = (product[:COLS] + product[COLS:]) * (1.0 / TOKENS)
         for half in range(2):
             j = 2 * k + half
@@ -228,7 +235,7 @@
     output = []
     for row in range(0, TABLE, WIDE):
         rows = slice(row, row + WIDE)
-        table_rows = jnp.concatenate([table[rows, :] for table in tables], axis=1)
+        table_rows = jnp.concatenate([table[rows, :] for table in refs[:5]], axis=1)
         output.append(turned_product(weights, table_rows))
     store_output(output_ref, jnp.concatenate(output, axis=1))
 
@@ -329,16 +336,17 @@
     gather_place = jnp.where(core == 0, y, z)
 
     own = widened(shared_inputs, private_inputs[0])
-    tables = [narrowed(own)]
+    own_table = narrowed(own)
+    tables = []
     upward = downward = own
     for hop in range(3):
-        if hop >= 1:
-            upward, tables[hop - 1] = lax.optimization_barrier((upward, tables[hop - 1]))
+        if hop >= 2:
+            upward, tables[hop - 2] = lax.optimization_barrier((upward, tables[hop - 2]))
         upward = lax.ppermute(upward, CZY, UP)
         downward = lax.ppermute(downward, CZY, DOWN)
-        tables.append(narrowed(upward, downward))
-    opposite, tables[2] = lax.optimization_barrier((upward, tables[2]))
-    opposite = lax.ppermute(opposite, CZY, UP)
+        if hop == 0:
+            opposite = lax.ppermute(own, CZY, ACROSS)
+        tables.append(narrowed(upward, downward) if hop < 2 else None)
 
     start = kernel_call(
         states_kernel, shaped(SIDE, 3 * COLS, LANES), weight, first_moment[0], second_moment[0]
@@ -359,13 +367,19 @@
         start,
         targets,
         counts,
-        *tables,
-    )
-    tables[0], parts = kernel_call(
+        own_table,
+        *tables[:2],
+    )
+    tables[2], opposite, parts = kernel_call(
         late_kernel,
-        [shaped(TABLE, WIDE, dtype=BF16), shaped(SIDE, TILE, LANES)],
+        [
+            shaped(TABLE, WIDE, dtype=BF16),
+            shaped(TABLE, LANES, dtype=BF16),
+            shaped(SIDE, TILE, LANES),
+        ],
         start,
-        tables[0],
+        upward,
+        downward,
         opposite,
         part,
     )
@@ -378,7 +392,7 @@
         error = exchange(error, CZY, SUM_GROUPS)
         last = step == STEPS - 1
         body = functools.partial(step_kernel, step == 0, last)
-        operands = (place, error, *tables, start, states)
+        operands = (place, error, own_table, opposite, *tables, start, states)
         if last:
             updates = kernel_call(body, shaped(SIDE, COLS, LANES), *operands)
         else:

time: 241 us -> 246 us (1.021)
  starting transfers between devices: 32.4 us -> 37.7 us
  waiting for transfers between devices: 16.9 us -> 20.2 us
    ppermute x3, waiting for transfers between devices: 0.55 us -> 12.3 us  [on_device(): downward = lax.ppermute(downward, CZY, DOWN)]
    ppermute x3, waiting for transfers between devices: 16.3 us -> 7.84 us  [on_device(): upward = lax.ppermute(upward, CZY, UP)]
    ppermute x1, starting transfers between devices: 1.91 us -> 4.54 us  [on_device(): opposite = lax.ppermute(own, CZY, ACROSS)]
    unnamed x17 -> x19, local copies, waits for them, and re-layouts: 5.08 us -> 3.71 us
    pallas_call x19 -> x18, Pallas kernels: 14.1 us -> 14.6 us  [kernel_call(): pl.pallas_call(body, in_specs=in_specs, out_shape=out_shapes, compiler_pa...]
  transfers between devices with their start and end apart: 8 -> 8, of which waited for: 4 -> 3; matrix products, arithmetic and copies ran while one was open for 4% -> 2% of each run, Pallas kernels for 2% -> 2%
where the time goes in v3:
time: 246 us; the launch traced here: 245 us
  blocking collectives  164 us (67%)
  starting transfers between devices  37.7 us (15%)
  waiting for transfers between devices  20.2 us (8%)
  Pallas kernels  14.8 us (6%)
  local copies, waits for them, and re-layouts  4.72 us (2%)
  other arithmetic  3.66 us (1%)
    all_to_all x12, blocking collectives, exchange(): lax.all_to_all(blocks, axes, split_axis=0, concat_axis=0, tiled=True, axi...  164 us
    ppermute x3, starting transfers between devices, on_device(): downward = lax.ppermute(downward, CZY, DOWN)  19 us
    pallas_call x18, Pallas kernels, kernel_call(): pl.pallas_call(body, in_specs=in_specs, out_shape=out_shapes, compiler_pa...  14.6 us
    ppermute x3, waiting for transfers between devices, on_device(): downward = lax.ppermute(downward, CZY, DOWN)  12.3 us
    ppermute x3, starting transfers between devices, on_device(): upward = lax.ppermute(upward, CZY, UP)  9.93 us
    ppermute x3, waiting for transfers between devices, on_device(): upward = lax.ppermute(upward, CZY, UP)  7.84 us
  transfers between devices with their start and end apart: 8, of which 3 were waited for; matrix products, arithmetic and copies ran while one was open for 2% of the time, Pallas kernels for 2%

profile of v3, /device:TPU:1, one launch (start us, length us, event | category | flops | bytes accessed | tf_op | source)
XLA Modules:
  0.0 244.9 jit_solution(16871693276793593616)
XLA Ops:
  2.2 4.8 %collective-permute-start = (f32[1536,128]{1,0:T(8,128)S(1)}, f32[1536,128]{1,0:T(8,128)}, u32[]{:S(2)}, u32[]{:S(2)}) collective-permute-start(f32[1536,128]{1,0:T(8,128)S(1)} %shard_map.83.refs_0_), channel_id=1, source_target_pairs={{0,1},{1,2},{2,3},{3,4},{4,5},{5,6},{6,7},{7,0},{8,9},{9,10},{10,1... | collective-permute-start | bytes 2359304 | tf_op jit(solution)/shard_map/ppermute | solution.py:345
  7.0 8.6 %collective-permute-start.2 = (f32[1536,128]{1,0:T(8,128)S(1)}, f32[1536,128]{1,0:T(8,128)S(1)}, u32[]{:S(2)}, u32[]{:S(2)}) collective-permute-start(f32[1536,128]{1,0:T(8,128)S(1)} %shard_map.83.refs_0_), channel_id=1, source_target_pairs={{0,7},{1,0},{2,1},{3,2},{4,3},{5,4},{6,5},{7,6},{8,15},{9,8},{10,9... | collective-permute-start | bytes 2359304 | tf_op jit(solution)/shard_map/ppermute | solution.py:346
  15.6 7.8 %collective-permute-done.refs_0_ = f32[1536,128]{1,0:T(8,128)} collective-permute-done((f32[1536,128]{1,0:T(8,128)S(1)}, f32[1536,128]{1,0:T(8,128)}, u32[]{:S(2)}, u32[]{:S(2)}) %collective-permute-start) | collective-permute-done | bytes 786464 | tf_op jit(solution)/shard_map/ppermute | solution.py:345
  23.5 1.9 collective-permute-start.1
  25.4 4.6 %collective-permute-start.3 = (f32[1536,128]{1,0:T(8,128)S(1)}, f32[1536,128]{1,0:T(8,128)}, u32[]{:S(2)}, u32[]{:S(2)}) collective-permute-start(f32[1536,128]{1,0:T(8,128)S(1)} %collective-permute-done.2.refs_1_), channel_id=1, source_target_pairs={{0,7},{1,0},{2,1},{3,2},{4,3},{5,4},{6,5},{7,6},{8,15},{9,8},{10,9... | collective-permute-start | bytes 2359304 | tf_op jit(solution)/shard_map/ppermute | solution.py:346
  30.0 4.5 %collective-permute-start.6 = (f32[1536,128]{1,0:T(8,128)S(1)}, f32[1536,128]{1,0:T(8,128)}, u32[]{:S(2)}, u32[]{:S(2)}) collective-permute-start(f32[1536,128]{1,0:T(8,128)S(1)} %shard_map.83.refs_0_), channel_id=1, source_target_pairs={{0,4},{1,5},{2,6},{3,7},{4,0},{5,1},{6,2},{7,3},{8,12},{9,13},{10,... | collective-permute-start | bytes 2359304 | tf_op jit(solution)/shard_map/ppermute | solution.py:348
  35.6 4.2 %all-to-all-start = ((f32[8,144,128]{2,1,0:T(8,128)}), f32[8,144,128]{2,1,0:T(8,128)}, u32[]{:S(2)}, u32[]{:S(2)}) async-start(f32[8,144,128]{2,1,0:T(8,128)} %shard_map.82), calls=%async_computation | async-start | bytes 1179648 | tf_op jit(solution)/shard_map/all_to_all | solution.py:56
  42.6 3.2 %collective-permute-start.4 = (f32[1536,128]{1,0:T(8,128)}, f32[1536,128]{1,0:T(8,128)}, u32[]{:S(2)}, u32[]{:S(2)}) collective-permute-start(f32[1536,128]{1,0:T(8,128)} %collective-permute-done.1.refs_0_), channel_id=1, source_target_pairs={{0,1},{1,2},{2,3},{3,4},{4,5},{5,6},{6,7},{7,0},{8,9},{9,10},{10,1... | collective-permute-start | bytes 2359304 | tf_op jit(solution)/shard_map/ppermute | solution.py:345
  45.8 11.4 %collective-permute-done.3.refs_1_ = f32[1536,128]{1,0:T(8,128)} collective-permute-done((f32[1536,128]{1,0:T(8,128)S(1)}, f32[1536,128]{1,0:T(8,128)}, u32[]{:S(2)}, u32[]{:S(2)}) %collective-permute-start.3) | collective-permute-done | bytes 786464 | tf_op jit(solution)/shard_map/ppermute | solution.py:346
  57.2 5.9 %collective-permute-start.5 = (f32[1536,128]{1,0:T(8,128)}, f32[1536,128]{1,0:T(8,128)}, u32[]{:S(2)}, u32[]{:S(2)}) collective-permute-start(f32[1536,128]{1,0:T(8,128)} %collective-permute-done.3.refs_1_), channel_id=1, source_target_pairs={{0,7},{1,0},{2,1},{3,2},{4,3},{5,4},{6,5},{7,6},{8,15},{9,8},{10,9... | collective-permute-start | bytes 2359304 | tf_op jit(solution)/shard_map/ppermute | solution.py:346
  69.5 1.8 shard_map.87
  72.3 2.1 shard_map.88
  74.4 16.0 %all_to_all.65.parts_ref = f32[8,72,128]{2,1,0:T(8,128)S(1)} all-to-all(f32[8,72,128]{2,1,0:T(8,128)S(1)} %get-tuple-element.23), channel_id=1, replica_groups={{0,8,16,24,32,40,48,56},{1,9,17,25,33,41,49,57},{2,10,18,26,34,42,50,58..., dimensions={0} | all-to-all | bytes 589824 | tf_op jit(solution)/shard_map/all_to_all | solution.py:56
  90.5 12.3 %all_to_all.66.error_ref = f32[8,72,128]{2,1,0:T(8,128)S(1)} all-to-all(f32[8,72,128]{2,1,0:T(8,128)S(1)} %shard_map.89), channel_id=1, replica_groups={{0,8,16,24,32,40,48,56},{1,9,17,25,33,41,49,57},{2,10,18,26,34,42,50,58..., dimensions={0} | all-to-all | bytes 589824 | tf_op jit(solution)/shard_map/all_to_all | solution.py:56
  104.4 12.1 %all_to_all.67.parts_ref = f32[8,72,128]{2,1,0:T(8,128)S(1)} all-to-all(f32[8,72,128]{2,1,0:T(8,128)S(1)} %get-tuple-element.27), channel_id=1, replica_groups={{0,8,16,24,32,40,48,56},{1,9,17,25,33,41,49,57},{2,10,18,26,34,42,50,58..., dimensions={0} | all-to-all | bytes 589824 | tf_op jit(solution)/shard_map/all_to_all | solution.py:56
  116.5 12.1 %all_to_all.68.error_ref = f32[8,72,128]{2,1,0:T(8,128)S(1)} all-to-all(f32[8,72,128]{2,1,0:T(8,128)S(1)} %shard_map.91), channel_id=1, replica_groups={{0,8,16,24,32,40,48,56},{1,9,17,25,33,41,49,57},{2,10,18,26,34,42,50,58..., dimensions={0} | all-to-all | bytes 589824 | tf_op jit(solution)/shard_map/all_to_all | solution.py:56
  130.2 12.1 %all_to_all.69.parts_ref = f32[8,72,128]{2,1,0:T(8,128)S(1)} all-to-all(f32[8,72,128]{2,1,0:T(8,128)S(1)} %get-tuple-element.29), channel_id=1, replica_groups={{0,8,16,24,32,40,48,56},{1,9,17,25,33,41,49,57},{2,10,18,26,34,42,50,58..., dimensions={0} | all-to-all | bytes 589824 | tf_op jit(solution)/shard_map/all_to_all | solution.py:56
  142.3 12.1 %all_to_all.70.error_ref = f32[8,72,128]{2,1,0:T(8,128)S(1)} all-to-all(f32[8,72,128]{2,1,0:T(8,128)S(1)} %shard_map.93), channel_id=1, replica_groups={{0,8,16,24,32,40,48,56},{1,9,17,25,33,41,49,57},{2,10,18,26,34,42,50,58..., dimensions={0} | all-to-all | bytes 589824 | tf_op jit(solution)/shard_map/all_to_all | solution.py:56
  155.9 12.1 %all_to_all.71.parts_ref = f32[8,72,128]{2,1,0:T(8,128)S(1)} all-to-all(f32[8,72,128]{2,1,0:T(8,128)S(1)} %get-tuple-element.31), channel_id=1, replica_groups={{0,8,16,24,32,40,48,56},{1,9,17,25,33,41,49,57},{2,10,18,26,34,42,50,58..., dimensions={0} | all-to-all | bytes 589824 | tf_op jit(solution)/shard_map/all_to_all | solution.py:56
  168.0 12.1 %all_to_all.72.error_ref = f32[8,72,128]{2,1,0:T(8,128)S(1)} all-to-all(f32[8,72,128]{2,1,0:T(8,128)S(1)} %shard_map.95), channel_id=1, replica_groups={{0,8,16,24,32,40,48,56},{1,9,17,25,33,41,49,57},{2,10,18,26,34,42,50,58..., dimensions={0} | all-to-all | bytes 589824 | tf_op jit(solution)/shard_map/all_to_all | solution.py:56
  180.8 14.5 %all_to_all.73.parts_ref = f32[8,48,128]{2,1,0:T(8,128)S(1)} all-to-all(f32[8,48,128]{2,1,0:T(8,128)S(1)} %shard_map.96), channel_id=1, replica_groups={{0,1,2,3,4,5,6,7},{8,9,10,11,12,13,14,15},{16,17,18,19,20,21,22,23},{24..., dimensions={0} | all-to-all | bytes 393216 | tf_op jit(solution)/shard_map/all_to_all | solution.py:56
  195.5 25.9 %all_to_all.74.updates_ref = f32[8,16,384]{2,1,0:T(8,128)S(1)} all-to-all(f32[8,16,384]{2,1,0:T(8,128)S(1)} %shard_map.97), channel_id=1, replica_groups=mesh['x'=4,'core'=2,'z'=8,'y'=8] {'x','core'}, dimensions={0} | all-to-all | bytes 393216 | tf_op jit(solution)/shard_map/all_to_all | solution.py:56
  221.6 7.9 %all_to_all.75.parts_ref = f32[8,1,128]{2,1,0:T(1,128)S(1)} all-to-all(f32[8,1,128]{2,1,0:T(1,128)S(1)} %shard_map.98), channel_id=1, replica_groups=mesh['x'=4,'core'=2,'z'=8,'y'=8] {'x','core'}, dimensions={0} | all-to-all | bytes 8192 | tf_op jit(solution)/shard_map/all_to_all | solution.py:56
  229.5 14.6 %all_to_all.76.parts_ref = f32[64,1,128]{2,1,0:T(1,128)S(1)} all-to-all(f32[64,1,128]{2,1,0:T(1,128)S(1)} %shard_map.99), channel_id=1, replica_groups=mesh['x'=4,'core'=2,'z'=8,'y'=8] {'z','y'}, dimensions={0} | all-to-all | bytes 65536 | tf_op jit(solution)/shard_map/all_to_all | solution.py:56
  (53 shorter events, 20.2 us)
Async XLA Ops:
  0.0 41.4 %copy-start = (bf16[1024,384]{1,0:T(8,128)(2,1)S(1)}, bf16[1024,384]{1,0:T(8,128)(2,1)}, u32[]{:S(2)}) copy-start(bf16[1024,384]{1,0:T(8,128)(2,1)} %param.14) | copy-start | bytes 2359300
  0.0 1.0 copy-start.2
  1.0 0.9 copy-start.4
  1.9 32.6 %copy-start.5 = (bf16[128,384]{1,0:T(8,128)(2,1)S(1)}, bf16[128,384]{1,0:T(8,128)(2,1)}, u32[]{:S(2)}) copy-start(bf16[128,384]{1,0:T(8,128)(2,1)} %w_ref.1) | copy-start | bytes 294916
  1.9 32.6 %copy-start.6 = (bf16[1,128,384]{2,1,0:T(8,128)(2,1)S(1)}, bf16[1,128,384]{2,1,0:T(8,128)(2,1)}, u32[]{:S(2)}) copy-start(bf16[1,128,384]{2,1,0:T(8,128)(2,1)} %param.9) | copy-start | bytes 294916
  1.9 32.6 %copy-start.7 = (bf16[1,128,384]{2,1,0:T(8,128)(2,1)S(1)}, bf16[1,128,384]{2,1,0:T(8,128)(2,1)}, u32[]{:S(2)}) copy-start(bf16[1,128,384]{2,1,0:T(8,128)(2,1)} %param.10) | copy-start | bytes 294916
  2.2 21.3 %collective-permute-start = (f32[1536,128]{1,0:T(8,128)S(1)}, f32[1536,128]{1,0:T(8,128)}, u32[]{:S(2)}, u32[]{:S(2)}) collective-permute-start(f32[1536,128]{1,0:T(8,128)S(1)} %shard_map.83.refs_0_), channel_id=1, source_target_pairs={{0,1},{1,2},{2,3},{3,4},{4,5},{5,6},{6,7},{7,0},{8,9},{9,10},{10,1... | collective-permute-start | bytes 2359304 | tf_op jit(solution)/shard_map/ppermute | solution.py:345
  7.0 18.4 %collective-permute-start.2 = (f32[1536,128]{1,0:T(8,128)S(1)}, f32[1536,128]{1,0:T(8,128)S(1)}, u32[]{:S(2)}, u32[]{:S(2)}) collective-permute-start(f32[1536,128]{1,0:T(8,128)S(1)} %shard_map.83.refs_0_), channel_id=1, source_target_pairs={{0,7},{1,0},{2,1},{3,2},{4,3},{5,4},{6,5},{7,6},{8,15},{9,8},{10,9... | collective-permute-start | bytes 2359304 | tf_op jit(solution)/shard_map/ppermute | solution.py:346
  23.5 19.2 %collective-permute-start.1 = (f32[1536,128]{1,0:T(8,128)}, f32[1536,128]{1,0:T(8,128)}, u32[]{:S(2)}, u32[]{:S(2)}) collective-permute-start(f32[1536,128]{1,0:T(8,128)} %collective-permute-done.refs_0_), channel_id=1, source_target_pairs={{0,1},{1,2},{2,3},{3,4},{4,5},{5,6},{6,7},{7,0},{8,9},{9,10},{10,1... | collective-permute-start | bytes 2359304 | tf_op jit(solution)/shard_map/ppermute | solution.py:345
  25.4 31.8 %collective-permute-start.3 = (f32[1536,128]{1,0:T(8,128)S(1)}, f32[1536,128]{1,0:T(8,128)}, u32[]{:S(2)}, u32[]{:S(2)}) collective-permute-start(f32[1536,128]{1,0:T(8,128)S(1)} %collective-permute-done.2.refs_1_), channel_id=1, source_target_pairs={{0,7},{1,0},{2,1},{3,2},{4,3},{5,4},{6,5},{7,6},{8,15},{9,8},{10,9... | collective-permute-start | bytes 2359304 | tf_op jit(solution)/shard_map/ppermute | solution.py:346
  30.0 41.4 %collective-permute-start.6 = (f32[1536,128]{1,0:T(8,128)S(1)}, f32[1536,128]{1,0:T(8,128)}, u32[]{:S(2)}, u32[]{:S(2)}) collective-permute-start(f32[1536,128]{1,0:T(8,128)S(1)} %shard_map.83.refs_0_), channel_id=1, source_target_pairs={{0,4},{1,5},{2,6},{3,7},{4,0},{5,1},{6,2},{7,3},{8,12},{9,13},{10,... | collective-permute-start | bytes 2359304 | tf_op jit(solution)/shard_map/ppermute | solution.py:348
  35.6 32.3 %all-to-all-start = ((f32[8,144,128]{2,1,0:T(8,128)}), f32[8,144,128]{2,1,0:T(8,128)}, u32[]{:S(2)}, u32[]{:S(2)}) async-start(f32[8,144,128]{2,1,0:T(8,128)} %shard_map.82), calls=%async_computation | async-start | bytes 1179648 | tf_op jit(solution)/shard_map/all_to_all | solution.py:56
  42.6 22.2 %copy-start.8 = (s32[1,4,1024]{2,1,0:T(4,128)S(1)}, s32[1,4,1024]{2,1,0:T(4,128)}, u32[]{:S(2)}) copy-start(s32[1,4,1024]{2,1,0:T(4,128)} %param.11) | copy-start | bytes 49156
  42.6 29.7 %collective-permute-start.4 = (f32[1536,128]{1,0:T(8,128)}, f32[1536,128]{1,0:T(8,128)}, u32[]{:S(2)}, u32[]{:S(2)}) collective-permute-start(f32[1536,128]{1,0:T(8,128)} %collective-permute-done.1.refs_0_), channel_id=1, source_target_pairs={{0,1},{1,2},{2,3},{3,4},{4,5},{5,6},{6,7},{7,0},{8,9},{9,10},{10,1... | collective-permute-start | bytes 2359304 | tf_op jit(solution)/shard_map/ppermute | solution.py:345
  57.2 15.1 %collective-permute-start.5 = (f32[1536,128]{1,0:T(8,128)}, f32[1536,128]{1,0:T(8,128)}, u32[]{:S(2)}, u32[]{:S(2)}) collective-permute-start(f32[1536,128]{1,0:T(8,128)} %collective-permute-done.3.refs_1_), channel_id=1, source_target_pairs={{0,7},{1,0},{2,1},{3,2},{4,3},{5,4},{6,5},{7,6},{8,15},{9,8},{10,9... | collective-permute-start | bytes 2359304 | tf_op jit(solution)/shard_map/ppermute | solution.py:346
  67.8 0.9 copy-start.1
  68.8 0.8 copy-start.3

commit v4 on v1

v4 whole, which is shorter than its diff:
```python
import functools

import jax
import jax.numpy as jnp
from jax import lax
from jax.experimental import pallas as pl
from jax.experimental.pallas import tpu as pltpu
from jax.sharding import Mesh
from jax.sharding import PartitionSpec as P

CZY = ("core", "z", "y")
F32 = jnp.float32
BF16 = jnp.bfloat16

learn_rate = 0.001
beta_one = 0.9
beta_two = 0.95
adam_eps = 1e-08
weight_decay = 0.1
norm_eps = 1e-06

SIDE = 8
LANES = 128
COLS = 48
HALF = COLS // 2
STATE = 3 * COLS
TILE = COLS + HALF
POOL = 1024
TABLE = 1536
STEPS = 4
TOKENS = 1024
REPLICAS = 8
PAIRS = [(i, j) for i in range(REPLICAS) for j in range(i, REPLICAS)]
MIB = 1024 * 1024
WIDE = 2 * LANES


def position(core, z, y):
    return (core * SIDE + z) * SIDE + y


SUM_GROUPS = [[position(0, z, y) for z in range(SIDE)] for y in range(SIDE)] + [
    [position(1, z, y) for y in range(SIDE)] for z in range(SIDE)
]
GATHER_GROUPS = [[position(0, z, y) for y in range(SIDE)] for z in range(SIDE)] + [
    [position(1, z, y) for z in range(SIDE)] for y in range(SIDE)
]


def exchange(blocks, axes, groups=None):
    return lax.all_to_all(
        blocks, axes, split_axis=0, concat_axis=0, tiled=True, axis_index_groups=groups
    )


def kernel_call(body, out_shapes, *operands, room=12):
    in_specs = [
        pl.BlockSpec(memory_space=pltpu.SMEM if operand.dtype == jnp.int32 else pltpu.VMEM)
        for operand in operands
    ]
    return pl.pallas_call(
        body,
        in_specs=in_specs,
        out_shape=out_shapes,
        compiler_params=pltpu.CompilerParams(vmem_limit_bytes=room * MIB),
    )(*operands)


def shaped(*dims, dtype=F32):
    return jax.ShapeDtypeStruct(dims, dtype)


def store_output(out_ref, output):
    for j in range(SIDE):
        out_ref[j, :COLS, :] = output[:, j * LANES : (j + 1) * LANES]
        private = POOL + (j // 2) * LANES
        line = (j % 2) * HALF
        out_ref[j, COLS:, :] = output[line : line + HALF, private : private + LANES]


def turned_product(left, right):
    return lax.dot_general(left, right, (((1,), (1,)), ((), ())), preferred_element_type=F32)


def whole_error(error_ref):
    error = jnp.concatenate(
        [error_ref[j, :COLS, :] for j in range(SIDE)]
        + [
            jnp.concatenate([error_ref[2 * k, COLS:, :], error_ref[2 * k + 1, COLS:, :]], axis=0)
            for k in range(SIDE // 2)
        ],
        axis=1,
    )
    high = error.astype(BF16)
    low = (error - high.astype(F32)).astype(BF16)
    return jnp.concatenate([high, low], axis=0)


def stepped(gradient, weight_start, moment_one, moment_two, update_sum):
    if update_sum is None:
        weight_now = weight_start
    else:
        weight_now = weight_start - learn_rate * update_sum
    moment_one = beta_one * moment_one + (1.0 - beta_one) * gradient
    moment_two = beta_two * moment_two + (1.0 - beta_two) * gradient * gradient
    direction = moment_one / (jnp.sqrt(moment_two) + adam_eps) + weight_decay * weight_now
    update_sum = direction if update_sum is None else update_sum + direction
    return moment_one, moment_two, update_sum


def widen_kernel(shared_ref, private_ref, out_ref):
    out_ref[:POOL, :] = shared_ref[...].astype(F32)
    out_ref[POOL:, :] = private_ref[...].astype(F32)


def own_kernel(slice_ref, weight_ref, out_ref):
    weights = weight_ref[...].astype(F32).T.astype(BF16)
    own = slice_ref[...].astype(BF16)
    for i in range(SIDE):
        shared = turned_product(weights, own[i * LANES : (i + 1) * LANES, :])
        for j in range(SIDE):
            out_ref[i, j * TILE : j * TILE + COLS, :] = shared[j * COLS : (j + 1) * COLS, :]
    for k in range(SIDE // 2):
        row = POOL + k * LANES
        private = turned_product(weights, own[row : row + LANES, :])
        for j in range(SIDE):
            for half in range(2):
                line = j * COLS + half * HALF
                place = j * TILE + COLS
                out_ref[2 * k + half, place : place + HALF, :] = private[line : line + HALF, :]


def constant_kernel(place_ref, ids_ref, shared_ref, private_ref, out_ref, rows, turned, arrived):
    i, j = place_ref[0], place_ref[1]
    shared_rows = pl.ds(pl.multiple_of(i * LANES, LANES), LANES)
    private_rows = pl.ds(pl.multiple_of(lax.div(i, 2) * LANES, LANES), LANES)
    copies = [
        pltpu.make_async_copy(shared_ref.at[shared_rows], rows.at[0], arrived.at[0]),
        pltpu.make_async_copy(private_ref.at[private_rows], rows.at[1], arrived.at[1]),
    ]
    for copy in copies:
        copy.start()
    row = lax.broadcasted_iota(jnp.int32, (LANES, TOKENS), 0)
    ones = jnp.ones((16, TOKENS), BF16)
    for start, lines in (
        (i * LANES, slice(0, COLS)),
        (POOL + lax.div(i, 2) * LANES, slice(COLS, TILE)),
    ):
        for step in range(STEPS):
            hits = jnp.where(ids_ref[step : step + 1, :] == row + start, 1.0, 0.0).astype(BF16)
            count = turned_product(ones, hits)[:1]
            out_ref[step, lines, :] = jnp.broadcast_to(count, (lines.stop - lines.start, LANES))
    for copy in copies:
        copy.wait()
    turned[...] = rows[0].astype(F32).T
    columns = pl.ds(pl.multiple_of(j * COLS, 8), COLS)
    out_ref[STEPS, :COLS, :] = turned[columns, :]
    turned[...] = rows[1].astype(F32).T
    columns = pl.ds(pl.multiple_of(j * COLS + lax.rem(i, 2) * HALF, 8), HALF)
    out_ref[STEPS, COLS:, :] = turned[columns, :]


def own_constants(places, ids, shared_targets, private_targets):
    return pl.pallas_call(
        constant_kernel,
        in_specs=[
            pl.BlockSpec(memory_space=pltpu.SMEM),
            pl.BlockSpec(memory_space=pltpu.VMEM),
            pl.BlockSpec(memory_space=pl.ANY),
            pl.BlockSpec(memory_space=pl.ANY),
        ],
        out_shape=shaped(STEPS + 1, TILE, LANES),
        scratch_shapes=[
            pltpu.VMEM((2, LANES, SIDE * COLS), BF16),
            pltpu.VMEM((SIDE * COLS, LANES), F32),
            pltpu.SemaphoreType.DMA((2,)),
        ],
        compiler_params=pltpu.CompilerParams(vmem_limit_bytes=8 * MIB),
    )(places, ids, shared_targets, private_targets)


def between_kernel(parts_ref, w_ref, m_ref, v_ref, out_ref):
    for part, ref in enumerate((w_ref, m_ref, v_ref)):
        turned = ref[...].astype(F32).T.reshape(SIDE, COLS, LANES)
        out_ref[:, part * COLS : (part + 1) * COLS, :] = turned
    for j in range(SIDE):
        lines = slice(j * TILE, (j + 1) * TILE)
        output = parts_ref[0, lines, :]
        for source in range(1, SIDE):
            output = output + parts_ref[source, lines, :]
        out_ref[j, STATE:, :] = output


def first_kernel(
    gathered_ref, error_ref, start_ref, table_ref, states_ref, output_ref, slices, arrived
):
    copies = [
        pltpu.make_async_copy(gathered_ref.at[j], slices.at[j], arrived.at[j]) for j in range(SIDE)
    ]
    for copy in copies:
        copy.start()
    both = whole_error(error_ref)
    total = None
    for k in range(SIDE // 2):
        copies[2 * k].wait()
        copies[2 * k + 1].wait()
        pair = jnp.concatenate([slices[2 * k], slices[2 * k + 1]], axis=1).astype(BF16)
        columns = slice(k * WIDE, (k + 1) * WIDE)
        table_ref[:, columns] = pair
        product = jnp.dot(both, table_ref[:, columns], preferred_element_type=F32)
        gradients = (product[:COLS] + product[COLS:]) * (1.0 / TOKENS)
        weights = []
        for half in range(2):
            j = 2 * k + half
            weight_start = start_ref[j, :COLS, :]
            moment_one, moment_two, update_sum = stepped(
                gradients[:, half * LANES : (half + 1) * LANES],
                weight_start,
                start_ref[j, COLS : 2 * COLS, :],
                start_ref[j, 2 * COLS : STATE, :],
                None,
            )
            states_ref[j, :COLS, :] = moment_one
            states_ref[j, COLS : 2 * COLS, :] = moment_two
            states_ref[j, 2 * COLS :, :] = update_sum
            weights.append((weight_start - learn_rate * update_sum).astype(BF16))
        part = turned_product(jnp.concatenate(weights, axis=1), table_ref[:, columns])
        total = part if total is None else total + part
    store_output(output_ref, total)


def first_step(gathered, error, start):
    vmem = pl.BlockSpec(memory_space=pltpu.VMEM)
    return pl.pallas_call(
        first_kernel,
        in_specs=[pl.BlockSpec(memory_space=pl.ANY), vmem, vmem],
        out_shape=[
            shaped(TABLE, SIDE * LANES, dtype=BF16),
            shaped(SIDE, STATE, LANES),
            shaped(SIDE, TILE, LANES),
        ],
        out_specs=[vmem, vmem, vmem],
        scratch_shapes=[
            pltpu.VMEM((SIDE, TABLE, LANES), F32),
            pltpu.SemaphoreType.DMA((SIDE,)),
        ],
        compiler_params=pltpu.CompilerParams(vmem_limit_bytes=20 * MIB),
    )(gathered, error, start)


def broadcast_error(output, constant_ref, step, out_ref):
    error = (output - constant_ref[STEPS]).astype(BF16).astype(F32)
    weighted = error * constant_ref[step]
    for j in range(SIDE):
        out_ref[j] = weighted


def first_error_kernel(parts_ref, constant_ref, out_ref):
    output = parts_ref[0, STATE:, :]
    for j in range(1, SIDE):
        output = output + parts_ref[j, STATE:, :]
    broadcast_error(output, constant_ref, 0, out_ref)


def error_kernel(step, parts_ref, constant_ref, out_ref):
    output = parts_ref[0]
    for j in range(1, SIDE):
        output = output + parts_ref[j]
    broadcast_error(output, constant_ref, step, out_ref)


def step_kernel(last, error_ref, table_ref, w_ref, states_ref, *rest):
    if last:
        (total_out,) = rest
    else:
        new_states, output_ref = rest
    both = whole_error(error_ref)
    weights = []
    for k in range(SIDE // 2):
        columns = slice(k * WIDE, (k + 1) * WIDE)
        product = jnp.dot(both, table_ref[:, columns], preferred_element_type=F32)
        gradients = (product[:COLS] + product[COLS:]) * (1.0 / TOKENS)
        for half in range(2):
            j = 2 * k + half
            weight_start = w_ref[j, :COLS, :]
            moment_one, moment_two, update_sum = stepped(
                gradients[:, half * LANES : (half + 1) * LANES],
                weight_start,
                states_ref[j, :COLS, :],
                states_ref[j, COLS : 2 * COLS, :],
                states_ref[j, 2 * COLS :, :],
            )
            if last:
                total_out[j] = update_sum
            else:
                new_states[j, :COLS, :] = moment_one
                new_states[j, COLS : 2 * COLS, :] = moment_two
                new_states[j, 2 * COLS :, :] = update_sum
                weights.append((weight_start - learn_rate * update_sum).astype(BF16))
    if last:
        return
    weights = jnp.concatenate(weights, axis=1)
    output = [
        turned_product(weights, table_ref[row : row + WIDE, :]) for row in range(0, TABLE, WIDE)
    ]
    store_output(output_ref, jnp.concatenate(output, axis=1))


def turn_kernel(parts_ref, out_ref):
    turned = parts_ref[...].reshape(SIDE * COLS, LANES).T
    out_ref[...] = turned.reshape(REPLICAS, LANES // REPLICAS, SIDE * COLS)


def gram_kernel(updates_ref, out_ref):
    updates = [updates_ref[r] for r in range(REPLICAS)]
    lines = []
    for i, j in PAIRS:
        product = updates[i] * updates[j]
        lines.append(jnp.sum(product, axis=0, keepdims=True))
    while len(lines) % 8:
        lines.append(jnp.zeros_like(lines[0]))
    sums = jnp.sum(jnp.concatenate(lines, axis=0), axis=1, keepdims=True)
    spread = jnp.broadcast_to(sums, (len(lines), LANES))
    line = lax.broadcasted_iota(jnp.int32, spread.shape, 0)
    lane = lax.broadcasted_iota(jnp.int32, spread.shape, 1)
    packed = jnp.sum(jnp.where(line == lane, spread, 0.0), axis=0, keepdims=True)
    for j in range(REPLICAS):
        out_ref[j] = packed


def gram_sum_kernel(parts_ref, out_ref):
    packed = jnp.sum(parts_ref[...], axis=0)
    for j in range(SIDE * SIDE):
        out_ref[j] = packed


def merge_kernel(parts_ref, updates_ref, out_ref):
    packed = jnp.sum(parts_ref[...], axis=0)
    lane = lax.broadcasted_iota(jnp.int32, packed.shape, 1)
    gram = {}
    for place, (i, j) in enumerate(PAIRS):
        value = jnp.sum(jnp.where(lane == place, packed, 0.0), axis=1, keepdims=True)
        gram[i, j] = value
        gram[j, i] = value
    members = [[r] for r in range(REPLICAS)]
    while len(members) > 1:
        merged = []
        for lower, upper in zip(members[0::2], members[1::2]):
            cross_dot = sum(gram[i, j] for i in lower for j in upper)
            lower_norm = sum(gram[i, j] for i in lower for j in lower)
            upper_norm = sum(gram[i, j] for i in upper for j in upper)
            lower_coef = 1.0 - cross_dot / (2.0 * (lower_norm + norm_eps))
            upper_coef = 1.0 - cross_dot / (2.0 * (upper_norm + norm_eps))
            scale = {**{i: lower_coef for i in lower}, **{i: upper_coef for i in upper}}
            merged.append((lower + upper, scale))
        factor = {i: scale[i] for _, scale in merged for i in scale}
        gram = {(i, j): factor[i] * factor[j] * value for (i, j), value in gram.items()}
        total = factor if len(merged) * 2 == REPLICAS else {i: total[i] * factor[i] for i in total}
        members = [group for group, _ in merged]
    result = total[0] * updates_ref[0]
    for r in range(1, REPLICAS):
        result = result + total[r] * updates_ref[r]
    out_ref[...] = result


def on_device(
    weight,
    first_moment,
    second_moment,
    token_ids,
    shared_inputs,
    private_inputs,
    shared_targets,
    private_targets,
):
    core = lax.axis_index("core")
    z = lax.axis_index("z")
    y = lax.axis_index("y")
    sum_place = jnp.where(core == 0, z, y)
    gather_place = jnp.where(core == 0, y, z)

    places = jnp.stack([sum_place, gather_place]).astype(jnp.int32)

    own = kernel_call(widen_kernel, shaped(TABLE, LANES), shared_inputs, private_inputs[0])
    gathered = lax.all_gather(
        own, CZY, axis=0, tiled=True, axis_index_groups=GATHER_GROUPS
    ).reshape(SIDE, TABLE, LANES)

    parts = kernel_call(own_kernel, shaped(SIDE, SIDE * TILE, LANES), own, weight)
    parts = exchange(parts, CZY, SUM_GROUPS)
    constants = own_constants(places, token_ids[0], shared_targets, private_targets[0])
    start = kernel_call(
        between_kernel,
        shaped(SIDE, STATE + TILE, LANES),
        parts,
        weight,
        first_moment[0],
        second_moment[0],
    )
    start = exchange(start, CZY, GATHER_GROUPS)
    error = kernel_call(first_error_kernel, shaped(SIDE, TILE, LANES), start, constants)
    error = exchange(error, CZY, SUM_GROUPS)
    table, states, parts = first_step(gathered, error, start)

    for step in range(1, STEPS):
        parts = exchange(parts, CZY, SUM_GROUPS)
        error = kernel_call(
            functools.partial(error_kernel, step), shaped(SIDE, TILE, LANES), parts, constants
        )
        error = exchange(error, CZY, SUM_GROUPS)
        last = step == STEPS - 1
        body = functools.partial(step_kernel, last)
        operands = (error, table, start, states)
        if last:
            updates = kernel_call(body, shaped(SIDE, COLS, LANES), *operands)
        else:
            states, parts = kernel_call(
                body, [shaped(SIDE, STATE, LANES), shaped(SIDE, TILE, LANES)], *operands
            )

    updates = exchange(updates, CZY, GATHER_GROUPS)
    turned = kernel_call(turn_kernel, shaped(REPLICAS, LANES // REPLICAS, SIDE * COLS), updates)
    updates = exchange(turned, ("x", "core"))
    gram = kernel_call(gram_kernel, shaped(REPLICAS, 1, LANES), updates)
    gram = exchange(gram, ("x", "core"))
    gram = kernel_call(gram_sum_kernel, shaped(SIDE * SIDE, 1, LANES), gram)
    gram = exchange(gram, ("z", "y"))
    return kernel_call(
        merge_kernel, shaped(LANES // REPLICAS, SIDE * COLS), gram, updates
    )


def solution(mesh):
    torus = Mesh(mesh.devices.reshape(4, 2, SIDE, SIDE), ("x", "core", "z", "y"))
    row = ("z", "y")
    rep = ("x", "core")
    placed = (
        P(row, None),
        P(rep, row, None),
        P(rep, row, None),
        P(rep, None, None),
        P(None, row),
        P(rep, None, row),
        P(),
        P(rep, None, None),
    )
    return jax.shard_map(
        on_device,
        mesh=torus,
        in_specs=placed,
        out_specs=P((*row, *rep), None),
        check_vma=False,
    )
```

time: 248 us -> 253 us (1.020)
  blocking collectives: 144 us -> 189 us
  waiting for transfers between devices: 49 us -> 19 us
  starting transfers between devices: 17.4 us -> 12.2 us
  other arithmetic: 3.85 us -> 0.07 us
    all_to_all x11 -> x12, blocking collectives: 144 us -> 189 us  [exchange(): lax.all_to_all(blocks, axes, split_axis=0, concat_axis=0, tiled=True, axi...]
    all_gather x1, waiting for transfers between devices: 28.5 us -> 0.01 us  [on_device(): lax.all_gather(own, CZY, axis=0, tiled=True, axis_index_groups=GATHER_GRO...]
    all_to_all x2 -> x1, starting transfers between devices: 17.4 us -> 12.2 us  [exchange(): lax.all_to_all(blocks, axes, split_axis=0, concat_axis=0, tiled=True, axi...]
    convert_element_type x2 -> x0, other arithmetic: 2.97 us -> none  [the longest x1 2.04 us: on_device(): jnp.concatenate([shared_inputs, private_inputs[0]], axis=0).astype(F32)]
    all_to_all x2 -> x1, waiting for transfers between devices: 20.5 us -> 19 us  [exchange(): lax.all_to_all(blocks, axes, split_axis=0, concat_axis=0, tiled=True, axi...]
    unnamed x17 -> x20, local copies, waits for them, and re-layouts: 6.29 us -> 5.56 us
    pallas_call x14 -> x16, Pallas kernels: 13.2 us -> 13.7 us  [the longest x14 9.08 us: kernel_call(): pl.pallas_call(body, in_specs=in_specs, out_shape=out_shapes, compiler_pa...]
  transfers between devices with their start and end apart: 3 -> 2, of which waited for: 3 -> 1; matrix products, arithmetic and copies ran while one was open for 1% -> 0% of each run, Pallas kernels for 0% -> 2%
where the time goes in v4:
time: 253 us
  blocking collectives  189 us (75%)
  waiting for transfers between devices  19 us (8%)
  Pallas kernels  13.7 us (5%)
  between operations  13.5 us (5%)
  starting transfers between devices  12.2 us (5%)
  local copies, waits for them, and re-layouts  5.56 us (2%)
    all_to_all x12, blocking collectives, exchange(): lax.all_to_all(blocks, axes, split_axis=0, concat_axis=0, tiled=True, axi...  189 us
    all_to_all x1, waiting for transfers between devices, exchange(): lax.all_to_all(blocks, axes, split_axis=0, concat_axis=0, tiled=True, axi...  19 us
    all_to_all x1, starting transfers between devices, exchange(): lax.all_to_all(blocks, axes, split_axis=0, concat_axis=0, tiled=True, axi...  12.2 us
    pallas_call x14, Pallas kernels, kernel_call(): pl.pallas_call(body, in_specs=in_specs, out_shape=out_shapes, compiler_pa...  9.08 us
    unnamed x20, local copies, waits for them, and re-layouts  5.56 us
  transfers between devices with their start and end apart: 2, of which 1 were waited for; matrix products, arithmetic and copies ran while one was open for 0% of the time, Pallas kernels for 2%

profile of v4, /device:TPU:1, one launch (start us, length us, event | category | flops | bytes accessed | tf_op | source)
XLA Modules:
  0.0 252.6 jit_solution(13418065247190504306)
XLA Ops:
  6.5 0.9 copy-done.5
  7.5 0.9 copy-done.6
  8.4 0.9 shard_map.82.slice_ref
  10.2 1.7 shard_map.83
  11.9 47.3 %all_to_all.65.parts_ref = f32[8,576,128]{2,1,0:T(8,128)S(1)} all-to-all(f32[8,576,128]{2,1,0:T(8,128)S(1)} %shard_map.83), channel_id=1, replica_groups={{0,8,16,24,32,40,48,56},{1,9,17,25,33,41,49,57},{2,10,18,26,34,42,50,58..., dimensions={0} | all-to-all | bytes 4718592 | tf_op jit(solution)/shard_map/all_to_all | solution.py:51
  59.3 1.1 shard_map.84
  60.4 12.2 %all-to-all-start.1 = ((f32[8,216,128]{2,1,0:T(8,128)}), f32[8,216,128]{2,1,0:T(8,128)S(1)}, u32[]{:S(2)}, u32[]{:S(2)}) async-start(f32[8,216,128]{2,1,0:T(8,128)} %shard_map.84), calls=%async_computation.1 | async-start | bytes 1769472 | tf_op jit(solution)/shard_map/all_to_all | solution.py:51
  72.6 1.6 shard_map.85.constant_ref
  74.3 19.0 %all-to-all-done.1.parts_ref.start_ref.w_ref = f32[8,216,128]{2,1,0:T(8,128)S(1)} async-done(((f32[8,216,128]{2,1,0:T(8,128)}), f32[8,216,128]{2,1,0:T(8,128)S(1)}, u32[]{:S(2)}, u32[]{:S(2)}) %all-to-all-start.1) | async-done | bytes 884768 | tf_op jit(solution)/shard_map/all_to_all | solution.py:51
  93.3 12.1 %all_to_all.66.error_ref = f32[8,72,128]{2,1,0:T(8,128)S(1)} all-to-all(f32[8,72,128]{2,1,0:T(8,128)S(1)} %shard_map.86), channel_id=1, replica_groups={{0,8,16,24,32,40,48,56},{1,9,17,25,33,41,49,57},{2,10,18,26,34,42,50,58..., dimensions={0} | all-to-all | bytes 589824 | tf_op jit(solution)/shard_map/all_to_all | solution.py:51
  105.4 2.8 %copy-done = f32[12288,128]{1,0:T(8,128)S(1)} copy-done((f32[12288,128]{1,0:T(8,128)S(1)}, f32[12288,128]{1,0:T(8,128)}, u32[]{:S(2)}) %copy-start) | copy-done | bytes 6291480
  108.2 3.0 %shard_map.87 = (bf16[1536,1024]{1,0:T(8,128)(2,1)S(1)}, f32[8,144,128]{2,1,0:T(8,128)S(1)}, f32[8,72,128]{2,1,0:T(8,128)S(1)}) custom-call(f32[8,1536,128]{2,1,0:T(8,128)S(1)} %bitcast.8, f32[8,72,128]{2,1,0:T(8,128)S(1)} %all_to_all.66.error_ref, f32[8,216,128]{2,1,0:T(8,128)S(1)} %all-to-all-done.1.parts_ref.start_ref.w_ref), custom_call_target="tpu_custom_call" | custom-call | tf_op jit(solution)/shard_map/pallas_call | solution.py:234
  111.2 12.1 %all_to_all.67.parts_ref = f32[8,72,128]{2,1,0:T(8,128)S(1)} all-to-all(f32[8,72,128]{2,1,0:T(8,128)S(1)} %get-tuple-element.12), channel_id=1, replica_groups={{0,8,16,24,32,40,48,56},{1,9,17,25,33,41,49,57},{2,10,18,26,34,42,50,58..., dimensions={0} | all-to-all | bytes 589824 | tf_op jit(solution)/shard_map/all_to_all | solution.py:51
  123.3 12.1 %all_to_all.68.error_ref = f32[8,72,128]{2,1,0:T(8,128)S(1)} all-to-all(f32[8,72,128]{2,1,0:T(8,128)S(1)} %shard_map.88), channel_id=1, replica_groups={{0,8,16,24,32,40,48,56},{1,9,17,25,33,41,49,57},{2,10,18,26,34,42,50,58..., dimensions={0} | all-to-all | bytes 589824 | tf_op jit(solution)/shard_map/all_to_all | solution.py:51
  135.4 1.6 shard_map.89
  137.0 12.1 %all_to_all.69.parts_ref = f32[8,72,128]{2,1,0:T(8,128)S(1)} all-to-all(f32[8,72,128]{2,1,0:T(8,128)S(1)} %get-tuple-element.15), channel_id=1, replica_groups={{0,8,16,24,32,40,48,56},{1,9,17,25,33,41,49,57},{2,10,18,26,34,42,50,58..., dimensions={0} | all-to-all | bytes 589824 | tf_op jit(solution)/shard_map/all_to_all | solution.py:51
  149.1 12.1 %all_to_all.70.error_ref = f32[8,72,128]{2,1,0:T(8,128)S(1)} all-to-all(f32[8,72,128]{2,1,0:T(8,128)S(1)} %shard_map.90), channel_id=1, replica_groups={{0,8,16,24,32,40,48,56},{1,9,17,25,33,41,49,57},{2,10,18,26,34,42,50,58..., dimensions={0} | all-to-all | bytes 589824 | tf_op jit(solution)/shard_map/all_to_all | solution.py:51
  161.1 1.6 shard_map.91
  162.8 12.1 %all_to_all.71.parts_ref = f32[8,72,128]{2,1,0:T(8,128)S(1)} all-to-all(f32[8,72,128]{2,1,0:T(8,128)S(1)} %get-tuple-element.17), channel_id=1, replica_groups={{0,8,16,24,32,40,48,56},{1,9,17,25,33,41,49,57},{2,10,18,26,34,42,50,58..., dimensions={0} | all-to-all | bytes 589824 | tf_op jit(solution)/shard_map/all_to_all | solution.py:51
  174.9 12.1 %all_to_all.72.error_ref = f32[8,72,128]{2,1,0:T(8,128)S(1)} all-to-all(f32[8,72,128]{2,1,0:T(8,128)S(1)} %shard_map.92), channel_id=1, replica_groups={{0,8,16,24,32,40,48,56},{1,9,17,25,33,41,49,57},{2,10,18,26,34,42,50,58..., dimensions={0} | all-to-all | bytes 589824 | tf_op jit(solution)/shard_map/all_to_all | solution.py:51
  187.7 12.2 %all_to_all.73.parts_ref = f32[8,48,128]{2,1,0:T(8,128)S(1)} all-to-all(f32[8,48,128]{2,1,0:T(8,128)S(1)} %shard_map.93), channel_id=1, replica_groups={{0,1,2,3,4,5,6,7},{8,9,10,11,12,13,14,15},{16,17,18,19,20,21,22,23},{24..., dimensions={0} | all-to-all | bytes 393216 | tf_op jit(solution)/shard_map/all_to_all | solution.py:51
  200.0 22.2 %all_to_all.74.updates_ref = f32[8,16,384]{2,1,0:T(8,128)S(1)} all-to-all(f32[8,16,384]{2,1,0:T(8,128)S(1)} %shard_map.94), channel_id=1, replica_groups=mesh['x'=4,'core'=2,'z'=8,'y'=8] {'x','core'}, dimensions={0} | all-to-all | bytes 393216 | tf_op jit(solution)/shard_map/all_to_all | solution.py:51
  222.4 7.9 %all_to_all.75.parts_ref = f32[8,1,128]{2,1,0:T(1,128)S(1)} all-to-all(f32[8,1,128]{2,1,0:T(1,128)S(1)} %shard_map.95), channel_id=1, replica_groups=mesh['x'=4,'core'=2,'z'=8,'y'=8] {'x','core'}, dimensions={0} | all-to-all | bytes 8192 | tf_op jit(solution)/shard_map/all_to_all | solution.py:51
  230.3 14.6 %all_to_all.76.parts_ref = f32[64,1,128]{2,1,0:T(1,128)S(1)} all-to-all(f32[64,1,128]{2,1,0:T(1,128)S(1)} %shard_map.96), channel_id=1, replica_groups=mesh['x'=4,'core'=2,'z'=8,'y'=8] {'z','y'}, dimensions={0} | all-to-all | bytes 65536 | tf_op jit(solution)/shard_map/all_to_all | solution.py:51
  (30 shorter events, 3.1 us)
Async XLA Ops:
  6.5 98.9 %all-gather.2.cloned.1.call-start = ((), (), s32[]{:S(2)}) async-start(), calls=%async_computation.13 | async-start | bytes 7077888 | tf_op jit(solution)/shard_map/all_gather | solution.py:385
  6.5 0.9 copy-start.5
  7.5 0.9 copy-start.6
  9.3 0.9 copy-start.2
  11.9 47.3 %copy-start.3 = (bf16[128,384]{1,0:T(8,128)(2,1)S(1)}, bf16[128,384]{1,0:T(8,128)(2,1)}, u32[]{:S(2)}) copy-start(bf16[128,384]{1,0:T(8,128)(2,1)} %w_ref.1) | copy-start | bytes 294916
  11.9 47.3 %copy-start.7 = (bf16[1,128,384]{2,1,0:T(8,128)(2,1)S(1)}, bf16[1,128,384]{2,1,0:T(8,128)(2,1)}, u32[]{:S(2)}) copy-start(bf16[1,128,384]{2,1,0:T(8,128)(2,1)} %param.9) | copy-start | bytes 294916
  11.9 47.3 %copy-start.8 = (bf16[1,128,384]{2,1,0:T(8,128)(2,1)S(1)}, bf16[1,128,384]{2,1,0:T(8,128)(2,1)}, u32[]{:S(2)}) copy-start(bf16[1,128,384]{2,1,0:T(8,128)(2,1)} %param.10) | copy-start | bytes 294916
  59.2 13.4 %copy-start.1 = (bf16[1024,384]{1,0:T(8,128)(2,1)S(1)}, bf16[1024,384]{1,0:T(8,128)(2,1)}, u32[]{:S(2)}) copy-start(bf16[1024,384]{1,0:T(8,128)(2,1)} %shared_ref.3) | copy-start | bytes 2359300
  59.2 13.4 %copy-start.4 = (bf16[1,512,384]{2,1,0:T(8,128)(2,1)S(1)}, bf16[1,512,384]{2,1,0:T(8,128)(2,1)}, u32[]{:S(2)}) copy-start(bf16[1,512,384]{2,1,0:T(8,128)(2,1)} %param.15) | copy-start | bytes 1179652
  59.2 13.4 %copy-start.9 = (s32[1,4,1024]{2,1,0:T(4,128)S(1)}, s32[1,4,1024]{2,1,0:T(4,128)}, u32[]{:S(2)}) copy-start(s32[1,4,1024]{2,1,0:T(4,128)} %param.11) | copy-start | bytes 49156
  60.4 32.9 %all-to-all-start.1 = ((f32[8,216,128]{2,1,0:T(8,128)}), f32[8,216,128]{2,1,0:T(8,128)S(1)}, u32[]{:S(2)}, u32[]{:S(2)}) async-start(f32[8,216,128]{2,1,0:T(8,128)} %shard_map.84), calls=%async_computation.1 | async-start | bytes 1769472 | tf_op jit(solution)/shard_map/all_to_all | solution.py:51
  105.4 2.8 %copy-start = (f32[12288,128]{1,0:T(8,128)S(1)}, f32[12288,128]{1,0:T(8,128)}, u32[]{:S(2)}) copy-start(f32[12288,128]{1,0:T(8,128)} %all-gather.2.cloned.1.call-done) | copy-start | bytes 18874372
Sparse Core Ops, SparseCore 0:
  9.5 82.8 all-gather.1

commit v5 on v4

--- a/solution.py
+++ b/solution.py
@@ -23,6 +23,9 @@
 LANES = 128
 COLS = 48
 HALF = COLS // 2
+OWN = COLS // SIDE
+FIRST = HALF + 2 * SIDE
+CHIPS = 4
 STATE = 3 * COLS
 TILE = COLS + HALF
 POOL = 1024
@@ -82,6 +85,12 @@
     return lax.dot_general(left, right, (((1,), (1,)), ((), ())), preferred_element_type=F32)
 
 
+def in_two_parts(error):
+    high = error.astype(BF16)
+    low = (error - high.astype(F32)).astype(BF16)
+    return jnp.concatenate([high, low], axis=0)
+
+
 def whole_error(error_ref):
     error = jnp.concatenate(
         [error_ref[j, :COLS, :] for j in range(SIDE)]
@@ -91,9 +100,7 @@
         ],
         axis=1,
     )
-    high = error.astype(BF16)
-    low = (error - high.astype(F32)).astype(BF16)
-    return jnp.concatenate([high, low], axis=0)
+    return in_two_parts(error)
 
 
 def stepped(gradient, weight_start, moment_one, moment_two, update_sum):
@@ -113,51 +120,81 @@
     out_ref[POOL:, :] = private_ref[...].astype(F32)
 
 
-def own_kernel(slice_ref, weight_ref, out_ref):
+def own_kernel(place_ref, slice_ref, weight_ref, constant_ref, out_ref):
     weights = weight_ref[...].astype(F32).T.astype(BF16)
-    own = slice_ref[...].astype(BF16)
+    line = lax.broadcasted_iota(jnp.int32, (SIDE * SIDE * SIDE, SIDE * COLS), 0)
+    lane = lax.broadcasted_iota(jnp.int32, (SIDE * SIDE * SIDE, SIDE * COLS), 1)
+    spot = line & (SIDE - 1)
+    column = ((line >> 3) & (SIDE - 1)) * COLS + (line >> 6) * OWN + spot
+    order = jnp.where((lane == column) & (spot < OWN), 1.0, 0.0).astype(BF16)
+    ordered = jnp.dot(order, weights, preferred_element_type=F32).astype(BF16)
+    quarter = pl.ds(pl.multiple_of(place_ref[2] * WIDE, WIDE), WIDE)
+    shared = turned_product(ordered, slice_ref[quarter, :].astype(BF16))
     for i in range(SIDE):
-        shared = turned_product(weights, own[i * LANES : (i + 1) * LANES, :])
         for j in range(SIDE):
-            out_ref[i, j * TILE : j * TILE + COLS, :] = shared[j * COLS : (j + 1) * COLS, :]
+            line = (i * SIDE + j) * SIDE
+            place = j * FIRST + HALF
+            out_ref[i, place : place + SIDE, :] = shared[line : line + SIDE, :LANES]
+            out_ref[i, place + SIDE : place + 2 * SIDE, :] = shared[line : line + SIDE, LANES:]
     for k in range(SIDE // 2):
         row = POOL + k * LANES
-        private = turned_product(weights, own[row : row + LANES, :])
+        private = turned_product(weights, slice_ref[row : row + LANES, :].astype(BF16))
         for j in range(SIDE):
             for half in range(2):
                 line = j * COLS + half * HALF
-                place = j * TILE + COLS
+                place = j * FIRST
                 out_ref[2 * k + half, place : place + HALF, :] = private[line : line + HALF, :]
 
 
-def constant_kernel(place_ref, ids_ref, shared_ref, private_ref, out_ref, rows, turned, arrived):
-    i, j = place_ref[0], place_ref[1]
+def constant_kernel(
+    place_ref, ids_ref, shared_ref, private_ref, out_ref, first_ref, row_ref, rows, turned, arrived
+):
+    i, j, x = place_ref[0], place_ref[1], place_ref[2]
     shared_rows = pl.ds(pl.multiple_of(i * LANES, LANES), LANES)
     private_rows = pl.ds(pl.multiple_of(lax.div(i, 2) * LANES, LANES), LANES)
+    quarter = pl.ds(pl.multiple_of(x * WIDE, WIDE), WIDE)
     copies = [
-        pltpu.make_async_copy(shared_ref.at[shared_rows], rows.at[0], arrived.at[0]),
-        pltpu.make_async_copy(private_ref.at[private_rows], rows.at[1], arrived.at[1]),
+        pltpu.make_async_copy(shared_ref.at[shared_rows], rows.at[pl.ds(0, LANES)], arrived.at[0]),
+        pltpu.make_async_copy(
+            private_ref.at[private_rows], rows.at[pl.ds(LANES, LANES)], arrived.at[1]
+        ),
+        pltpu.make_async_copy(shared_ref.at[quarter], rows.at[pl.ds(WIDE, WIDE)], arrived.at[2]),
     ]
     for copy in copies:
         copy.start()
     row = lax.broadcasted_iota(jnp.int32, (LANES, TOKENS), 0)
     ones = jnp.ones((16, TOKENS), BF16)
+
+    def count_of(step, start):
+        hits = jnp.where(ids_ref[step : step + 1, :] == row + start, 1.0, 0.0).astype(BF16)
+        return turned_product(ones, hits)
+
+    for start in range(0, TABLE, LANES):
+        row_ref[:, start : start + LANES] = count_of(0, start)[:SIDE]
     for start, lines in (
         (i * LANES, slice(0, COLS)),
         (POOL + lax.div(i, 2) * LANES, slice(COLS, TILE)),
     ):
-        for step in range(STEPS):
-            hits = jnp.where(ids_ref[step : step + 1, :] == row + start, 1.0, 0.0).astype(BF16)
-            count = turned_product(ones, hits)[:1]
-            out_ref[step, lines, :] = jnp.broadcast_to(count, (lines.stop - lines.start, LANES))
+        for step in range(1, STEPS):
+            count = count_of(step, start)[:1]
+            out_ref[step - 1, lines, :] = jnp.broadcast_to(
+                count, (lines.stop - lines.start, LANES)
+            )
     for copy in copies:
         copy.wait()
-    turned[...] = rows[0].astype(F32).T
-    columns = pl.ds(pl.multiple_of(j * COLS, 8), COLS)
-    out_ref[STEPS, :COLS, :] = turned[columns, :]
-    turned[...] = rows[1].astype(F32).T
+    turned[...] = rows[:LANES, :].astype(F32).T
+    out_ref[STEPS - 1, :COLS, :] = turned[pl.ds(pl.multiple_of(j * COLS, 8), COLS), :]
+    turned[...] = rows[LANES:WIDE, :].astype(F32).T
     columns = pl.ds(pl.multiple_of(j * COLS + lax.rem(i, 2) * HALF, 8), HALF)
-    out_ref[STEPS, COLS:, :] = turned[columns, :]
+    private = turned[columns, :]
+    out_ref[STEPS - 1, COLS:, :] = private
+    first_ref[:HALF, :] = private
+    spot = lax.broadcasted_iota(jnp.int32, (16, SIDE * COLS), 0)
+    lane = lax.broadcasted_iota(jnp.int32, (16, SIDE * COLS), 1)
+    mine = (lane == j * COLS + i * OWN + spot) & (spot < OWN)
+    shared = turned_product(jnp.where(mine, 1.0, 0.0).astype(BF16), rows[WIDE:, :])
+    first_ref[HALF : HALF + SIDE, :] = shared[:SIDE, :LANES]
+    first_ref[HALF + SIDE :, :] = shared[:SIDE, LANES:]
 
 
 def own_constants(places, ids, shared_targets, private_targets):
@@ -169,11 +206,11 @@
             pl.BlockSpec(memory_space=pl.ANY),
             pl.BlockSpec(memory_space=pl.ANY),
         ],
-        out_shape=shaped(STEPS + 1, TILE, LANES),
+        out_shape=[shaped(STEPS, TILE, LANES), shaped(FIRST, LANES), shaped(SIDE, TABLE)],
         scratch_shapes=[
-            pltpu.VMEM((2, LANES, SIDE * COLS), BF16),
+            pltpu.VMEM((2 * WIDE, SIDE * COLS), BF16),
             pltpu.VMEM((SIDE * COLS, LANES), F32),
-            pltpu.SemaphoreType.DMA((2,)),
+            pltpu.SemaphoreType.DMA((3,)),
         ],
         compiler_params=pltpu.CompilerParams(vmem_limit_bytes=8 * MIB),
     )(places, ids, shared_targets, private_targets)
@@ -184,22 +221,51 @@
         turned = ref[...].astype(F32).T.reshape(SIDE, COLS, LANES)
         out_ref[:, part * COLS : (part + 1) * COLS, :] = turned
     for j in range(SIDE):
-        lines = slice(j * TILE, (j + 1) * TILE)
+        lines = slice(j * FIRST, (j + 1) * FIRST)
         output = parts_ref[0, lines, :]
         for source in range(1, SIDE):
             output = output + parts_ref[source, lines, :]
         out_ref[j, STATE:, :] = output
 
 
+def first_whole_error(error_ref, row_ref):
+    private = jnp.concatenate(
+        [
+            jnp.concatenate([error_ref[2 * k, :HALF, :], error_ref[2 * k + 1, :HALF, :]], axis=0)
+            for k in range(SIDE // 2)
+        ],
+        axis=1,
+    )
+    padded = jnp.concatenate(
+        [
+            jnp.concatenate(
+                [error_ref[i, HALF + b * SIDE : HALF + (b + 1) * SIDE, :] for i in range(SIDE)],
+                axis=0,
+            )
+            for b in range(SIDE)
+        ],
+        axis=1,
+    ).astype(BF16)
+    line = lax.broadcasted_iota(jnp.int32, (COLS, SIDE * SIDE), 0)
+    lane = lax.broadcasted_iota(jnp.int32, (COLS, SIDE * SIDE), 1)
+    spot = lane & (SIDE - 1)
+    kept = (line == (lane >> 3) * OWN + spot) & (spot < OWN)
+    shared = jnp.dot(
+        jnp.where(kept, 1.0, 0.0).astype(BF16), padded, preferred_element_type=F32
+    )
+    error = jnp.concatenate([shared, private], axis=1) * row_ref[:1, :]
+    return in_two_parts(error)
+
+
 def first_kernel(
-    gathered_ref, error_ref, start_ref, table_ref, states_ref, output_ref, slices, arrived
+    gathered_ref, error_ref, row_ref, start_ref, table_ref, states_ref, output_ref, slices, arrived
 ):
     copies = [
         pltpu.make_async_copy(gathered_ref.at[j], slices.at[j], arrived.at[j]) for j in range(SIDE)
     ]
     for copy in copies:
         copy.start()
-    both = whole_error(error_ref)
+    both = first_whole_error(error_ref, row_ref)
     total = None
     for k in range(SIDE // 2):
         copies[2 * k].wait()
@@ -229,11 +295,11 @@
     store_output(output_ref, total)
 
 
-def first_step(gathered, error, start):
+def first_step(gathered, error, count_row, start):
     vmem = pl.BlockSpec(memory_space=pltpu.VMEM)
     return pl.pallas_call(
         first_kernel,
-        in_specs=[pl.BlockSpec(memory_space=pl.ANY), vmem, vmem],
+        in_specs=[pl.BlockSpec(memory_space=pl.ANY), vmem, vmem, vmem],
         out_shape=[
             shaped(TABLE, SIDE * LANES, dtype=BF16),
             shaped(SIDE, STATE, LANES),
@@ -244,29 +310,36 @@
             pltpu.VMEM((SIDE, TABLE, LANES), F32),
             pltpu.SemaphoreType.DMA((SIDE,)),
         ],
-        compiler_params=pltpu.CompilerParams(vmem_limit_bytes=20 * MIB),
-    )(gathered, error, start)
-
-
-def broadcast_error(output, constant_ref, step, out_ref):
-    error = (output - constant_ref[STEPS]).astype(BF16).astype(F32)
-    weighted = error * constant_ref[step]
-    for j in range(SIDE):
-        out_ref[j] = weighted
-
-
-def first_error_kernel(parts_ref, constant_ref, out_ref):
+        compiler_params=pltpu.CompilerParams(vmem_limit_bytes=44 * MIB),
+    )(gathered, error, count_row, start)
+
+
+def first_error_kernel(parts_ref, target_ref, private_ref, shared_ref):
     output = parts_ref[0, STATE:, :]
     for j in range(1, SIDE):
         output = output + parts_ref[j, STATE:, :]
-    broadcast_error(output, constant_ref, 0, out_ref)
+    error = (output - target_ref[...]).astype(BF16).astype(F32)
+    private_ref[...] = error[:HALF]
+    for x in range(CHIPS):
+        shared_ref[x] = error[HALF:]
+
+
+def collect_kernel(private_ref, shared_ref, out_ref):
+    for j in range(SIDE):
+        out_ref[j, :HALF, :] = private_ref[...]
+        for x in range(CHIPS):
+            line = HALF + 2 * SIDE * x
+            out_ref[j, line : line + 2 * SIDE, :] = shared_ref[x]
 
 
 def error_kernel(step, parts_ref, constant_ref, out_ref):
     output = parts_ref[0]
     for j in range(1, SIDE):
         output = output + parts_ref[j]
-    broadcast_error(output, constant_ref, step, out_ref)
+    error = (output - constant_ref[STEPS - 1]).astype(BF16).astype(F32)
+    weighted = error * constant_ref[step - 1]
+    for j in range(SIDE):
+        out_ref[j] = weighted
 
 
 def step_kernel(last, error_ref, table_ref, w_ref, states_ref, *rest):
@@ -379,28 +452,41 @@
     sum_place = jnp.where(core == 0, z, y)
     gather_place = jnp.where(core == 0, y, z)
 
-    places = jnp.stack([sum_place, gather_place]).astype(jnp.int32)
+    places = jnp.stack([sum_place, gather_place, lax.axis_index("x")]).astype(jnp.int32)
 
     own = kernel_call(widen_kernel, shaped(TABLE, LANES), shared_inputs, private_inputs[0])
     gathered = lax.all_gather(
         own, CZY, axis=0, tiled=True, axis_index_groups=GATHER_GROUPS
     ).reshape(SIDE, TABLE, LANES)
 
-    parts = kernel_call(own_kernel, shaped(SIDE, SIDE * TILE, LANES), own, weight)
+    constants, first_targets, count_row = own_constants(
+        places, token_ids[0], shared_targets, private_targets[0]
+    )
+    parts = kernel_call(
+        own_kernel, shaped(SIDE, SIDE * FIRST, LANES), places, own, weight, first_targets
+    )
     parts = exchange(parts, CZY, SUM_GROUPS)
-    constants = own_constants(places, token_ids[0], shared_targets, private_targets[0])
     start = kernel_call(
         between_kernel,
-        shaped(SIDE, STATE + TILE, LANES),
+        shaped(SIDE, STATE + FIRST, LANES),
         parts,
         weight,
         first_moment[0],
         second_moment[0],
     )
     start = exchange(start, CZY, GATHER_GROUPS)
-    error = kernel_call(first_error_kernel, shaped(SIDE, TILE, LANES), start, constants)
+    private, shared = kernel_call(
+        first_error_kernel,
+        [shaped(HALF, LANES), shaped(CHIPS, 2 * SIDE, LANES)],
+        start,
+        first_targets,
+    )
+    shared = exchange(shared, "x")
+    error = kernel_call(
+        collect_kernel, shaped(SIDE, HALF + SIDE * SIDE, LANES), private, shared
+    )
     error = exchange(error, CZY, SUM_GROUPS)
-    table, states, parts = first_step(gathered, error, start)
+    table, states, parts = first_step(gathered, error, count_row, start)
 
     for step in range(1, STEPS):
         parts = exchange(parts, CZY, SUM_GROUPS)

time: 253 us -> 248 us (0.980)
  blocking collectives: 189 us -> 214 us
  waiting for transfers between devices: 19 us -> 0.02 us
  starting transfers between devices: 12.2 us -> 0.01 us
    all_to_all x12 -> x14, blocking collectives: 189 us -> 214 us  [exchange(): lax.all_to_all(blocks, axes, split_axis=0, concat_axis=0, tiled=True, axi...]
    all_to_all x1 -> x0, waiting for transfers between devices: 19 us -> none  [exchange(): lax.all_to_all(blocks, axes, split_axis=0, concat_axis=0, tiled=True, axi...]
    all_to_all x1 -> x0, starting transfers between devices: 12.2 us -> none  [exchange(): lax.all_to_all(blocks, axes, split_axis=0, concat_axis=0, tiled=True, axi...]
    pallas_call x14 -> x15, Pallas kernels: 9.08 us -> 8.23 us  [kernel_call(): pl.pallas_call(body, in_specs=in_specs, out_shape=out_shapes, compiler_pa...]
    unnamed x20 -> x16, local copies, waits for them, and re-layouts: 5.56 us -> 4.74 us
  transfers between devices with their start and end apart: 2 -> 1, of which waited for: 1 -> 0; matrix products, arithmetic and copies ran while one was open for 0% -> 0% of each run, Pallas kernels for 2% -> 2%
where the time goes in v5:
time: 248 us; the launch traced here: 247 us
  blocking collectives  214 us (86%)
  Pallas kernels  14.9 us (6%)
  between operations  13.5 us (5%)
  local copies, waits for them, and re-layouts  4.74 us (2%)
    all_to_all x14, blocking collectives, exchange(): lax.all_to_all(blocks, axes, split_axis=0, concat_axis=0, tiled=True, axi...  214 us
    pallas_call x15, Pallas kernels, kernel_call(): pl.pallas_call(body, in_specs=in_specs, out_shape=out_shapes, compiler_pa...  8.23 us
  transfers between devices with their start and end apart: 1, of which 0 were waited for; matrix products, arithmetic and copies ran while one was open for 0% of the time, Pallas kernels for 2%

profile of v5, /device:TPU:1, one launch (start us, length us, event | category | flops | bytes accessed | tf_op | source)
XLA Modules:
  0.0 246.9 jit_solution(8424970179273982112)
XLA Ops:
  6.5 1.0 copy-done.3
  7.5 0.9 copy-done.4
  8.4 1.0 shard_map.82.slice_ref
  9.5 1.1 copy-done
  10.6 1.0 copy-done.2
  12.4 2.7 %shard_map.83 = (f32[4,72,128]{2,1,0:T(8,128)S(1)}, f32[40,128]{1,0:T(8,128)S(1)}, f32[8,1536]{1,0:T(8,128)S(1)}) custom-call(s32[3]{0:T(128)S(1)} %pad_add_fusion.place_ref, s32[4,1024]{1,0:T(4,128)S(1)} %bitcast.13, bf16[1024,384]{1,0:T(8,128)(2,1)S(1)} %copy-done, bf16[512,384]{1,0:T(8,128)(2,1)S(1)} %bitcast.9), custom_call_target="tpu_custom_call" | custom-call | tf_op jit(solution)/shard_map/pallas_call | solution.py:201
  15.0 1.8 shard_map.84
  16.8 32.6 %all_to_all.70.parts_ref = f32[8,320,128]{2,1,0:T(8,128)S(1)} all-to-all(f32[8,320,128]{2,1,0:T(8,128)S(1)} %shard_map.84), channel_id=1, replica_groups={{0,8,16,24,32,40,48,56},{1,9,17,25,33,41,49,57},{2,10,18,26,34,42,50,58..., dimensions={0} | all-to-all | bytes 2621440 | tf_op jit(solution)/shard_map/all_to_all | solution.py:54
  49.5 30.9 %all_to_all.71.parts_ref.start_ref.w_ref = f32[8,184,128]{2,1,0:T(8,128)S(1)} all-to-all(f32[8,184,128]{2,1,0:T(8,128)S(1)} %shard_map.85), channel_id=1, replica_groups={{0,1,2,3,4,5,6,7},{8,9,10,11,12,13,14,15},{16,17,18,19,20,21,22,23},{24..., dimensions={0} | all-to-all | bytes 1507328 | tf_op jit(solution)/shard_map/all_to_all | solution.py:54
  80.5 8.1 %all_to_all.72.shared_ref = f32[4,16,128]{2,1,0:T(8,128)S(1)} all-to-all(f32[4,16,128]{2,1,0:T(8,128)S(1)} %get-tuple-element.19), channel_id=1, replica_groups=mesh['x'=4,'core'=2,'z'=8,'y'=8] {'x'}, dimensions={0} | all-to-all | bytes 65536 | tf_op jit(solution)/shard_map/all_to_all | solution.py:54
  88.6 12.8 %all_to_all.73.error_ref = f32[8,88,128]{2,1,0:T(8,128)S(1)} all-to-all(f32[8,88,128]{2,1,0:T(8,128)S(1)} %shard_map.87), channel_id=1, replica_groups={{0,8,16,24,32,40,48,56},{1,9,17,25,33,41,49,57},{2,10,18,26,34,42,50,58..., dimensions={0} | all-to-all | bytes 720896 | tf_op jit(solution)/shard_map/all_to_all | solution.py:54
  101.3 4.0 %shard_map.88 = (bf16[1536,1024]{1,0:T(8,128)(2,1)S(1)}, f32[8,144,128]{2,1,0:T(8,128)S(1)}, f32[8,72,128]{2,1,0:T(8,128)S(1)}) custom-call(f32[8,1536,128]{2,1,0:T(8,128)} %bitcast.14, f32[8,88,128]{2,1,0:T(8,128)S(1)} %all_to_all.73.error_ref, f32[8,1536]{1,0:T(8,128)S(1)} %get-tuple-element.20.row_ref, f32[8,184,128]{2,1,0:T(8,128)S(1)} %all_to_all.71.parts_ref.start_ref.w_ref), custom_call_target="tpu_custom_call" | custom-call | tf_op jit(solution)/shard_map/pallas_call | solution.py:300
  105.4 12.1 %all_to_all.74.parts_ref = f32[8,72,128]{2,1,0:T(8,128)S(1)} all-to-all(f32[8,72,128]{2,1,0:T(8,128)S(1)} %get-tuple-element.21), channel_id=1, replica_groups={{0,8,16,24,32,40,48,56},{1,9,17,25,33,41,49,57},{2,10,18,26,34,42,50,58..., dimensions={0} | all-to-all | bytes 589824 | tf_op jit(solution)/shard_map/all_to_all | solution.py:54
  117.5 12.1 %all_to_all.75.error_ref = f32[8,72,128]{2,1,0:T(8,128)S(1)} all-to-all(f32[8,72,128]{2,1,0:T(8,128)S(1)} %shard_map.89), channel_id=1, replica_groups={{0,8,16,24,32,40,48,56},{1,9,17,25,33,41,49,57},{2,10,18,26,34,42,50,58..., dimensions={0} | all-to-all | bytes 589824 | tf_op jit(solution)/shard_map/all_to_all | solution.py:54
  129.5 1.6 shard_map.90
  131.1 12.1 %all_to_all.76.parts_ref = f32[8,72,128]{2,1,0:T(8,128)S(1)} all-to-all(f32[8,72,128]{2,1,0:T(8,128)S(1)} %get-tuple-element.25), channel_id=1, replica_groups={{0,8,16,24,32,40,48,56},{1,9,17,25,33,41,49,57},{2,10,18,26,34,42,50,58..., dimensions={0} | all-to-all | bytes 589824 | tf_op jit(solution)/shard_map/all_to_all | solution.py:54
  143.2 12.1 %all_to_all.77.error_ref = f32[8,72,128]{2,1,0:T(8,128)S(1)} all-to-all(f32[8,72,128]{2,1,0:T(8,128)S(1)} %shard_map.91), channel_id=1, replica_groups={{0,8,16,24,32,40,48,56},{1,9,17,25,33,41,49,57},{2,10,18,26,34,42,50,58..., dimensions={0} | all-to-all | bytes 589824 | tf_op jit(solution)/shard_map/all_to_all | solution.py:54
  155.3 1.6 shard_map.92
  156.9 12.1 %all_to_all.78.parts_ref = f32[8,72,128]{2,1,0:T(8,128)S(1)} all-to-all(f32[8,72,128]{2,1,0:T(8,128)S(1)} %get-tuple-element.27), channel_id=1, replica_groups={{0,8,16,24,32,40,48,56},{1,9,17,25,33,41,49,57},{2,10,18,26,34,42,50,58..., dimensions={0} | all-to-all | bytes 589824 | tf_op jit(solution)/shard_map/all_to_all | solution.py:54
  169.0 12.1 %all_to_all.79.error_ref = f32[8,72,128]{2,1,0:T(8,128)S(1)} all-to-all(f32[8,72,128]{2,1,0:T(8,128)S(1)} %shard_map.93), channel_id=1, replica_groups={{0,8,16,24,32,40,48,56},{1,9,17,25,33,41,49,57},{2,10,18,26,34,42,50,58..., dimensions={0} | all-to-all | bytes 589824 | tf_op jit(solution)/shard_map/all_to_all | solution.py:54
  181.8 12.9 %all_to_all.80.parts_ref = f32[8,48,128]{2,1,0:T(8,128)S(1)} all-to-all(f32[8,48,128]{2,1,0:T(8,128)S(1)} %shard_map.94), channel_id=1, replica_groups={{0,1,2,3,4,5,6,7},{8,9,10,11,12,13,14,15},{16,17,18,19,20,21,22,23},{24..., dimensions={0} | all-to-all | bytes 393216 | tf_op jit(solution)/shard_map/all_to_all | solution.py:54
  194.8 21.6 %all_to_all.81.updates_ref = f32[8,16,384]{2,1,0:T(8,128)S(1)} all-to-all(f32[8,16,384]{2,1,0:T(8,128)S(1)} %shard_map.95), channel_id=1, replica_groups=mesh['x'=4,'core'=2,'z'=8,'y'=8] {'x','core'}, dimensions={0} | all-to-all | bytes 393216 | tf_op jit(solution)/shard_map/all_to_all | solution.py:54
  216.7 7.9 %all_to_all.82.parts_ref = f32[8,1,128]{2,1,0:T(1,128)S(1)} all-to-all(f32[8,1,128]{2,1,0:T(1,128)S(1)} %shard_map.96), channel_id=1, replica_groups=mesh['x'=4,'core'=2,'z'=8,'y'=8] {'x','core'}, dimensions={0} | all-to-all | bytes 8192 | tf_op jit(solution)/shard_map/all_to_all | solution.py:54
  224.6 14.6 %all_to_all.83.parts_ref = f32[64,1,128]{2,1,0:T(1,128)S(1)} all-to-all(f32[64,1,128]{2,1,0:T(1,128)S(1)} %shard_map.97), channel_id=1, replica_groups=mesh['x'=4,'core'=2,'z'=8,'y'=8] {'z','y'}, dimensions={0} | all-to-all | bytes 65536 | tf_op jit(solution)/shard_map/all_to_all | solution.py:54
  (27 shorter events, 3.1 us)
Async XLA Ops:
  6.5 8.5 %copy-start.1 = (bf16[128,384]{1,0:T(8,128)(2,1)S(1)}, bf16[128,384]{1,0:T(8,128)(2,1)}, u32[]{:S(2)}) copy-start(bf16[128,384]{1,0:T(8,128)(2,1)} %w_ref.1) | copy-start | bytes 294916
  6.5 94.8 %all-gather.2.cloned.1.call-start = ((), (), s32[]{:S(2)}) async-start(), calls=%async_computation.14 | async-start | bytes 7077888 | tf_op jit(solution)/shard_map/all_gather | solution.py:458
  6.5 1.0 copy-start.3
  7.5 0.9 copy-start.4
  9.4 40.0 %copy-start.5 = (bf16[1,128,384]{2,1,0:T(8,128)(2,1)S(1)}, bf16[1,128,384]{2,1,0:T(8,128)(2,1)}, u32[]{:S(2)}) copy-start(bf16[1,128,384]{2,1,0:T(8,128)(2,1)} %param.9) | copy-start | bytes 294916
  9.4 40.0 %copy-start.6 = (bf16[1,128,384]{2,1,0:T(8,128)(2,1)S(1)}, bf16[1,128,384]{2,1,0:T(8,128)(2,1)}, u32[]{:S(2)}) copy-start(bf16[1,128,384]{2,1,0:T(8,128)(2,1)} %param.10) | copy-start | bytes 294916
  9.5 1.1 copy-start
  10.6 1.0 copy-start.2
  11.6 0.7 copy-start.7
Sparse Core Ops, SparseCore 0:
  9.5 75.3 all-gather.1

commit v6 on v3

--- a/solution.py
+++ b/solution.py
@@ -49,7 +49,6 @@
 
 UP = [(group[i], group[(i + 1) % SIDE]) for group in GATHER_GROUPS for i in range(SIDE)]
 DOWN = [(group[i], group[(i - 1) % SIDE]) for group in GATHER_GROUPS for i in range(SIDE)]
-ACROSS = [(group[i], group[(i + 4) % SIDE]) for group in GATHER_GROUPS for i in range(SIDE)]
 
 
 def exchange(blocks, axes, groups=None):
@@ -112,59 +111,104 @@
             pltpu.VMEM((TABLE - POOL, LANES), BF16),
             pltpu.SemaphoreType.DMA((2,)),
         ],
-        compiler_params=pltpu.CompilerParams(vmem_limit_bytes=4 * MIB),
+        compiler_params=pltpu.CompilerParams(vmem_limit_bytes=56 * MIB),
     )(shared_inputs, private_inputs)
 
 
+def turned_product(left, right):
+    return lax.dot_general(left, right, (((1,), (1,)), ((), ())), preferred_element_type=F32)
+
+
+def constant_kernel(place_ref, ids_ref, shared_ref, private_ref, out_ref, rows, turned, arrived):
+    i, j = place_ref[0], place_ref[1]
+    shared_rows = pl.ds(pl.multiple_of(i * LANES, LANES), LANES)
+    private_rows = pl.ds(pl.multiple_of(lax.div(i, 2) * LANES, LANES), LANES)
+    copies = [
+        pltpu.make_async_copy(shared_ref.at[shared_rows], rows.at[0], arrived.at[0]),
+        pltpu.make_async_copy(private_ref.at[private_rows], rows.at[1], arrived.at[1]),
+    ]
+    for copy in copies:
+        copy.start()
+    row = lax.broadcasted_iota(jnp.int32, (LANES, TOKENS), 0)
+    ones = jnp.ones((16, TOKENS), BF16)
+    for start, lines in (
+        (i * LANES, slice(0, COLS)),
+        (POOL + lax.div(i, 2) * LANES, slice(COLS, TILE)),
+    ):
+        for step in range(STEPS):
+            hits = jnp.where(ids_ref[step : step + 1, :] == row + start, 1.0, 0.0).astype(BF16)
+            count = turned_product(ones, hits)[:1]
+            out_ref[step, lines, :] = jnp.broadcast_to(count, (lines.stop - lines.start, LANES))
+    for copy in copies:
+        copy.wait()
+    turned[...] = rows[0].astype(F32).T
+    columns = pl.ds(pl.multiple_of(j * COLS, 8), COLS)
+    out_ref[STEPS, :COLS, :] = turned[columns, :]
+    turned[...] = rows[1].astype(F32).T
+    columns = pl.ds(pl.multiple_of(j * COLS + lax.rem(i, 2) * HALF, 8), HALF)
+    out_ref[STEPS, COLS:, :] = turned[columns, :]
+
+
+def own_constants(places, ids, shared_targets, private_targets):
+    return pl.pallas_call(
+        constant_kernel,
+        in_specs=[
+            pl.BlockSpec(memory_space=pltpu.SMEM),
+            pl.BlockSpec(memory_space=pltpu.VMEM),
+            pl.BlockSpec(memory_space=pl.ANY),
+            pl.BlockSpec(memory_space=pl.ANY),
+        ],
+        out_shape=shaped(STEPS + 1, TILE, LANES),
+        scratch_shapes=[
+            pltpu.VMEM((2, LANES, SIDE * COLS), BF16),
+            pltpu.VMEM((SIDE * COLS, LANES), F32),
+            pltpu.SemaphoreType.DMA((2,)),
+        ],
+        compiler_params=pltpu.CompilerParams(vmem_limit_bytes=8 * MIB),
+    )(places, ids, shared_targets, private_targets)
+
+
 def narrow_kernel(*refs):
-    *blocks, out_ref = refs
+    *blocks, out_ref, turned_ref = refs
     for k, block in enumerate(blocks):
-        out_ref[:, k * LANES : (k + 1) * LANES] = block[...].astype(BF16)
+        columns = slice(k * LANES, (k + 1) * LANES)
+        narrow = block[...].astype(BF16)
+        out_ref[:, columns] = narrow
+        turned_ref[columns, :] = narrow.T
 
 
 def narrowed(*blocks):
-    return kernel_call(narrow_kernel, shaped(TABLE, len(blocks) * LANES, dtype=BF16), *blocks)
-
-
-def turned_product(weights, table_rows):
-    return lax.dot_general(
-        weights, table_rows, (((1,), (1,)), ((), ())), preferred_element_type=F32
-    )
-
-
-def early_kernel(
-    place_ref, start_ref, target_ref, count_ref, own_ref, *refs
-):
-    pairs, (states_ref, constant_ref, part_ref) = refs[:2], refs[2:]
-    place = place_ref[0]
+    columns = len(blocks) * LANES
+    return kernel_call(
+        narrow_kernel, [shaped(TABLE, columns, dtype=BF16), shaped(columns, TABLE, dtype=BF16)], *blocks
+    )
+
+
+def product_of(left, right):
+    return jnp.dot(left, right, preferred_element_type=F32)
+
+
+def weights_of(states_ref, *places):
+    return jnp.concatenate([states_ref[k, :COLS, :] for k in places], axis=1).astype(BF16)
+
+
+def early_kernel(place_ref, start_ref, constant_ref, own_ref, *refs):
+    pairs, (states_ref, part_ref) = refs[:3], refs[3:]
+    place = place_ref[1]
     for k, offset in enumerate(OFFSETS):
         states_ref[k] = start_ref[lax.rem(place + (offset + SIDE), SIDE)]
-    constant_ref[:STEPS] = count_ref[...]
-    constant_ref[STEPS] = target_ref[...]
-    weights = [states_ref[k, :COLS, :].astype(BF16) for k in range(SIDE)]
-    for row in range(0, TABLE, WIDE):
-        rows = slice(row, row + WIDE)
-        part = turned_product(weights[0], own_ref[rows, :])
-        for k, pair in enumerate(pairs):
-            both = jnp.concatenate(weights[2 * k + 2 : 2 * k + 4], axis=1)
-            part = part + turned_product(both, pair[rows, :])
-        part_ref[:, rows] = part
-
-
-def late_kernel(
-    states_ref, upward_ref, downward_ref, opposite_ref, part_ref, pair_ref, single_ref, out_ref
-):
-    pair_ref[:, :LANES] = upward_ref[...].astype(BF16)
-    pair_ref[:, LANES:] = downward_ref[...].astype(BF16)
-    single_ref[...] = opposite_ref[...].astype(BF16)
-    weights = jnp.concatenate([states_ref[k, :COLS, :] for k in (6, 7)], axis=1).astype(BF16)
-    single = states_ref[1, :COLS, :].astype(BF16)
-    output = []
-    for row in range(0, TABLE, WIDE):
-        rows = slice(row, row + WIDE)
-        part = part_ref[:, rows] + turned_product(weights, pair_ref[rows, :])
-        output.append(part + turned_product(single, single_ref[rows, :]))
-    store_output(out_ref, jnp.concatenate(output, axis=1))
+    part = product_of(weights_of(states_ref, 0), own_ref[...])
+    for k, pair in enumerate(pairs):
+        part = part + product_of(weights_of(states_ref, 2 * k + 2, 2 * k + 3), pair[...])
+    part_ref[...] = part
+
+
+def late_kernel(states_ref, opposite_ref, part_ref, table_ref, turned_ref, out_ref):
+    narrow = opposite_ref[...].astype(BF16)
+    table_ref[...] = narrow
+    turned_ref[...] = narrow.T
+    output = part_ref[...] + product_of(weights_of(states_ref, 1), turned_ref[...])
+    store_output(out_ref, output)
 
 
 def error_kernel(step, parts_ref, constant_ref, out_ref):
@@ -179,12 +223,11 @@
 
 def step_kernel(first, last, place_ref, error_ref, *refs):
     own, opposite, *pairs = refs[:5]
-    w_ref, states_ref, *rest = refs[5:]
     if last:
-        (total_out,) = rest
-        place = place_ref[0]
+        w_ref, states_ref, total_out = refs[5:]
+        place = place_ref[1]
     else:
-        new_states, output_ref = rest
+        turned, (w_ref, states_ref, new_states, output_ref) = refs[5:10], refs[10:]
     error = jnp.concatenate(
         [error_ref[j, :COLS, :] for j in range(SIDE)]
         + [
@@ -202,7 +245,7 @@
             columns = jnp.concatenate([own[...], opposite[...]], axis=1)
         else:
             columns = pairs[k - 1][...]
-        product = jnp.dot(both, columns, preferred_element_type=F32)
+        product = product_of(both, columns)
         gradients = (product[:COLS] + product[COLS:]) * (1.0 / TOKENS)
         for half in range(2):
             j = 2 * k + half
@@ -231,13 +274,14 @@
                 updated.append((weight_start - learn_rate * update_sum).astype(BF16))
     if last:
         return
-    weights = jnp.concatenate(updated, axis=1)
-    output = []
-    for row in range(0, TABLE, WIDE):
-        rows = slice(row, row + WIDE)
-        table_rows = jnp.concatenate([table[rows, :] for table in refs[:5]], axis=1)
-        output.append(turned_product(weights, table_rows))
-    store_output(output_ref, jnp.concatenate(output, axis=1))
+    output = product_of(
+        jnp.concatenate(updated[:2], axis=1),
+        jnp.concatenate([turned[0][...], turned[1][...]], axis=0),
+    )
+    for k in range(1, SIDE // 2):
+        weights = jnp.concatenate(updated[2 * k : 2 * k + 2], axis=1)
+        output = output + product_of(weights, turned[k + 1][...])
+    store_output(output_ref, output)
 
 
 def turn_kernel(parts_ref, out_ref):
@@ -297,28 +341,6 @@
     out_ref[...] = result
 
 
-def own_targets(shared_targets, private_targets, sum_place, gather_place):
-    rows = lax.dynamic_slice_in_dim(shared_targets, sum_place * LANES, LANES, 0)
-    shared = lax.dynamic_slice_in_dim(rows.astype(F32).T, gather_place * COLS, COLS, 0)
-    rows = lax.dynamic_slice_in_dim(private_targets, (sum_place // 2) * LANES, LANES, 0)
-    line = gather_place * COLS + (sum_place % 2) * HALF
-    private = lax.dynamic_slice_in_dim(rows.astype(F32).T, line, HALF, 0)
-    return jnp.concatenate([shared, private], axis=0)
-
-
-def own_counts(token_ids, sum_place):
-    lane = lax.iota(jnp.int32, LANES)
-    counts = []
-    for start, lines in (
-        (sum_place * LANES, COLS),
-        (POOL + (sum_place // 2) * LANES, HALF),
-    ):
-        hits = (token_ids[:, :, None] == (start + lane)[None, None, :]).astype(F32)
-        count = jnp.sum(hits, axis=1)
-        counts.append(jnp.broadcast_to(count[:, None, :], (STEPS, lines, LANES)))
-    return jnp.concatenate(counts, axis=1)
-
-
 def on_device(
     weight,
     first_moment,
@@ -335,8 +357,10 @@
     sum_place = jnp.where(core == 0, z, y)
     gather_place = jnp.where(core == 0, y, z)
 
+    places = jnp.stack([sum_place, gather_place]).astype(jnp.int32)
+    constants = own_constants(places, token_ids[0], shared_targets, private_targets[0])
     own = widened(shared_inputs, private_inputs[0])
-    own_table = narrowed(own)
+    own_table, own_turned = narrowed(own)
     tables = []
     upward = downward = own
     for hop in range(3):
@@ -344,45 +368,36 @@
             upward, tables[hop - 2] = lax.optimization_barrier((upward, tables[hop - 2]))
         upward = lax.ppermute(upward, CZY, UP)
         downward = lax.ppermute(downward, CZY, DOWN)
-        if hop == 0:
-            opposite = lax.ppermute(own, CZY, ACROSS)
-        tables.append(narrowed(upward, downward) if hop < 2 else None)
+        tables.append(narrowed(upward, downward))
+    opposite, tables[1] = lax.optimization_barrier((upward, tables[1]))
+    opposite = lax.ppermute(opposite, CZY, UP)
 
     start = kernel_call(
         states_kernel, shaped(SIDE, 3 * COLS, LANES), weight, first_moment[0], second_moment[0]
     )
     start = exchange(start, CZY, GATHER_GROUPS)
-    targets = own_targets(shared_targets, private_targets[0], sum_place, gather_place)
-    counts = own_counts(token_ids[0], sum_place)
-    place = gather_place.astype(jnp.int32).reshape(1)
-
-    start, constants, part = kernel_call(
+    start, part = kernel_call(
         early_kernel,
-        [
-            shaped(SIDE, 3 * COLS, LANES),
-            shaped(STEPS + 1, TILE, LANES),
-            shaped(COLS, TABLE),
-        ],
-        place,
+        [shaped(SIDE, 3 * COLS, LANES), shaped(COLS, TABLE)],
+        places,
         start,
-        targets,
-        counts,
-        own_table,
-        *tables[:2],
-    )
-    tables[2], opposite, parts = kernel_call(
+        constants,
+        own_turned,
+        *[turned for _, turned in tables],
+        room=20,
+    )
+    opposite_table, opposite_turned, parts = kernel_call(
         late_kernel,
         [
-            shaped(TABLE, WIDE, dtype=BF16),
             shaped(TABLE, LANES, dtype=BF16),
+            shaped(LANES, TABLE, dtype=BF16),
             shaped(SIDE, TILE, LANES),
         ],
         start,
-        upward,
-        downward,
         opposite,
         part,
     )
+    tables = [(own_table, own_turned), (opposite_table, opposite_turned), *tables]
     states = start
     for step in range(STEPS):
         parts = exchange(parts, CZY, SUM_GROUPS)
@@ -392,12 +407,17 @@
         error = exchange(error, CZY, SUM_GROUPS)
         last = step == STEPS - 1
         body = functools.partial(step_kernel, step == 0, last)
-        operands = (place, error, own_table, opposite, *tables, start, states)
+        operands = (places, error, *[table for table, _ in tables])
         if last:
-            updates = kernel_call(body, shaped(SIDE, COLS, LANES), *operands)
+            updates = kernel_call(body, shaped(SIDE, COLS, LANES), *operands, start, states)
         else:
             states, parts = kernel_call(
-                body, [shaped(SIDE, 3 * COLS, LANES), shaped(SIDE, TILE, LANES)], *operands
+                body,
+                [shaped(SIDE, 3 * COLS, LANES), shaped(SIDE, TILE, LANES)],
+                *operands,
+                *[turned for _, turned in tables],
+                start,
+                states,
             )
 
     updates = exchange(updates, CZY, GATHER_GROUPS)

time: 246 us -> 245 us (level)
  starting transfers between devices: 37.7 us -> 32.6 us
  Pallas kernels: 14.8 us -> 19.1 us
  other arithmetic: 3.66 us -> 0.08 us
  local copies, waits for them, and re-layouts: 4.72 us -> 7.35 us
    ppermute x3, waiting for transfers between devices: 12.3 us -> 2.46 us  [on_device(): downward = lax.ppermute(downward, CZY, DOWN)]
    ppermute x3, waiting for transfers between devices: 7.84 us -> 17.5 us  [on_device(): upward = lax.ppermute(upward, CZY, UP)]
    unnamed x19 -> x32, local copies, waits for them, and re-layouts: 3.71 us -> 7.35 us
    ppermute x1, starting transfers between devices: 4.54 us -> 1.91 us  [on_device(): opposite = lax.ppermute(opposite, CZY, UP)]
    pallas_call x18 -> x19, Pallas kernels: 14.6 us -> 15.6 us  [kernel_call(): pl.pallas_call(body, in_specs=in_specs, out_shape=out_shapes, compiler_pa...]
  transfers between devices with their start and end apart: 8 -> 8, of which waited for: 3 -> 4; matrix products, arithmetic and copies ran while one was open for 2% -> 0% of each run, Pallas kernels for 2% -> 3%
where the time goes in v6:
time: 245 us; the launch traced here: 244 us
  blocking collectives  164 us (67%)
  starting transfers between devices  32.6 us (13%)
  waiting for transfers between devices  20 us (8%)
  Pallas kernels  19.1 us (8%)
  local copies, waits for them, and re-layouts  7.35 us (3%)
    all_to_all x12, blocking collectives, exchange(): lax.all_to_all(blocks, axes, split_axis=0, concat_axis=0, tiled=True, axi...  164 us
    ppermute x3, starting transfers between devices, on_device(): downward = lax.ppermute(downward, CZY, DOWN)  17.7 us
    ppermute x3, waiting for transfers between devices, on_device(): upward = lax.ppermute(upward, CZY, UP)  17.5 us
    pallas_call x19, Pallas kernels, kernel_call(): pl.pallas_call(body, in_specs=in_specs, out_shape=out_shapes, compiler_pa...  15.6 us
    ppermute x3, starting transfers between devices, on_device(): upward = lax.ppermute(upward, CZY, UP)  8.78 us
    unnamed x32, local copies, waits for them, and re-layouts  7.35 us
  transfers between devices with their start and end apart: 8, of which 4 were waited for; matrix products, arithmetic and copies ran while one was open for 0% of the time, Pallas kernels for 3%

profile of v6, /device:TPU:1, one launch (start us, length us, event | category | flops | bytes accessed | tf_op | source)
XLA Modules:
  0.0 243.6 jit_solution(3441331744426588908)
XLA Ops:
  2.0 5.0 %collective-permute-start = (f32[1536,128]{1,0:T(8,128)}, f32[1536,128]{1,0:T(8,128)S(1)}, u32[]{:S(2)}, u32[]{:S(2)}) collective-permute-start(f32[1536,128]{1,0:T(8,128)} %shard_map.84.refs_0_), channel_id=1, source_target_pairs={{0,1},{1,2},{2,3},{3,4},{4,5},{5,6},{6,7},{7,0},{8,9},{9,10},{10,1... | collective-permute-start | bytes 2359304 | tf_op jit(solution)/shard_map/ppermute | solution.py:369
  6.9 8.6 %collective-permute-start.2 = (f32[1536,128]{1,0:T(8,128)}, f32[1536,128]{1,0:T(8,128)S(1)}, u32[]{:S(2)}, u32[]{:S(2)}) collective-permute-start(f32[1536,128]{1,0:T(8,128)} %shard_map.84.refs_0_), channel_id=1, source_target_pairs={{0,7},{1,0},{2,1},{3,2},{4,3},{5,4},{6,5},{7,6},{8,15},{9,8},{10,9... | collective-permute-start | bytes 2359304 | tf_op jit(solution)/shard_map/ppermute | solution.py:370
  15.5 7.9 %collective-permute-done.refs_0_ = f32[1536,128]{1,0:T(8,128)S(1)} collective-permute-done((f32[1536,128]{1,0:T(8,128)}, f32[1536,128]{1,0:T(8,128)S(1)}, u32[]{:S(2)}, u32[]{:S(2)}) %collective-permute-start) | collective-permute-done | bytes 786464 | tf_op jit(solution)/shard_map/ppermute | solution.py:369
  23.5 1.9 collective-permute-start.1
  25.4 4.6 %collective-permute-start.4 = (f32[1536,128]{1,0:T(8,128)S(1)}, f32[1536,128]{1,0:T(8,128)}, u32[]{:S(2)}, u32[]{:S(2)}) collective-permute-start(f32[1536,128]{1,0:T(8,128)S(1)} %collective-permute-done.2.refs_1_), channel_id=1, source_target_pairs={{0,7},{1,0},{2,1},{3,2},{4,3},{5,4},{6,5},{7,6},{8,15},{9,8},{10,9... | collective-permute-start | bytes 2359304 | tf_op jit(solution)/shard_map/ppermute | solution.py:370
  30.3 7.5 %collective-permute-done.1.refs_0_ = f32[1536,128]{1,0:T(8,128)} collective-permute-done((f32[1536,128]{1,0:T(8,128)S(1)}, f32[1536,128]{1,0:T(8,128)}, u32[]{:S(2)}, u32[]{:S(2)}) %collective-permute-start.1) | collective-permute-done | bytes 786464 | tf_op jit(solution)/shard_map/ppermute | solution.py:369
  37.8 1.9 collective-permute-start.3
  40.7 4.2 %all-to-all-start = ((f32[8,144,128]{2,1,0:T(8,128)}), f32[8,144,128]{2,1,0:T(8,128)}, u32[]{:S(2)}, u32[]{:S(2)}) async-start(f32[8,144,128]{2,1,0:T(8,128)} %shard_map.82), calls=%async_computation | async-start | bytes 1179648 | tf_op jit(solution)/shard_map/all_to_all | solution.py:55
  44.9 4.5 %collective-permute-start.5 = (f32[1536,128]{1,0:T(8,128)}, f32[1536,128]{1,0:T(8,128)}, u32[]{:S(2)}, u32[]{:S(2)}) collective-permute-start(f32[1536,128]{1,0:T(8,128)} %collective-permute-done.4.refs_1_), channel_id=1, source_target_pairs={{0,7},{1,0},{2,1},{3,2},{4,3},{5,4},{6,5},{7,6},{8,15},{9,8},{10,9... | collective-permute-start | bytes 2359304 | tf_op jit(solution)/shard_map/ppermute | solution.py:370
  51.2 2.0 collective-permute-done.3.refs_0_
  53.2 1.9 collective-permute-start.6
  60.2 2.5 %collective-permute-done.5.refs_1_ = f32[1536,128]{1,0:T(8,128)} collective-permute-done((f32[1536,128]{1,0:T(8,128)}, f32[1536,128]{1,0:T(8,128)}, u32[]{:S(2)}, u32[]{:S(2)}) %collective-permute-start.5) | collective-permute-done | bytes 786464 | tf_op jit(solution)/shard_map/ppermute | solution.py:370
  71.6 16.3 %all_to_all.65.parts_ref = f32[8,72,128]{2,1,0:T(8,128)S(1)} all-to-all(f32[8,72,128]{2,1,0:T(8,128)S(1)} %get-tuple-element.42), channel_id=1, replica_groups={{0,8,16,24,32,40,48,56},{1,9,17,25,33,41,49,57},{2,10,18,26,34,42,50,58..., dimensions={0} | all-to-all | bytes 589824 | tf_op jit(solution)/shard_map/all_to_all | solution.py:55
  87.9 12.2 %all_to_all.66.error_ref = f32[8,72,128]{2,1,0:T(8,128)S(1)} all-to-all(f32[8,72,128]{2,1,0:T(8,128)S(1)} %shard_map.91), channel_id=1, replica_groups={{0,8,16,24,32,40,48,56},{1,9,17,25,33,41,49,57},{2,10,18,26,34,42,50,58..., dimensions={0} | all-to-all | bytes 589824 | tf_op jit(solution)/shard_map/all_to_all | solution.py:55
  101.8 12.1 %all_to_all.67.parts_ref = f32[8,72,128]{2,1,0:T(8,128)S(1)} all-to-all(f32[8,72,128]{2,1,0:T(8,128)S(1)} %get-tuple-element.49), channel_id=1, replica_groups={{0,8,16,24,32,40,48,56},{1,9,17,25,33,41,49,57},{2,10,18,26,34,42,50,58..., dimensions={0} | all-to-all | bytes 589824 | tf_op jit(solution)/shard_map/all_to_all | solution.py:55
  113.9 12.2 %all_to_all.68.error_ref = f32[8,72,128]{2,1,0:T(8,128)S(1)} all-to-all(f32[8,72,128]{2,1,0:T(8,128)S(1)} %shard_map.93), channel_id=1, replica_groups={{0,8,16,24,32,40,48,56},{1,9,17,25,33,41,49,57},{2,10,18,26,34,42,50,58..., dimensions={0} | all-to-all | bytes 589824 | tf_op jit(solution)/shard_map/all_to_all | solution.py:55
  127.9 12.1 %all_to_all.69.parts_ref = f32[8,72,128]{2,1,0:T(8,128)S(1)} all-to-all(f32[8,72,128]{2,1,0:T(8,128)S(1)} %get-tuple-element.51), channel_id=1, replica_groups={{0,8,16,24,32,40,48,56},{1,9,17,25,33,41,49,57},{2,10,18,26,34,42,50,58..., dimensions={0} | all-to-all | bytes 589824 | tf_op jit(solution)/shard_map/all_to_all | solution.py:55
  139.9 12.1 %all_to_all.70.error_ref = f32[8,72,128]{2,1,0:T(8,128)S(1)} all-to-all(f32[8,72,128]{2,1,0:T(8,128)S(1)} %shard_map.95), channel_id=1, replica_groups={{0,8,16,24,32,40,48,56},{1,9,17,25,33,41,49,57},{2,10,18,26,34,42,50,58..., dimensions={0} | all-to-all | bytes 589824 | tf_op jit(solution)/shard_map/all_to_all | solution.py:55
  153.7 12.1 %all_to_all.71.parts_ref = f32[8,72,128]{2,1,0:T(8,128)S(1)} all-to-all(f32[8,72,128]{2,1,0:T(8,128)S(1)} %get-tuple-element.53), channel_id=1, replica_groups={{0,8,16,24,32,40,48,56},{1,9,17,25,33,41,49,57},{2,10,18,26,34,42,50,58..., dimensions={0} | all-to-all | bytes 589824 | tf_op jit(solution)/shard_map/all_to_all | solution.py:55
  165.8 12.1 %all_to_all.72.error_ref = f32[8,72,128]{2,1,0:T(8,128)S(1)} all-to-all(f32[8,72,128]{2,1,0:T(8,128)S(1)} %shard_map.97), channel_id=1, replica_groups={{0,8,16,24,32,40,48,56},{1,9,17,25,33,41,49,57},{2,10,18,26,34,42,50,58..., dimensions={0} | all-to-all | bytes 589824 | tf_op jit(solution)/shard_map/all_to_all | solution.py:55
  179.1 14.2 %all_to_all.73.parts_ref = f32[8,48,128]{2,1,0:T(8,128)S(1)} all-to-all(f32[8,48,128]{2,1,0:T(8,128)S(1)} %shard_map.98), channel_id=1, replica_groups={{0,1,2,3,4,5,6,7},{8,9,10,11,12,13,14,15},{16,17,18,19,20,21,22,23},{24..., dimensions={0} | all-to-all | bytes 393216 | tf_op jit(solution)/shard_map/all_to_all | solution.py:55
  193.5 26.5 %all_to_all.74.updates_ref = f32[8,16,384]{2,1,0:T(8,128)S(1)} all-to-all(f32[8,16,384]{2,1,0:T(8,128)S(1)} %shard_map.99), channel_id=1, replica_groups=mesh['x'=4,'core'=2,'z'=8,'y'=8] {'x','core'}, dimensions={0} | all-to-all | bytes 393216 | tf_op jit(solution)/shard_map/all_to_all | solution.py:55
  220.2 7.9 %all_to_all.75.parts_ref = f32[8,1,128]{2,1,0:T(1,128)S(1)} all-to-all(f32[8,1,128]{2,1,0:T(1,128)S(1)} %shard_map.100), channel_id=1, replica_groups=mesh['x'=4,'core'=2,'z'=8,'y'=8] {'x','core'}, dimensions={0} | all-to-all | bytes 8192 | tf_op jit(solution)/shard_map/all_to_all | solution.py:55
  228.1 14.6 %all_to_all.76.parts_ref = f32[64,1,128]{2,1,0:T(1,128)S(1)} all-to-all(f32[64,1,128]{2,1,0:T(1,128)S(1)} %shard_map.101), channel_id=1, replica_groups=mesh['x'=4,'core'=2,'z'=8,'y'=8] {'z','y'}, dimensions={0} | all-to-all | bytes 65536 | tf_op jit(solution)/shard_map/all_to_all | solution.py:55
  (58 shorter events, 26.6 us)
Async XLA Ops:
  1.9 37.8 %copy-start.12 = (bf16[128,384]{1,0:T(8,128)(2,1)S(1)}, bf16[128,384]{1,0:T(8,128)(2,1)}, u32[]{:S(2)}) copy-start(bf16[128,384]{1,0:T(8,128)(2,1)} %w_ref.1) | copy-start | bytes 294916
  1.9 37.8 %copy-start.13 = (bf16[1,128,384]{2,1,0:T(8,128)(2,1)S(1)}, bf16[1,128,384]{2,1,0:T(8,128)(2,1)}, u32[]{:S(2)}) copy-start(bf16[1,128,384]{2,1,0:T(8,128)(2,1)} %param.9) | copy-start | bytes 294916
  1.9 37.8 %copy-start.14 = (bf16[1,128,384]{2,1,0:T(8,128)(2,1)S(1)}, bf16[1,128,384]{2,1,0:T(8,128)(2,1)}, u32[]{:S(2)}) copy-start(bf16[1,128,384]{2,1,0:T(8,128)(2,1)} %param.10) | copy-start | bytes 294916
  2.0 21.5 %collective-permute-start = (f32[1536,128]{1,0:T(8,128)}, f32[1536,128]{1,0:T(8,128)S(1)}, u32[]{:S(2)}, u32[]{:S(2)}) collective-permute-start(f32[1536,128]{1,0:T(8,128)} %shard_map.84.refs_0_), channel_id=1, source_target_pairs={{0,1},{1,2},{2,3},{3,4},{4,5},{5,6},{6,7},{7,0},{8,9},{9,10},{10,1... | collective-permute-start | bytes 2359304 | tf_op jit(solution)/shard_map/ppermute | solution.py:369
  6.9 18.5 %collective-permute-start.2 = (f32[1536,128]{1,0:T(8,128)}, f32[1536,128]{1,0:T(8,128)S(1)}, u32[]{:S(2)}, u32[]{:S(2)}) collective-permute-start(f32[1536,128]{1,0:T(8,128)} %shard_map.84.refs_0_), channel_id=1, source_target_pairs={{0,7},{1,0},{2,1},{3,2},{4,3},{5,4},{6,5},{7,6},{8,15},{9,8},{10,9... | collective-permute-start | bytes 2359304 | tf_op jit(solution)/shard_map/ppermute | solution.py:370
  23.5 14.3 %collective-permute-start.1 = (f32[1536,128]{1,0:T(8,128)S(1)}, f32[1536,128]{1,0:T(8,128)}, u32[]{:S(2)}, u32[]{:S(2)}) collective-permute-start(f32[1536,128]{1,0:T(8,128)S(1)} %collective-permute-done.refs_0_), channel_id=1, source_target_pairs={{0,1},{1,2},{2,3},{3,4},{4,5},{5,6},{6,7},{7,0},{8,9},{9,10},{10,1... | collective-permute-start | bytes 2359304 | tf_op jit(solution)/shard_map/ppermute | solution.py:369
  25.4 19.5 %collective-permute-start.4 = (f32[1536,128]{1,0:T(8,128)S(1)}, f32[1536,128]{1,0:T(8,128)}, u32[]{:S(2)}, u32[]{:S(2)}) collective-permute-start(f32[1536,128]{1,0:T(8,128)S(1)} %collective-permute-done.2.refs_1_), channel_id=1, source_target_pairs={{0,7},{1,0},{2,1},{3,2},{4,3},{5,4},{6,5},{7,6},{8,15},{9,8},{10,9... | collective-permute-start | bytes 2359304 | tf_op jit(solution)/shard_map/ppermute | solution.py:370
  37.8 15.4 %collective-permute-start.3 = (f32[1536,128]{1,0:T(8,128)}, f32[1536,128]{1,0:T(8,128)}, u32[]{:S(2)}, u32[]{:S(2)}) collective-permute-start(f32[1536,128]{1,0:T(8,128)} %collective-permute-done.1.refs_0_), channel_id=1, source_target_pairs={{0,1},{1,2},{2,3},{3,4},{4,5},{5,6},{6,7},{7,0},{8,9},{9,10},{10,1... | collective-permute-start | bytes 2359304 | tf_op jit(solution)/shard_map/ppermute | solution.py:369
  40.7 24.5 %all-to-all-start = ((f32[8,144,128]{2,1,0:T(8,128)}), f32[8,144,128]{2,1,0:T(8,128)}, u32[]{:S(2)}, u32[]{:S(2)}) async-start(f32[8,144,128]{2,1,0:T(8,128)} %shard_map.82), calls=%async_computation | async-start | bytes 1179648 | tf_op jit(solution)/shard_map/all_to_all | solution.py:55
  44.9 17.7 %collective-permute-start.5 = (f32[1536,128]{1,0:T(8,128)}, f32[1536,128]{1,0:T(8,128)}, u32[]{:S(2)}, u32[]{:S(2)}) collective-permute-start(f32[1536,128]{1,0:T(8,128)} %collective-permute-done.4.refs_1_), channel_id=1, source_target_pairs={{0,7},{1,0},{2,1},{3,2},{4,3},{5,4},{6,5},{7,6},{8,15},{9,8},{10,9... | collective-permute-start | bytes 2359304 | tf_op jit(solution)/shard_map/ppermute | solution.py:370
  49.5 7.1 %copy-start.15 = (s32[1,4,1024]{2,1,0:T(4,128)S(1)}, s32[1,4,1024]{2,1,0:T(4,128)}, u32[]{:S(2)}) copy-start(s32[1,4,1024]{2,1,0:T(4,128)} %param.11) | copy-start | bytes 49156
  51.2 9.0 %copy-start = (bf16[256,1536]{1,0:T(8,128)(2,1)}, bf16[256,1536]{1,0:T(8,128)(2,1)S(1)}, u32[]{:S(2)}) copy-start(bf16[256,1536]{1,0:T(8,128)(2,1)S(1)} %get-tuple-element.37.refs_1_.refs_8_) | copy-start | bytes 2359300
  53.2 16.9 %collective-permute-start.6 = (f32[1536,128]{1,0:T(8,128)}, f32[1536,128]{1,0:T(8,128)}, u32[]{:S(2)}, u32[]{:S(2)}) collective-permute-start(f32[1536,128]{1,0:T(8,128)} %collective-permute-done.3.refs_0_), channel_id=1, source_target_pairs={{0,1},{1,2},{2,3},{3,4},{4,5},{5,6},{6,7},{7,0},{8,9},{9,10},{10,1... | collective-permute-start | bytes 2359304 | tf_op jit(solution)/shard_map/ppermute | solution.py:373
  55.2 1.1 copy-start.9
  56.3 1.3 copy-start.10
  56.4 3.8 %copy-start.4 = (bf16[1536,128]{1,0:T(8,128)(2,1)}, bf16[1536,128]{1,0:T(8,128)(2,1)S(1)}, u32[]{:S(2)}) copy-start(bf16[1536,128]{1,0:T(8,128)(2,1)S(1)} %get-tuple-element.43.refs_0_) | copy-start | bytes 1179652
  56.5 3.8 %copy-start.6 = (bf16[128,1536]{1,0:T(8,128)(2,1)}, bf16[128,1536]{1,0:T(8,128)(2,1)S(1)}, u32[]{:S(2)}) copy-start(bf16[128,1536]{1,0:T(8,128)(2,1)S(1)} %get-tuple-element.30.own_ref.refs_5_) | copy-start | bytes 1179652
  57.6 1.0 copy-start.11
  64.3 0.9 copy-start.2
  65.3 1.1 copy-start.1
  66.4 1.1 copy-start.3
  67.5 1.0 copy-start.7
  87.9 12.2 %copy-start.5 = (bf16[1536,128]{1,0:T(8,128)(2,1)S(1)}, bf16[1536,128]{1,0:T(8,128)(2,1)}, u32[]{:S(2)}) copy-start(bf16[1536,128]{1,0:T(8,128)(2,1)} %copy-done.4) | copy-start | bytes 1179652
  113.9 12.2 %copy-start.8 = (bf16[128,1536]{1,0:T(8,128)(2,1)S(1)}, bf16[128,1536]{1,0:T(8,128)(2,1)}, u32[]{:S(2)}) copy-start(bf16[128,1536]{1,0:T(8,128)(2,1)} %copy-done.6) | copy-start | bytes 1179652

commit v7 on v2

--- a/solution.py
+++ b/solution.py
@@ -22,8 +22,6 @@
 SIDE = 8
 LANES = 128
 COLS = 48
-HALF = COLS // 2
-TILE = COLS + HALF
 POOL = 1024
 TABLE = 1536
 STEPS = 4
@@ -32,7 +30,7 @@
 PAIRS = [(i, j) for i in range(REPLICAS) for j in range(i, REPLICAS)]
 MIB = 1024 * 1024
 WIDE = 2 * LANES
-OFFSETS = (0, 4, -1, 1, -2, 2, -3, 3)
+OFFSETS = (0, -1, 1, -2, 2, -3, 3, 4)
 
 
 def position(core, z, y):
@@ -74,12 +72,17 @@
     return jax.ShapeDtypeStruct(dims, dtype)
 
 
-def store_output(out_ref, output):
-    for j in range(SIDE):
-        out_ref[j, :COLS, :] = output[:, j * LANES : (j + 1) * LANES]
-        private = POOL + (j // 2) * LANES
-        line = (j % 2) * HALF
-        out_ref[j, COLS:, :] = output[line : line + HALF, private : private + LANES]
+def product_of(left, right):
+    return jnp.dot(left, right, preferred_element_type=F32)
+
+
+def turned_product(left, right):
+    return lax.dot_general(left, right, (((1,), (1,)), ((), ())), preferred_element_type=F32)
+
+
+def store_output(out_ref, token, output):
+    for half in range(2):
+        out_ref[token // LANES + half] = output[:, half * LANES : (half + 1) * LANES]
 
 
 def states_kernel(w_ref, m_ref, v_ref, out_ref):
@@ -115,88 +118,100 @@
     )(shared_inputs, private_inputs)
 
 
-def narrow_kernel(*refs):
-    *blocks, out_ref = refs
-    for k, block in enumerate(blocks):
-        out_ref[:, k * LANES : (k + 1) * LANES] = block[...].astype(BF16)
-
-
-def narrowed(*blocks):
-    return kernel_call(narrow_kernel, shaped(TABLE, len(blocks) * LANES, dtype=BF16), *blocks)
-
-
-def turned_product(weights, table_rows):
-    return lax.dot_general(
-        weights, table_rows, (((1,), (1,)), ((), ())), preferred_element_type=F32
-    )
-
-
-def early_kernel(
-    place_ref, start_ref, target_ref, count_ref, own_ref, *refs
-):
-    pairs, (states_ref, constant_ref, part_ref) = refs[:3], refs[3:]
-    place = place_ref[0]
+def choice(ids, width=TABLE, start=0):
+    row = lax.broadcasted_iota(jnp.int32, (ids.shape[0], width), 1).astype(F32) + start
+    return jnp.where(row == ids, 1.0, 0.0).astype(BF16)
+
+
+def choose(ids_ref, step, pair, out_ref):
+    for token in range(0, TOKENS, WIDE):
+        tokens = slice(token, token + WIDE)
+        chosen = choice(ids_ref[tokens, step : step + 1])
+        out_ref[tokens, :] = product_of(chosen, pair).astype(BF16)
+
+
+def target_kernel(place_ref, ids_ref, shared_ref, private_ref, target_ref, turned):
+    own = pl.ds(pl.multiple_of(place_ref[0] * LANES, LANES), LANES)
+    columns = pl.ds(pl.multiple_of(place_ref[1] * COLS, 16), COLS)
+    for step in range(STEPS):
+        ids = ids_ref[own, step : step + 1]
+        targets = product_of(choice(ids, POOL), shared_ref[...])
+        targets = targets + product_of(choice(ids, TABLE - POOL, POOL), private_ref[...])
+        turned[...] = targets.T
+        target_ref[step] = turned[columns, :]
+
+
+def own_targets(places, ids, shared_targets, private_targets):
+    return pl.pallas_call(
+        target_kernel,
+        in_specs=[pl.BlockSpec(memory_space=pltpu.SMEM)]
+        + [pl.BlockSpec(memory_space=pltpu.VMEM)] * 3,
+        out_shape=shaped(STEPS, COLS, LANES),
+        scratch_shapes=[pltpu.VMEM((SIDE * COLS, LANES), F32)],
+        compiler_params=pltpu.CompilerParams(vmem_limit_bytes=12 * MIB),
+    )(places, ids, shared_targets, private_targets)
+
+
+def pair_of(first_ref, second_ref):
+    return jnp.concatenate([first_ref[...], second_ref[...]], axis=1).astype(BF16)
+
+
+def rows_kernel(ids_ref, first_ref, second_ref, *outs):
+    pair = pair_of(first_ref, second_ref)
+    for step in range(STEPS):
+        choose(ids_ref, step, pair, outs[step])
+
+
+def chosen_rows(ids, first, second):
+    return kernel_call(
+        rows_kernel, [shaped(TOKENS, WIDE, dtype=BF16)] * STEPS, ids, first, second
+    )
+
+
+def early_kernel(place_ref, start_ref, target_ref, *refs):
+    pairs, (states_ref, part_ref) = refs[:3], refs[3:]
+    place = place_ref[1]
     for k, offset in enumerate(OFFSETS):
         states_ref[k] = start_ref[lax.rem(place + (offset + SIDE), SIDE)]
-    constant_ref[:STEPS] = count_ref[...]
-    constant_ref[STEPS] = target_ref[...]
-    weights = [states_ref[k, :COLS, :].astype(BF16) for k in range(SIDE)]
-    for row in range(0, TABLE, WIDE):
-        rows = slice(row, row + WIDE)
-        part = turned_product(weights[0], own_ref[rows, :])
-        for k, pair in enumerate(pairs):
-            both = jnp.concatenate(weights[2 * k + 2 : 2 * k + 4], axis=1)
-            part = part + turned_product(both, pair[rows, :])
-        part_ref[:, rows] = part
-
-
-def late_kernel(states_ref, own_ref, opposite_ref, part_ref, table_ref, out_ref):
-    table_ref[:, :LANES] = own_ref[...]
-    table_ref[:, LANES:] = opposite_ref[...].astype(BF16)
-    weights = states_ref[1, :COLS, :].astype(BF16)
-    output = jnp.concatenate(
-        [
-            part_ref[:, row : row + WIDE]
-            + turned_product(weights, table_ref[row : row + WIDE, LANES:])
-            for row in range(0, TABLE, WIDE)
-        ],
-        axis=1,
-    )
-    store_output(out_ref, output)
-
-
-def error_kernel(step, parts_ref, constant_ref, out_ref):
+    weights = jnp.concatenate([states_ref[k, :COLS, :] for k in range(6)], axis=1).astype(BF16)
+    for token in range(0, TOKENS, WIDE):
+        tokens = slice(token, token + WIDE)
+        rows = jnp.concatenate([pair[tokens, :] for pair in pairs], axis=1)
+        part_ref[:, tokens] = turned_product(weights, rows)
+
+
+def late_kernel(ids_ref, states_ref, first_ref, second_ref, part_ref, *outs):
+    out_ref = outs[STEPS]
+    pair = pair_of(first_ref, second_ref)
+    weights = jnp.concatenate([states_ref[k, :COLS, :] for k in (6, 7)], axis=1).astype(BF16)
+    for step in range(STEPS):
+        choose(ids_ref, step, pair, outs[step])
+    for token in range(0, TOKENS, WIDE):
+        tokens = slice(token, token + WIDE)
+        output = part_ref[:, tokens] + turned_product(weights, outs[0][tokens, :])
+        store_output(out_ref, token, output)
+
+
+def error_kernel(step, parts_ref, target_ref, out_ref):
     output = parts_ref[0]
     for j in range(1, SIDE):
         output = output + parts_ref[j]
-    error = (output - constant_ref[STEPS]).astype(BF16).astype(F32)
-    weighted = error * constant_ref[step]
+    error = (output - target_ref[step]).astype(BF16).astype(F32)
     for j in range(SIDE):
-        out_ref[j] = weighted
-
-
-def step_kernel(first, last, place_ref, error_ref, *refs):
-    tables, (w_ref, states_ref, *rest) = refs[: SIDE // 2], refs[SIDE // 2 :]
+        out_ref[j] = error
+
+
+def step_kernel(first, last, place_ref, error_ref, w_ref, states_ref, *refs):
+    pairs, rest = refs[: SIDE // 2], refs[SIDE // 2 :]
     if last:
         (total_out,) = rest
-        place = place_ref[0]
+        place = place_ref[1]
     else:
-        new_states, output_ref = rest
-    error = jnp.concatenate(
-        [error_ref[j, :COLS, :] for j in range(SIDE)]
-        + [
-            jnp.concatenate([error_ref[2 * k, COLS:, :], error_ref[2 * k + 1, COLS:, :]], axis=0)
-            for k in range(SIDE // 2)
-        ],
-        axis=1,
-    )
-    high = error.astype(BF16)
-    low = (error - high.astype(F32)).astype(BF16)
-    both = jnp.concatenate([high, low], axis=0)
+        next_pairs, (new_states, output_ref) = rest[: SIDE // 2], rest[SIDE // 2 :]
+    error = jnp.concatenate([error_ref[j] for j in range(SIDE)], axis=1).astype(BF16)
     updated = []
     for k in range(SIDE // 2):
-        product = jnp.dot(both, tables[k][...], preferred_element_type=F32)
-        gradients = (product[:COLS] + product[COLS:]) * (1.0 / TOKENS)
+        gradients = product_of(error, pairs[k][...]) * (1.0 / TOKENS)
         for half in range(2):
             j = 2 * k + half
             gradient = gradients[:, half * LANES : (half + 1) * LANES]
@@ -225,12 +240,10 @@
     if last:
         return
     weights = jnp.concatenate(updated, axis=1)
-    output = []
-    for row in range(0, TABLE, WIDE):
-        rows = slice(row, row + WIDE)
-        table_rows = jnp.concatenate([table[rows, :] for table in tables], axis=1)
-        output.append(turned_product(weights, table_rows))
-    store_output(output_ref, jnp.concatenate(output, axis=1))
+    for token in range(0, TOKENS, WIDE):
+        tokens = slice(token, token + WIDE)
+        rows = jnp.concatenate([pair[tokens, :] for pair in next_pairs], axis=1)
+        store_output(output_ref, token, turned_product(weights, rows))
 
 
 def turn_kernel(parts_ref, out_ref):
@@ -290,28 +303,6 @@
     out_ref[...] = result
 
 
-def own_targets(shared_targets, private_targets, sum_place, gather_place):
-    rows = lax.dynamic_slice_in_dim(shared_targets, sum_place * LANES, LANES, 0)
-    shared = lax.dynamic_slice_in_dim(rows.astype(F32).T, gather_place * COLS, COLS, 0)
-    rows = lax.dynamic_slice_in_dim(private_targets, (sum_place // 2) * LANES, LANES, 0)
-    line = gather_place * COLS + (sum_place % 2) * HALF
-    private = lax.dynamic_slice_in_dim(rows.astype(F32).T, line, HALF, 0)
-    return jnp.concatenate([shared, private], axis=0)
-
-
-def own_counts(token_ids, sum_place):
-    lane = lax.iota(jnp.int32, LANES)
-    counts = []
-    for start, lines in (
-        (sum_place * LANES, COLS),
-        (POOL + (sum_place // 2) * LANES, HALF),
-    ):
-        hits = (token_ids[:, :, None] == (start + lane)[None, None, :]).astype(F32)
-        count = jnp.sum(hits, axis=1)
-        counts.append(jnp.broadcast_to(count[:, None, :], (STEPS, lines, LANES)))
-    return jnp.concatenate(counts, axis=1)
-
-
 def on_device(
     weight,
     first_moment,
@@ -329,61 +320,62 @@
     gather_place = jnp.where(core == 0, y, z)
 
     own = widened(shared_inputs, private_inputs[0])
-    tables = [narrowed(own)]
-    upward = downward = own
+    places = jnp.stack([sum_place, gather_place]).astype(jnp.int32)
+    ids = token_ids[0].astype(F32).T
+    targets = own_targets(places, ids, shared_targets, private_targets[0])
+
+    pairs = []
+    upward = downward = held = own
     for hop in range(3):
-        if hop >= 1:
-            upward, tables[hop - 1] = lax.optimization_barrier((upward, tables[hop - 1]))
+        if hop >= 2:
+            upward, pairs[hop - 2] = lax.optimization_barrier((upward, pairs[hop - 2]))
         upward = lax.ppermute(upward, CZY, UP)
         downward = lax.ppermute(downward, CZY, DOWN)
-        tables.append(narrowed(upward, downward))
-    opposite, tables[2] = lax.optimization_barrier((upward, tables[2]))
-    opposite = lax.ppermute(opposite, CZY, UP)
+        pairs.append(chosen_rows(ids, held, upward))
+        held = downward
+    upward, pairs[1] = lax.optimization_barrier((upward, pairs[1]))
+    opposite = lax.ppermute(upward, CZY, UP)
 
     start = kernel_call(
         states_kernel, shaped(SIDE, 3 * COLS, LANES), weight, first_moment[0], second_moment[0]
     )
     start = exchange(start, CZY, GATHER_GROUPS)
-    targets = own_targets(shared_targets, private_targets[0], sum_place, gather_place)
-    counts = own_counts(token_ids[0], sum_place)
-    place = gather_place.astype(jnp.int32).reshape(1)
-
-    start, constants, part = kernel_call(
+    start, part = kernel_call(
         early_kernel,
-        [
-            shaped(SIDE, 3 * COLS, LANES),
-            shaped(STEPS + 1, TILE, LANES),
-            shaped(COLS, TABLE),
-        ],
-        place,
+        [shaped(SIDE, 3 * COLS, LANES), shaped(COLS, TOKENS)],
+        places,
         start,
         targets,
-        counts,
-        *tables,
-    )
-    tables[0], parts = kernel_call(
+        *[pair[0] for pair in pairs],
+    )
+    *late, parts = kernel_call(
         late_kernel,
-        [shaped(TABLE, WIDE, dtype=BF16), shaped(SIDE, TILE, LANES)],
+        [shaped(TOKENS, WIDE, dtype=BF16)] * STEPS + [shaped(SIDE, COLS, LANES)],
+        ids,
         start,
-        tables[0],
+        held,
         opposite,
         part,
     )
+    pairs.append(late)
     states = start
     for step in range(STEPS):
         parts = exchange(parts, CZY, SUM_GROUPS)
         error = kernel_call(
-            functools.partial(error_kernel, step), shaped(SIDE, TILE, LANES), parts, constants
+            functools.partial(error_kernel, step), shaped(SIDE, COLS, LANES), parts, targets
         )
         error = exchange(error, CZY, SUM_GROUPS)
         last = step == STEPS - 1
         body = functools.partial(step_kernel, step == 0, last)
-        operands = (place, error, *tables, start, states)
+        operands = (places, error, start, states, *[pair[step] for pair in pairs])
         if last:
             updates = kernel_call(body, shaped(SIDE, COLS, LANES), *operands)
         else:
             states, parts = kernel_call(
-                body, [shaped(SIDE, 3 * COLS, LANES), shaped(SIDE, TILE, LANES)], *operands
+                body,
+                [shaped(SIDE, 3 * COLS, LANES), shaped(SIDE, COLS, LANES)],
+                *operands,
+                *[pair[step + 1] for pair in pairs],
             )
 
     updates = exchange(updates, CZY, GATHER_GROUPS)

time: 241 us -> 243 us (level)
  Pallas kernels: 14.3 us -> 30.7 us
  blocking collectives: 164 us -> 155 us
  waiting for transfers between devices: 16.9 us -> 10.8 us
  other arithmetic: 5.46 us -> 0.11 us
  local copies, waits for them, and re-layouts: 6.69 us -> 12 us
    pallas_call x19 -> x18, Pallas kernels: 14.1 us -> 28.7 us  [kernel_call(): pl.pallas_call(body, in_specs=in_specs, out_shape=out_shapes, compiler_pa...]
    all_to_all x12, blocking collectives: 164 us -> 155 us  [exchange(): lax.all_to_all(blocks, axes, split_axis=0, concat_axis=0, tiled=True, axi...]
    unnamed x17 -> x53, local copies, waits for them, and re-layouts: 5.08 us -> 12 us
    ppermute x3, waiting for transfers between devices: 16.3 us -> 10.8 us  [on_device(): upward = lax.ppermute(upward, CZY, UP)]
  transfers between devices with their start and end apart: 8 -> 8, of which waited for: 4 -> 2; matrix products, arithmetic and copies ran while one was open for 4% -> 0% of each run, Pallas kernels for 2% -> 7%
where the time goes in v7:
time: 243 us; the launch traced here: 242 us
  blocking collectives  155 us (64%)
  starting transfers between devices  32.8 us (13%)
  Pallas kernels  30.7 us (13%)
  local copies, waits for them, and re-layouts  12 us (5%)
  waiting for transfers between devices  10.8 us (4%)
    all_to_all x12, blocking collectives, exchange(): lax.all_to_all(blocks, axes, split_axis=0, concat_axis=0, tiled=True, axi...  155 us
    pallas_call x18, Pallas kernels, kernel_call(): pl.pallas_call(body, in_specs=in_specs, out_shape=out_shapes, compiler_pa...  28.7 us
    ppermute x3, starting transfers between devices, on_device(): downward = lax.ppermute(downward, CZY, DOWN)  17.9 us
    unnamed x53, local copies, waits for them, and re-layouts  12 us
    ppermute x3, waiting for transfers between devices, on_device(): upward = lax.ppermute(upward, CZY, UP)  10.8 us
    ppermute x3, starting transfers between devices, on_device(): upward = lax.ppermute(upward, CZY, UP)  8.65 us
  transfers between devices with their start and end apart: 8, of which 2 were waited for; matrix products, arithmetic and copies ran while one was open for 0% of the time, Pallas kernels for 7%

profile of v7, /device:TPU:1, one launch (start us, length us, event | category | flops | bytes accessed | tf_op | source)
XLA Modules:
  0.0 242.1 jit_solution(12430565097295093985)
XLA Ops:
  2.1 4.8 %collective-permute-start = (f32[1536,128]{1,0:T(8,128)S(1)}, f32[1536,128]{1,0:T(8,128)}, u32[]{:S(2)}, u32[]{:S(2)}) collective-permute-start(f32[1536,128]{1,0:T(8,128)S(1)} %shard_map.84.first_ref), channel_id=1, source_target_pairs={{0,1},{1,2},{2,3},{3,4},{4,5},{5,6},{6,7},{7,0},{8,9},{9,10},{10,1... | collective-permute-start | bytes 2359304 | tf_op jit(solution)/shard_map/ppermute | solution.py:332
  7.0 8.6 %collective-permute-start.3 = (f32[1536,128]{1,0:T(8,128)S(1)}, f32[1536,128]{1,0:T(8,128)}, u32[]{:S(2)}, u32[]{:S(2)}) collective-permute-start(f32[1536,128]{1,0:T(8,128)S(1)} %shard_map.84.first_ref), channel_id=1, source_target_pairs={{0,7},{1,0},{2,1},{3,2},{4,3},{5,4},{6,5},{7,6},{8,15},{9,8},{10,9... | collective-permute-start | bytes 2359304 | tf_op jit(solution)/shard_map/ppermute | solution.py:333
  15.6 7.8 %collective-permute-done.second_ref = f32[1536,128]{1,0:T(8,128)} collective-permute-done((f32[1536,128]{1,0:T(8,128)S(1)}, f32[1536,128]{1,0:T(8,128)}, u32[]{:S(2)}, u32[]{:S(2)}) %collective-permute-start) | collective-permute-done | bytes 786464 | tf_op jit(solution)/shard_map/ppermute | solution.py:332
  25.6 4.7 %collective-permute-start.4 = (f32[1536,128]{1,0:T(8,128)}, f32[1536,128]{1,0:T(8,128)}, u32[]{:S(2)}, u32[]{:S(2)}) collective-permute-start(f32[1536,128]{1,0:T(8,128)} %collective-permute-done.3.first_ref), channel_id=1, source_target_pairs={{0,7},{1,0},{2,1},{3,2},{4,3},{5,4},{6,5},{7,6},{8,15},{9,8},{10,9... | collective-permute-start | bytes 2359304 | tf_op jit(solution)/shard_map/ppermute | solution.py:333
  30.4 4.6 %shard_map.85 = (bf16[1024,256]{1,0:T(8,128)(2,1)S(1)}, bf16[1024,256]{1,0:T(8,128)(2,1)S(1)}, bf16[1024,256]{1,0:T(8,128)(2,1)S(1)}, bf16[1024,256]{1,0:T(8,128)(2,1)S(1)}) custom-call(f32[1024,4]{1,0:T(8,128)S(1)} %convert_bitcast_fusion.ids_ref, f32[1536,128]{1,0:T(8,128)S(1)} %shard_map.84.first_ref, f32[1536,128]{1,0:T(8,128)} %collective-permute-done.second_ref), custom_call_target="tpu_custom_call" | custom-call | tf_op jit(solution)/shard_map/pallas_call | solution.py:63
  35.0 3.0 %collective-permute-done.1.second_ref = f32[1536,128]{1,0:T(8,128)} collective-permute-done((f32[1536,128]{1,0:T(8,128)}, f32[1536,128]{1,0:T(8,128)}, u32[]{:S(2)}, u32[]{:S(2)}) %collective-permute-start.1) | collective-permute-done | bytes 786464 | tf_op jit(solution)/shard_map/ppermute | solution.py:332
  40.9 4.2 %all-to-all-start = ((f32[8,144,128]{2,1,0:T(8,128)}), f32[8,144,128]{2,1,0:T(8,128)S(1)}, u32[]{:S(2)}, u32[]{:S(2)}) async-start(f32[8,144,128]{2,1,0:T(8,128)} %shard_map.82), calls=%async_computation | async-start | bytes 1179648 | tf_op jit(solution)/shard_map/all_to_all | solution.py:53
  45.1 4.8 %shard_map.86 = (bf16[1024,256]{1,0:T(8,128)(2,1)S(1)}, bf16[1024,256]{1,0:T(8,128)(2,1)S(1)}, bf16[1024,256]{1,0:T(8,128)(2,1)S(1)}, bf16[1024,256]{1,0:T(8,128)(2,1)S(1)}) custom-call(f32[1024,4]{1,0:T(8,128)S(1)} %convert_bitcast_fusion.ids_ref, f32[1536,128]{1,0:T(8,128)} %collective-permute-done.3.first_ref, f32[1536,128]{1,0:T(8,128)} %collective-permute-done.1.second_ref), custom_call_target="tpu_custom_call" | custom-call | tf_op jit(solution)/shard_map/pallas_call | solution.py:63
  52.3 4.6 %collective-permute-start.5 = (f32[1536,128]{1,0:T(8,128)}, f32[1536,128]{1,0:T(8,128)}, u32[]{:S(2)}, u32[]{:S(2)}) collective-permute-start(f32[1536,128]{1,0:T(8,128)} %collective-permute-done.4.first_ref), channel_id=1, source_target_pairs={{0,7},{1,0},{2,1},{3,2},{4,3},{5,4},{6,5},{7,6},{8,15},{9,8},{10,9... | collective-permute-start | bytes 2359304 | tf_op jit(solution)/shard_map/ppermute | solution.py:333
  56.9 2.1 collective-permute-start.6
  62.9 4.8 %shard_map.87 = (bf16[1024,256]{1,0:T(8,128)(2,1)S(1)}, bf16[1024,256]{1,0:T(8,128)(2,1)S(1)}, bf16[1024,256]{1,0:T(8,128)(2,1)S(1)}, bf16[1024,256]{1,0:T(8,128)(2,1)S(1)}) custom-call(f32[1024,4]{1,0:T(8,128)S(1)} %convert_bitcast_fusion.ids_ref, f32[1536,128]{1,0:T(8,128)} %collective-permute-done.4.first_ref, f32[1536,128]{1,0:T(8,128)} %collective-permute-done.2.second_ref), custom_call_target="tpu_custom_call" | custom-call | tf_op jit(solution)/shard_map/pallas_call | solution.py:63
  74.2 5.0 %shard_map.89 = (bf16[1024,256]{1,0:T(8,128)(2,1)S(1)}, bf16[1024,256]{1,0:T(8,128)(2,1)S(1)}, bf16[1024,256]{1,0:T(8,128)(2,1)S(1)}, bf16[1024,256]{1,0:T(8,128)(2,1)S(1)}, f32[8,48,128]{2,1,0:T(8,128)S(1)}) custom-call(f32[1024,4]{1,0:T(8,128)S(1)} %convert_bitcast_fusion.ids_ref, f32[8,144,128]{2,1,0:T(8,128)S(1)} %get-tuple-element.52.states_ref.w_ref, ...), custom_call_target="tpu_custom_call" | custom-call | tf_op jit(solution)/shard_map/pallas_call | solution.py:63
  79.2 15.4 %all_to_all.65.parts_ref = f32[8,48,128]{2,1,0:T(8,128)S(1)} all-to-all(f32[8,48,128]{2,1,0:T(8,128)S(1)} %get-tuple-element.55), channel_id=1, replica_groups={{0,8,16,24,32,40,48,56},{1,9,17,25,33,41,49,57},{2,10,18,26,34,42,50,58..., dimensions={0} | all-to-all | bytes 393216 | tf_op jit(solution)/shard_map/all_to_all | solution.py:53
  94.7 11.2 %all_to_all.66.error_ref = f32[8,48,128]{2,1,0:T(8,128)S(1)} all-to-all(f32[8,48,128]{2,1,0:T(8,128)S(1)} %shard_map.90), channel_id=1, replica_groups={{0,8,16,24,32,40,48,56},{1,9,17,25,33,41,49,57},{2,10,18,26,34,42,50,58..., dimensions={0} | all-to-all | bytes 393216 | tf_op jit(solution)/shard_map/all_to_all | solution.py:53
  107.5 11.0 %all_to_all.67.parts_ref = f32[8,48,128]{2,1,0:T(8,128)S(1)} all-to-all(f32[8,48,128]{2,1,0:T(8,128)S(1)} %get-tuple-element.61), channel_id=1, replica_groups={{0,8,16,24,32,40,48,56},{1,9,17,25,33,41,49,57},{2,10,18,26,34,42,50,58..., dimensions={0} | all-to-all | bytes 393216 | tf_op jit(solution)/shard_map/all_to_all | solution.py:53
  118.6 11.2 %all_to_all.68.error_ref = f32[8,48,128]{2,1,0:T(8,128)S(1)} all-to-all(f32[8,48,128]{2,1,0:T(8,128)S(1)} %shard_map.92), channel_id=1, replica_groups={{0,8,16,24,32,40,48,56},{1,9,17,25,33,41,49,57},{2,10,18,26,34,42,50,58..., dimensions={0} | all-to-all | bytes 393216 | tf_op jit(solution)/shard_map/all_to_all | solution.py:53
  131.4 11.2 %all_to_all.69.parts_ref = f32[8,48,128]{2,1,0:T(8,128)S(1)} all-to-all(f32[8,48,128]{2,1,0:T(8,128)S(1)} %get-tuple-element.67), channel_id=1, replica_groups={{0,8,16,24,32,40,48,56},{1,9,17,25,33,41,49,57},{2,10,18,26,34,42,50,58..., dimensions={0} | all-to-all | bytes 393216 | tf_op jit(solution)/shard_map/all_to_all | solution.py:53
  142.6 11.2 %all_to_all.70.error_ref = f32[8,48,128]{2,1,0:T(8,128)S(1)} all-to-all(f32[8,48,128]{2,1,0:T(8,128)S(1)} %shard_map.94), channel_id=1, replica_groups={{0,8,16,24,32,40,48,56},{1,9,17,25,33,41,49,57},{2,10,18,26,34,42,50,58..., dimensions={0} | all-to-all | bytes 393216 | tf_op jit(solution)/shard_map/all_to_all | solution.py:53
  155.4 11.0 %all_to_all.71.parts_ref = f32[8,48,128]{2,1,0:T(8,128)S(1)} all-to-all(f32[8,48,128]{2,1,0:T(8,128)S(1)} %get-tuple-element.73), channel_id=1, replica_groups={{0,8,16,24,32,40,48,56},{1,9,17,25,33,41,49,57},{2,10,18,26,34,42,50,58..., dimensions={0} | all-to-all | bytes 393216 | tf_op jit(solution)/shard_map/all_to_all | solution.py:53
  166.5 11.3 %all_to_all.72.error_ref = f32[8,48,128]{2,1,0:T(8,128)S(1)} all-to-all(f32[8,48,128]{2,1,0:T(8,128)S(1)} %shard_map.96), channel_id=1, replica_groups={{0,8,16,24,32,40,48,56},{1,9,17,25,33,41,49,57},{2,10,18,26,34,42,50,58..., dimensions={0} | all-to-all | bytes 393216 | tf_op jit(solution)/shard_map/all_to_all | solution.py:53
  178.9 13.8 %all_to_all.73.parts_ref = f32[8,48,128]{2,1,0:T(8,128)S(1)} all-to-all(f32[8,48,128]{2,1,0:T(8,128)S(1)} %shard_map.97), channel_id=1, replica_groups={{0,1,2,3,4,5,6,7},{8,9,10,11,12,13,14,15},{16,17,18,19,20,21,22,23},{24..., dimensions={0} | all-to-all | bytes 393216 | tf_op jit(solution)/shard_map/all_to_all | solution.py:53
  192.9 25.6 %all_to_all.74.updates_ref = f32[8,16,384]{2,1,0:T(8,128)S(1)} all-to-all(f32[8,16,384]{2,1,0:T(8,128)S(1)} %shard_map.98), channel_id=1, replica_groups=mesh['x'=4,'core'=2,'z'=8,'y'=8] {'x','core'}, dimensions={0} | all-to-all | bytes 393216 | tf_op jit(solution)/shard_map/all_to_all | solution.py:53
  218.7 7.9 %all_to_all.75.parts_ref = f32[8,1,128]{2,1,0:T(1,128)S(1)} all-to-all(f32[8,1,128]{2,1,0:T(1,128)S(1)} %shard_map.99), channel_id=1, replica_groups=mesh['x'=4,'core'=2,'z'=8,'y'=8] {'x','core'}, dimensions={0} | all-to-all | bytes 8192 | tf_op jit(solution)/shard_map/all_to_all | solution.py:53
  226.6 14.6 %all_to_all.76.parts_ref = f32[64,1,128]{2,1,0:T(1,128)S(1)} all-to-all(f32[64,1,128]{2,1,0:T(1,128)S(1)} %shard_map.100), channel_id=1, replica_groups=mesh['x'=4,'core'=2,'z'=8,'y'=8] {'z','y'}, dimensions={0} | all-to-all | bytes 65536 | tf_op jit(solution)/shard_map/all_to_all | solution.py:53
  (79 shorter events, 27.4 us)
Async XLA Ops:
  1.9 23.5 %copy-start.25 = (s32[1,4,1024]{2,1,0:T(4,128)S(1)}, s32[1,4,1024]{2,1,0:T(4,128)}, u32[]{:S(2)}) copy-start(s32[1,4,1024]{2,1,0:T(4,128)} %param.11) | copy-start | bytes 49156
  2.1 21.3 %collective-permute-start = (f32[1536,128]{1,0:T(8,128)S(1)}, f32[1536,128]{1,0:T(8,128)}, u32[]{:S(2)}, u32[]{:S(2)}) collective-permute-start(f32[1536,128]{1,0:T(8,128)S(1)} %shard_map.84.first_ref), channel_id=1, source_target_pairs={{0,1},{1,2},{2,3},{3,4},{4,5},{5,6},{6,7},{7,0},{8,9},{9,10},{10,1... | collective-permute-start | bytes 2359304 | tf_op jit(solution)/shard_map/ppermute | solution.py:332
  7.0 18.7 %collective-permute-start.3 = (f32[1536,128]{1,0:T(8,128)S(1)}, f32[1536,128]{1,0:T(8,128)}, u32[]{:S(2)}, u32[]{:S(2)}) collective-permute-start(f32[1536,128]{1,0:T(8,128)S(1)} %shard_map.84.first_ref), channel_id=1, source_target_pairs={{0,7},{1,0},{2,1},{3,2},{4,3},{5,4},{6,5},{7,6},{8,15},{9,8},{10,9... | collective-permute-start | bytes 2359304 | tf_op jit(solution)/shard_map/ppermute | solution.py:333
  23.4 14.5 %collective-permute-start.1 = (f32[1536,128]{1,0:T(8,128)}, f32[1536,128]{1,0:T(8,128)}, u32[]{:S(2)}, u32[]{:S(2)}) collective-permute-start(f32[1536,128]{1,0:T(8,128)} %collective-permute-done.second_ref), channel_id=1, source_target_pairs={{0,1},{1,2},{2,3},{3,4},{4,5},{5,6},{6,7},{7,0},{8,9},{9,10},{10,1... | collective-permute-start | bytes 2359304 | tf_op jit(solution)/shard_map/ppermute | solution.py:332
  25.6 14.3 %copy-start.22 = (bf16[128,384]{1,0:T(8,128)(2,1)S(1)}, bf16[128,384]{1,0:T(8,128)(2,1)}, u32[]{:S(2)}) copy-start(bf16[128,384]{1,0:T(8,128)(2,1)} %w_ref.1) | copy-start | bytes 294916
  25.6 14.3 %copy-start.23 = (bf16[1,128,384]{2,1,0:T(8,128)(2,1)S(1)}, bf16[1,128,384]{2,1,0:T(8,128)(2,1)}, u32[]{:S(2)}) copy-start(bf16[1,128,384]{2,1,0:T(8,128)(2,1)} %param.9) | copy-start | bytes 294916
  25.6 14.3 %copy-start.24 = (bf16[1,128,384]{2,1,0:T(8,128)(2,1)S(1)}, bf16[1,128,384]{2,1,0:T(8,128)(2,1)}, u32[]{:S(2)}) copy-start(bf16[1,128,384]{2,1,0:T(8,128)(2,1)} %param.10) | copy-start | bytes 294916
  25.6 26.7 %collective-permute-start.4 = (f32[1536,128]{1,0:T(8,128)}, f32[1536,128]{1,0:T(8,128)}, u32[]{:S(2)}, u32[]{:S(2)}) collective-permute-start(f32[1536,128]{1,0:T(8,128)} %collective-permute-done.3.first_ref), channel_id=1, source_target_pairs={{0,7},{1,0},{2,1},{3,2},{4,3},{5,4},{6,5},{7,6},{8,15},{9,8},{10,9... | collective-permute-start | bytes 2359304 | tf_op jit(solution)/shard_map/ppermute | solution.py:333
  35.0 5.9 %copy-start.12 = (bf16[1024,256]{1,0:T(8,128)(2,1)}, bf16[1024,256]{1,0:T(8,128)(2,1)S(1)}, u32[]{:S(2)}) copy-start(bf16[1024,256]{1,0:T(8,128)(2,1)S(1)} %get-tuple-element.69.refs_4_.refs_0_) | copy-start | bytes 1572868
  37.9 19.0 %collective-permute-start.2 = (f32[1536,128]{1,0:T(8,128)}, f32[1536,128]{1,0:T(8,128)}, u32[]{:S(2)}, u32[]{:S(2)}) collective-permute-start(f32[1536,128]{1,0:T(8,128)} %collective-permute-done.1.second_ref), channel_id=1, source_target_pairs={{0,1},{1,2},{2,3},{3,4},{4,5},{5,6},{6,7},{7,0},{8,9},{9,10},{10,1... | collective-permute-start | bytes 2359304 | tf_op jit(solution)/shard_map/ppermute | solution.py:332
  40.9 30.1 %all-to-all-start = ((f32[8,144,128]{2,1,0:T(8,128)}), f32[8,144,128]{2,1,0:T(8,128)S(1)}, u32[]{:S(2)}, u32[]{:S(2)}) async-start(f32[8,144,128]{2,1,0:T(8,128)} %shard_map.82), calls=%async_computation | async-start | bytes 1179648 | tf_op jit(solution)/shard_map/all_to_all | solution.py:53
  52.3 21.9 %collective-permute-start.5 = (f32[1536,128]{1,0:T(8,128)}, f32[1536,128]{1,0:T(8,128)}, u32[]{:S(2)}, u32[]{:S(2)}) collective-permute-start(f32[1536,128]{1,0:T(8,128)} %collective-permute-done.4.first_ref), channel_id=1, source_target_pairs={{0,7},{1,0},{2,1},{3,2},{4,3},{5,4},{6,5},{7,6},{8,15},{9,8},{10,9... | collective-permute-start | bytes 2359304 | tf_op jit(solution)/shard_map/ppermute | solution.py:333
  56.9 17.3 %collective-permute-start.6 = (f32[1536,128]{1,0:T(8,128)}, f32[1536,128]{1,0:T(8,128)}, u32[]{:S(2)}, u32[]{:S(2)}) collective-permute-start(f32[1536,128]{1,0:T(8,128)} %collective-permute-done.2.second_ref), channel_id=1, source_target_pairs={{0,1},{1,2},{2,3},{3,4},{4,5},{5,6},{6,7},{7,0},{8,9},{9,10},{10,1... | collective-permute-start | bytes 2359304 | tf_op jit(solution)/shard_map/ppermute | solution.py:337
  59.1 1.1 copy-start.18
  71.0 1.0 copy-start.3
  72.0 1.0 copy-start.10
  74.2 31.6 %copy-start.8 = (bf16[1024,256]{1,0:T(8,128)(2,1)S(1)}, bf16[1024,256]{1,0:T(8,128)(2,1)}, u32[]{:S(2)}) copy-start(bf16[1024,256]{1,0:T(8,128)(2,1)} %copy-done.7) | copy-start | bytes 1572868
  74.2 31.6 %copy-start.11 = (bf16[1024,256]{1,0:T(8,128)(2,1)S(1)}, bf16[1024,256]{1,0:T(8,128)(2,1)}, u32[]{:S(2)}) copy-start(bf16[1024,256]{1,0:T(8,128)(2,1)} %copy-done.9) | copy-start | bytes 1572868
  79.2 26.6 %copy-start.4 = (bf16[1024,256]{1,0:T(8,128)(2,1)S(1)}, bf16[1024,256]{1,0:T(8,128)(2,1)}, u32[]{:S(2)}) copy-start(bf16[1024,256]{1,0:T(8,128)(2,1)} %copy-done.2) | copy-start | bytes 1572868
  94.6 11.2 %copy-start.1 = (bf16[1024,256]{1,0:T(8,128)(2,1)S(1)}, bf16[1024,256]{1,0:T(8,128)(2,1)}, u32[]{:S(2)}) copy-start(bf16[1024,256]{1,0:T(8,128)(2,1)} %copy-done) | copy-start | bytes 1572868
  118.5 11.2 %copy-start.6 = (bf16[1024,256]{1,0:T(8,128)(2,1)S(1)}, bf16[1024,256]{1,0:T(8,128)(2,1)}, u32[]{:S(2)}) copy-start(bf16[1024,256]{1,0:T(8,128)(2,1)} %copy-done.5) | copy-start | bytes 1572868
  129.7 24.0 %copy-start.17 = (bf16[1024,256]{1,0:T(8,128)(2,1)S(1)}, bf16[1024,256]{1,0:T(8,128)(2,1)}, u32[]{:S(2)}) copy-start(bf16[1024,256]{1,0:T(8,128)(2,1)} %copy-done.16) | copy-start | bytes 1572868
  131.4 22.4 %copy-start.15 = (bf16[1024,256]{1,0:T(8,128)(2,1)S(1)}, bf16[1024,256]{1,0:T(8,128)(2,1)}, u32[]{:S(2)}) copy-start(bf16[1024,256]{1,0:T(8,128)(2,1)} %copy-done.14) | copy-start | bytes 1572868
  142.6 11.2 %copy-start.13 = (bf16[1024,256]{1,0:T(8,128)(2,1)S(1)}, bf16[1024,256]{1,0:T(8,128)(2,1)}, u32[]{:S(2)}) copy-start(bf16[1024,256]{1,0:T(8,128)(2,1)} %copy-done.12) | copy-start | bytes 1572868
  (10 other events, 8.5 us)

commit v8 on v7

--- a/solution.py
+++ b/solution.py
@@ -156,16 +156,35 @@
     return jnp.concatenate([first_ref[...], second_ref[...]], axis=1).astype(BF16)
 
 
-def rows_kernel(ids_ref, first_ref, second_ref, *outs):
+def rows_kernel(ids_ref, first_ref, second_ref, now_ref, *refs):
+    later, (held, left) = refs[: STEPS - 1], refs[STEPS - 1 :]
     pair = pair_of(first_ref, second_ref)
-    for step in range(STEPS):
-        choose(ids_ref, step, pair, outs[step])
+    copies = []
+    for step in range(1, STEPS):
+        choose(ids_ref, step, pair, held.at[step - 1])
+        copies.append(pltpu.make_async_copy(held.at[step - 1], later[step - 1], left.at[step - 1]))
+        copies[-1].start()
+    choose(ids_ref, 0, pair, now_ref)
+    for copy in copies:
+        copy.wait()
 
 
 def chosen_rows(ids, first, second):
-    return kernel_call(
-        rows_kernel, [shaped(TOKENS, WIDE, dtype=BF16)] * STEPS, ids, first, second
-    )
+    return pl.pallas_call(
+        rows_kernel,
+        in_specs=[pl.BlockSpec(memory_space=pltpu.VMEM)] * 3,
+        out_shape=[shaped(TOKENS, WIDE, dtype=BF16)] * STEPS,
+        out_specs=[pl.BlockSpec(memory_space=pltpu.VMEM)]
+        + [pl.BlockSpec(memory_space=pltpu.HBM)] * (STEPS - 1),
+        scratch_shapes=[
+            pltpu.VMEM((STEPS - 1, TOKENS, WIDE), BF16),
+            pltpu.SemaphoreType.DMA((STEPS - 1,)),
+        ],
+        cost_estimate=pl.CostEstimate(
+            flops=2 * STEPS * TOKENS * TABLE * WIDE, bytes_accessed=4 * MIB, transcendentals=0
+        ),
+        compiler_params=pltpu.CompilerParams(vmem_limit_bytes=54 * MIB),
+    )(ids, first, second)
 
 
 def early_kernel(place_ref, start_ref, target_ref, *refs):

time: 243 us -> 238 us (0.979)
  local copies, waits for them, and re-layouts: 12 us -> 3.2 us
  Pallas kernels: 30.7 us -> 33.7 us
    pallas_call x0 -> x3, Pallas kernels: none -> 17.5 us  [chosen_rows(): pl.pallas_call(rows_kernel, in_specs=[pl.BlockSpec(memory_space=pltpu.VME...]
    pallas_call x18 -> x15, Pallas kernels: 28.7 us -> 14.3 us  [kernel_call(): pl.pallas_call(body, in_specs=in_specs, out_shape=out_shapes, compiler_pa...]
    unnamed x53 -> x51, local copies, waits for them, and re-layouts: 12 us -> 3.2 us
    ppermute x1, waiting for transfers between devices: 0.01 us -> 2.53 us  [on_device(): opposite = lax.ppermute(upward, CZY, UP)]
  transfers between devices with their start and end apart: 8 -> 8, of which waited for: 2 -> 3; matrix products, arithmetic and copies ran while one was open for 0% -> 0% of each run, Pallas kernels for 7% -> 9%
where the time goes in v8:
time: 238 us; the launch traced here: 237 us
  blocking collectives  154 us (65%)
  Pallas kernels  33.7 us (14%)
  starting transfers between devices  32.9 us (14%)
  waiting for transfers between devices  11.3 us (5%)
  local copies, waits for them, and re-layouts  3.2 us (1%)
    all_to_all x12, blocking collectives, exchange(): lax.all_to_all(blocks, axes, split_axis=0, concat_axis=0, tiled=True, axi...  154 us
    ppermute x3, starting transfers between devices, on_device(): downward = lax.ppermute(downward, CZY, DOWN)  18 us
    pallas_call x3, Pallas kernels, chosen_rows(): pl.pallas_call(rows_kernel, in_specs=[pl.BlockSpec(memory_space=pltpu.VME...  17.5 us
    pallas_call x15, Pallas kernels, kernel_call(): pl.pallas_call(body, in_specs=in_specs, out_shape=out_shapes, compiler_pa...  14.3 us
    ppermute x3, waiting for transfers between devices, on_device(): upward = lax.ppermute(upward, CZY, UP)  8.79 us
    ppermute x3, starting transfers between devices, on_device(): upward = lax.ppermute(upward, CZY, UP)  8.65 us
  transfers between devices with their start and end apart: 8, of which 3 were waited for; matrix products, arithmetic and copies ran while one was open for 0% of the time, Pallas kernels for 9%

profile of v8, /device:TPU:1, one launch (start us, length us, event | category | flops | bytes accessed | tf_op | source)
XLA Modules:
  0.0 236.5 jit_solution(18211272097194518853)
XLA Ops:
  2.1 4.8 %collective-permute-start = (f32[1536,128]{1,0:T(8,128)S(1)}, f32[1536,128]{1,0:T(8,128)}, u32[]{:S(2)}, u32[]{:S(2)}) collective-permute-start(f32[1536,128]{1,0:T(8,128)S(1)} %shard_map.84.first_ref), channel_id=1, source_target_pairs={{0,1},{1,2},{2,3},{3,4},{4,5},{5,6},{6,7},{7,0},{8,9},{9,10},{10,1... | collective-permute-start | bytes 2359304 | tf_op jit(solution)/shard_map/ppermute | solution.py:351
  7.0 8.6 %collective-permute-start.3 = (f32[1536,128]{1,0:T(8,128)S(1)}, f32[1536,128]{1,0:T(8,128)S(1)}, u32[]{:S(2)}, u32[]{:S(2)}) collective-permute-start(f32[1536,128]{1,0:T(8,128)S(1)} %shard_map.84.first_ref), channel_id=1, source_target_pairs={{0,7},{1,0},{2,1},{3,2},{4,3},{5,4},{6,5},{7,6},{8,15},{9,8},{10,9... | collective-permute-start | bytes 2359304 | tf_op jit(solution)/shard_map/ppermute | solution.py:352
  15.6 7.8 %collective-permute-done.second_ref = f32[1536,128]{1,0:T(8,128)} collective-permute-done((f32[1536,128]{1,0:T(8,128)S(1)}, f32[1536,128]{1,0:T(8,128)}, u32[]{:S(2)}, u32[]{:S(2)}) %collective-permute-start) | collective-permute-done | bytes 786464 | tf_op jit(solution)/shard_map/ppermute | solution.py:351
  26.4 4.7 %collective-permute-start.4 = (f32[1536,128]{1,0:T(8,128)S(1)}, f32[1536,128]{1,0:T(8,128)}, u32[]{:S(2)}, u32[]{:S(2)}) collective-permute-start(f32[1536,128]{1,0:T(8,128)S(1)} %collective-permute-done.3.first_ref), channel_id=1, source_target_pairs={{0,7},{1,0},{2,1},{3,2},{4,3},{5,4},{6,5},{7,6},{8,15},{9,8},{10,9... | collective-permute-start | bytes 2359304 | tf_op jit(solution)/shard_map/ppermute | solution.py:352
  31.2 5.8 %shard_map.85 = (bf16[1024,256]{1,0:T(8,128)(2,1)}, bf16[1024,256]{1,0:T(8,128)(2,1)}, bf16[1024,256]{1,0:T(8,128)(2,1)}, bf16[1024,256]{1,0:T(8,128)(2,1)}) custom-call(f32[1024,4]{1,0:T(8,128)} %convert_bitcast_fusion.ids_ref, f32[1536,128]{1,0:T(8,128)} %copy-done.15, f32[1536,128]{1,0:T(8,128)} %collective-permute-done.second_ref), custom_call_target="tpu_custom_call" | custom-call | flops 3221225472 | bytes 4194304 | tf_op jit(solution)/shard_map/pallas_call | solution.py:173
  40.9 4.2 %all-to-all-start = ((f32[8,144,128]{2,1,0:T(8,128)}), f32[8,144,128]{2,1,0:T(8,128)S(1)}, u32[]{:S(2)}, u32[]{:S(2)}) async-start(f32[8,144,128]{2,1,0:T(8,128)} %shard_map.82), calls=%async_computation | async-start | bytes 1179648 | tf_op jit(solution)/shard_map/all_to_all | solution.py:53
  45.1 4.7 %collective-permute-start.5 = (f32[1536,128]{1,0:T(8,128)}, f32[1536,128]{1,0:T(8,128)S(1)}, u32[]{:S(2)}, u32[]{:S(2)}) collective-permute-start(f32[1536,128]{1,0:T(8,128)} %collective-permute-done.4.first_ref), channel_id=1, source_target_pairs={{0,7},{1,0},{2,1},{3,2},{4,3},{5,4},{6,5},{7,6},{8,15},{9,8},{10,9... | collective-permute-start | bytes 2359304 | tf_op jit(solution)/shard_map/ppermute | solution.py:352
  49.8 5.8 %shard_map.86 = (bf16[1024,256]{1,0:T(8,128)(2,1)}, bf16[1024,256]{1,0:T(8,128)(2,1)}, bf16[1024,256]{1,0:T(8,128)(2,1)}, bf16[1024,256]{1,0:T(8,128)(2,1)}) custom-call(f32[1024,4]{1,0:T(8,128)} %convert_bitcast_fusion.ids_ref, f32[1536,128]{1,0:T(8,128)} %copy-done.24, f32[1536,128]{1,0:T(8,128)} %collective-permute-done.1.second_ref), custom_call_target="tpu_custom_call" | custom-call | flops 3221225472 | bytes 4194304 | tf_op jit(solution)/shard_map/pallas_call | solution.py:173
  55.7 2.1 collective-permute-start.6
  59.6 5.9 %shard_map.87 = (bf16[1024,256]{1,0:T(8,128)(2,1)}, bf16[1024,256]{1,0:T(8,128)(2,1)}, bf16[1024,256]{1,0:T(8,128)(2,1)}, bf16[1024,256]{1,0:T(8,128)(2,1)}) custom-call(f32[1024,4]{1,0:T(8,128)} %convert_bitcast_fusion.ids_ref, f32[1536,128]{1,0:T(8,128)} %collective-permute-done.4.first_ref, f32[1536,128]{1,0:T(8,128)} %collective-permute-done.2.second_ref), custom_call_target="tpu_custom_call" | custom-call | flops 3221225472 | bytes 4194304 | tf_op jit(solution)/shard_map/pallas_call | solution.py:173
  67.7 2.5 %collective-permute-done.6.second_ref = f32[1536,128]{1,0:T(8,128)} collective-permute-done((f32[1536,128]{1,0:T(8,128)}, f32[1536,128]{1,0:T(8,128)}, u32[]{:S(2)}, u32[]{:S(2)}) %collective-permute-start.6) | collective-permute-done | bytes 786464 | tf_op jit(solution)/shard_map/ppermute | solution.py:356
  70.2 4.8 %shard_map.89 = (bf16[1024,256]{1,0:T(8,128)(2,1)S(1)}, bf16[1024,256]{1,0:T(8,128)(2,1)S(1)}, bf16[1024,256]{1,0:T(8,128)(2,1)S(1)}, bf16[1024,256]{1,0:T(8,128)(2,1)S(1)}, f32[8,48,128]{2,1,0:T(8,128)S(1)}) custom-call(f32[1024,4]{1,0:T(8,128)S(1)} %copy-done.1, f32[8,144,128]{2,1,0:T(8,128)S(1)} %get-tuple-element.52.states_ref.w_ref, ...), custom_call_target="tpu_custom_call" | custom-call | tf_op jit(solution)/shard_map/pallas_call | solution.py:63
  75.0 15.4 %all_to_all.65.parts_ref = f32[8,48,128]{2,1,0:T(8,128)S(1)} all-to-all(f32[8,48,128]{2,1,0:T(8,128)S(1)} %get-tuple-element.55), channel_id=1, replica_groups={{0,8,16,24,32,40,48,56},{1,9,17,25,33,41,49,57},{2,10,18,26,34,42,50,58..., dimensions={0} | all-to-all | bytes 393216 | tf_op jit(solution)/shard_map/all_to_all | solution.py:53
  90.4 11.2 %all_to_all.66.error_ref = f32[8,48,128]{2,1,0:T(8,128)S(1)} all-to-all(f32[8,48,128]{2,1,0:T(8,128)S(1)} %shard_map.90), channel_id=1, replica_groups={{0,8,16,24,32,40,48,56},{1,9,17,25,33,41,49,57},{2,10,18,26,34,42,50,58..., dimensions={0} | all-to-all | bytes 393216 | tf_op jit(solution)/shard_map/all_to_all | solution.py:53
  103.3 11.2 %all_to_all.67.parts_ref = f32[8,48,128]{2,1,0:T(8,128)S(1)} all-to-all(f32[8,48,128]{2,1,0:T(8,128)S(1)} %get-tuple-element.61), channel_id=1, replica_groups={{0,8,16,24,32,40,48,56},{1,9,17,25,33,41,49,57},{2,10,18,26,34,42,50,58..., dimensions={0} | all-to-all | bytes 393216 | tf_op jit(solution)/shard_map/all_to_all | solution.py:53
  114.5 11.2 %all_to_all.68.error_ref = f32[8,48,128]{2,1,0:T(8,128)S(1)} all-to-all(f32[8,48,128]{2,1,0:T(8,128)S(1)} %shard_map.92), channel_id=1, replica_groups={{0,8,16,24,32,40,48,56},{1,9,17,25,33,41,49,57},{2,10,18,26,34,42,50,58..., dimensions={0} | all-to-all | bytes 393216 | tf_op jit(solution)/shard_map/all_to_all | solution.py:53
  127.3 11.2 %all_to_all.69.parts_ref = f32[8,48,128]{2,1,0:T(8,128)S(1)} all-to-all(f32[8,48,128]{2,1,0:T(8,128)S(1)} %get-tuple-element.67), channel_id=1, replica_groups={{0,8,16,24,32,40,48,56},{1,9,17,25,33,41,49,57},{2,10,18,26,34,42,50,58..., dimensions={0} | all-to-all | bytes 393216 | tf_op jit(solution)/shard_map/all_to_all | solution.py:53
  138.5 11.2 %all_to_all.70.error_ref = f32[8,48,128]{2,1,0:T(8,128)S(1)} all-to-all(f32[8,48,128]{2,1,0:T(8,128)S(1)} %shard_map.94), channel_id=1, replica_groups={{0,8,16,24,32,40,48,56},{1,9,17,25,33,41,49,57},{2,10,18,26,34,42,50,58..., dimensions={0} | all-to-all | bytes 393216 | tf_op jit(solution)/shard_map/all_to_all | solution.py:53
  151.4 11.0 %all_to_all.71.parts_ref = f32[8,48,128]{2,1,0:T(8,128)S(1)} all-to-all(f32[8,48,128]{2,1,0:T(8,128)S(1)} %get-tuple-element.73), channel_id=1, replica_groups={{0,8,16,24,32,40,48,56},{1,9,17,25,33,41,49,57},{2,10,18,26,34,42,50,58..., dimensions={0} | all-to-all | bytes 393216 | tf_op jit(solution)/shard_map/all_to_all | solution.py:53
  162.4 11.0 %all_to_all.72.error_ref = f32[8,48,128]{2,1,0:T(8,128)S(1)} all-to-all(f32[8,48,128]{2,1,0:T(8,128)S(1)} %shard_map.96), channel_id=1, replica_groups={{0,8,16,24,32,40,48,56},{1,9,17,25,33,41,49,57},{2,10,18,26,34,42,50,58..., dimensions={0} | all-to-all | bytes 393216 | tf_op jit(solution)/shard_map/all_to_all | solution.py:53
  174.5 14.2 %all_to_all.73.parts_ref = f32[8,48,128]{2,1,0:T(8,128)S(1)} all-to-all(f32[8,48,128]{2,1,0:T(8,128)S(1)} %shard_map.97), channel_id=1, replica_groups={{0,1,2,3,4,5,6,7},{8,9,10,11,12,13,14,15},{16,17,18,19,20,21,22,23},{24..., dimensions={0} | all-to-all | bytes 393216 | tf_op jit(solution)/shard_map/all_to_all | solution.py:53
  188.8 24.1 %all_to_all.74.updates_ref = f32[8,16,384]{2,1,0:T(8,128)S(1)} all-to-all(f32[8,16,384]{2,1,0:T(8,128)S(1)} %shard_map.98), channel_id=1, replica_groups=mesh['x'=4,'core'=2,'z'=8,'y'=8] {'x','core'}, dimensions={0} | all-to-all | bytes 393216 | tf_op jit(solution)/shard_map/all_to_all | solution.py:53
  213.2 7.9 %all_to_all.75.parts_ref = f32[8,1,128]{2,1,0:T(1,128)S(1)} all-to-all(f32[8,1,128]{2,1,0:T(1,128)S(1)} %shard_map.99), channel_id=1, replica_groups=mesh['x'=4,'core'=2,'z'=8,'y'=8] {'x','core'}, dimensions={0} | all-to-all | bytes 8192 | tf_op jit(solution)/shard_map/all_to_all | solution.py:53
  221.1 14.6 %all_to_all.76.parts_ref = f32[64,1,128]{2,1,0:T(1,128)S(1)} all-to-all(f32[64,1,128]{2,1,0:T(1,128)S(1)} %shard_map.100), channel_id=1, replica_groups=mesh['x'=4,'core'=2,'z'=8,'y'=8] {'z','y'}, dimensions={0} | all-to-all | bytes 65536 | tf_op jit(solution)/shard_map/all_to_all | solution.py:53
  (77 shorter events, 20.3 us)
Async XLA Ops:
  1.9 23.5 %copy-start.23 = (s32[1,4,1024]{2,1,0:T(4,128)S(1)}, s32[1,4,1024]{2,1,0:T(4,128)}, u32[]{:S(2)}) copy-start(s32[1,4,1024]{2,1,0:T(4,128)} %param.11) | copy-start | bytes 49156
  2.1 24.3 %copy-start.15 = (f32[1536,128]{1,0:T(8,128)}, f32[1536,128]{1,0:T(8,128)S(1)}, u32[]{:S(2)}) copy-start(f32[1536,128]{1,0:T(8,128)S(1)} %shard_map.84.first_ref) | copy-start | bytes 2359300
  2.1 21.3 %collective-permute-start = (f32[1536,128]{1,0:T(8,128)S(1)}, f32[1536,128]{1,0:T(8,128)}, u32[]{:S(2)}, u32[]{:S(2)}) collective-permute-start(f32[1536,128]{1,0:T(8,128)S(1)} %shard_map.84.first_ref), channel_id=1, source_target_pairs={{0,1},{1,2},{2,3},{3,4},{4,5},{5,6},{6,7},{7,0},{8,9},{9,10},{10,1... | collective-permute-start | bytes 2359304 | tf_op jit(solution)/shard_map/ppermute | solution.py:351
  7.0 19.5 %collective-permute-start.3 = (f32[1536,128]{1,0:T(8,128)S(1)}, f32[1536,128]{1,0:T(8,128)S(1)}, u32[]{:S(2)}, u32[]{:S(2)}) collective-permute-start(f32[1536,128]{1,0:T(8,128)S(1)} %shard_map.84.first_ref), channel_id=1, source_target_pairs={{0,7},{1,0},{2,1},{3,2},{4,3},{5,4},{6,5},{7,6},{8,15},{9,8},{10,9... | collective-permute-start | bytes 2359304 | tf_op jit(solution)/shard_map/ppermute | solution.py:352
  23.4 14.5 %collective-permute-start.1 = (f32[1536,128]{1,0:T(8,128)}, f32[1536,128]{1,0:T(8,128)}, u32[]{:S(2)}, u32[]{:S(2)}) collective-permute-start(f32[1536,128]{1,0:T(8,128)} %collective-permute-done.second_ref), channel_id=1, source_target_pairs={{0,1},{1,2},{2,3},{3,4},{4,5},{5,6},{6,7},{7,0},{8,9},{9,10},{10,1... | collective-permute-start | bytes 2359304 | tf_op jit(solution)/shard_map/ppermute | solution.py:351
  26.4 13.5 %copy-start.20 = (bf16[128,384]{1,0:T(8,128)(2,1)S(1)}, bf16[128,384]{1,0:T(8,128)(2,1)}, u32[]{:S(2)}) copy-start(bf16[128,384]{1,0:T(8,128)(2,1)} %w_ref.1) | copy-start | bytes 294916
  26.4 13.5 %copy-start.21 = (bf16[1,128,384]{2,1,0:T(8,128)(2,1)S(1)}, bf16[1,128,384]{2,1,0:T(8,128)(2,1)}, u32[]{:S(2)}) copy-start(bf16[1,128,384]{2,1,0:T(8,128)(2,1)} %param.9) | copy-start | bytes 294916
  26.4 13.5 %copy-start.22 = (bf16[1,128,384]{2,1,0:T(8,128)(2,1)S(1)}, bf16[1,128,384]{2,1,0:T(8,128)(2,1)}, u32[]{:S(2)}) copy-start(bf16[1,128,384]{2,1,0:T(8,128)(2,1)} %param.10) | copy-start | bytes 294916
  26.4 18.7 %collective-permute-start.4 = (f32[1536,128]{1,0:T(8,128)S(1)}, f32[1536,128]{1,0:T(8,128)}, u32[]{:S(2)}, u32[]{:S(2)}) collective-permute-start(f32[1536,128]{1,0:T(8,128)S(1)} %collective-permute-done.3.first_ref), channel_id=1, source_target_pairs={{0,7},{1,0},{2,1},{3,2},{4,3},{5,4},{6,5},{7,6},{8,15},{9,8},{10,9... | collective-permute-start | bytes 2359304 | tf_op jit(solution)/shard_map/ppermute | solution.py:352
  37.9 17.7 %collective-permute-start.2 = (f32[1536,128]{1,0:T(8,128)}, f32[1536,128]{1,0:T(8,128)}, u32[]{:S(2)}, u32[]{:S(2)}) collective-permute-start(f32[1536,128]{1,0:T(8,128)} %collective-permute-done.1.second_ref), channel_id=1, source_target_pairs={{0,1},{1,2},{2,3},{3,4},{4,5},{5,6},{6,7},{7,0},{8,9},{9,10},{10,1... | collective-permute-start | bytes 2359304 | tf_op jit(solution)/shard_map/ppermute | solution.py:351
  40.9 24.6 %all-to-all-start = ((f32[8,144,128]{2,1,0:T(8,128)}), f32[8,144,128]{2,1,0:T(8,128)S(1)}, u32[]{:S(2)}, u32[]{:S(2)}) async-start(f32[8,144,128]{2,1,0:T(8,128)} %shard_map.82), calls=%async_computation | async-start | bytes 1179648 | tf_op jit(solution)/shard_map/all_to_all | solution.py:53
  45.1 12.8 %copy-start = (f32[1024,4]{1,0:T(8,128)S(1)}, f32[1024,4]{1,0:T(8,128)}, u32[]{:S(2)}) copy-start(f32[1024,4]{1,0:T(8,128)} %convert_bitcast_fusion.ids_ref) | copy-start | bytes 49156
  45.1 12.8 %copy-start.16 = (bf16[1024,384]{1,0:T(8,128)(2,1)S(1)}, bf16[1024,384]{1,0:T(8,128)(2,1)}, u32[]{:S(2)}) copy-start(bf16[1024,384]{1,0:T(8,128)(2,1)} %shared_ref.2) | copy-start | bytes 2359300
  45.1 12.8 %copy-start.17 = (bf16[1,512,384]{2,1,0:T(8,128)(2,1)S(1)}, bf16[1,512,384]{2,1,0:T(8,128)(2,1)}, u32[]{:S(2)}) copy-start(bf16[1,512,384]{2,1,0:T(8,128)(2,1)} %param.15) | copy-start | bytes 1179652
  45.1 22.6 %collective-permute-start.5 = (f32[1536,128]{1,0:T(8,128)}, f32[1536,128]{1,0:T(8,128)S(1)}, u32[]{:S(2)}, u32[]{:S(2)}) collective-permute-start(f32[1536,128]{1,0:T(8,128)} %collective-permute-done.4.first_ref), channel_id=1, source_target_pairs={{0,7},{1,0},{2,1},{3,2},{4,3},{5,4},{6,5},{7,6},{8,15},{9,8},{10,9... | collective-permute-start | bytes 2359304 | tf_op jit(solution)/shard_map/ppermute | solution.py:352
  55.7 14.6 %collective-permute-start.6 = (f32[1536,128]{1,0:T(8,128)}, f32[1536,128]{1,0:T(8,128)}, u32[]{:S(2)}, u32[]{:S(2)}) collective-permute-start(f32[1536,128]{1,0:T(8,128)} %collective-permute-done.2.second_ref), channel_id=1, source_target_pairs={{0,1},{1,2},{2,3},{3,4},{4,5},{5,6},{6,7},{7,0},{8,9},{9,10},{10,1... | collective-permute-start | bytes 2359304 | tf_op jit(solution)/shard_map/ppermute | solution.py:356
  70.2 31.4 %copy-start.9 = (bf16[1024,256]{1,0:T(8,128)(2,1)S(1)}, bf16[1024,256]{1,0:T(8,128)(2,1)}, u32[]{:S(2)}) copy-start(bf16[1024,256]{1,0:T(8,128)(2,1)} %get-tuple-element.59.refs_6_.refs_2_) | copy-start | bytes 1572868
  70.2 31.4 %copy-start.11 = (bf16[1024,256]{1,0:T(8,128)(2,1)S(1)}, bf16[1024,256]{1,0:T(8,128)(2,1)}, u32[]{:S(2)}) copy-start(bf16[1024,256]{1,0:T(8,128)(2,1)} %get-tuple-element.51.refs_2_) | copy-start | bytes 1572868
  75.0 26.6 %copy-start.6 = (bf16[1024,256]{1,0:T(8,128)(2,1)S(1)}, bf16[1024,256]{1,0:T(8,128)(2,1)}, u32[]{:S(2)}) copy-start(bf16[1024,256]{1,0:T(8,128)(2,1)} %get-tuple-element.58.refs_5_.refs_1_) | copy-start | bytes 1572868
  90.4 11.2 %copy-start.3 = (bf16[1024,256]{1,0:T(8,128)(2,1)S(1)}, bf16[1024,256]{1,0:T(8,128)(2,1)}, u32[]{:S(2)}) copy-start(bf16[1024,256]{1,0:T(8,128)(2,1)} %get-tuple-element.57.refs_4_.refs_0_) | copy-start | bytes 1572868
  101.6 24.0 %copy-start.8 = (bf16[1024,256]{1,0:T(8,128)(2,1)S(1)}, bf16[1024,256]{1,0:T(8,128)(2,1)}, u32[]{:S(2)}) copy-start(bf16[1024,256]{1,0:T(8,128)(2,1)} %get-tuple-element.65.refs_6_.refs_2_) | copy-start | bytes 1572868
  103.3 22.4 %copy-start.4 = (bf16[1024,256]{1,0:T(8,128)(2,1)S(1)}, bf16[1024,256]{1,0:T(8,128)(2,1)}, u32[]{:S(2)}) copy-start(bf16[1024,256]{1,0:T(8,128)(2,1)} %get-tuple-element.64.refs_5_.refs_1_) | copy-start | bytes 1572868
  125.7 24.0 %copy-start.14 = (bf16[1024,256]{1,0:T(8,128)(2,1)S(1)}, bf16[1024,256]{1,0:T(8,128)(2,1)}, u32[]{:S(2)}) copy-start(bf16[1024,256]{1,0:T(8,128)(2,1)} %get-tuple-element.71.refs_6_.refs_2_) | copy-start | bytes 1572868
  127.3 22.4 %copy-start.13 = (bf16[1024,256]{1,0:T(8,128)(2,1)S(1)}, bf16[1024,256]{1,0:T(8,128)(2,1)}, u32[]{:S(2)}) copy-start(bf16[1024,256]{1,0:T(8,128)(2,1)} %get-tuple-element.70.refs_5_.refs_1_) | copy-start | bytes 1572868
  (9 other events, 51.4 us)

commit v9 on v8

--- a/solution.py
+++ b/solution.py
@@ -199,16 +199,31 @@
         part_ref[:, tokens] = turned_product(weights, rows)
 
 
-def late_kernel(ids_ref, states_ref, first_ref, second_ref, part_ref, *outs):
-    out_ref = outs[STEPS]
-    pair = pair_of(first_ref, second_ref)
+def late_kernel(ids_ref, states_ref, first_ref, second_ref, part_ref, now_ref, out_ref):
+    choose(ids_ref, 0, pair_of(first_ref, second_ref), now_ref)
     weights = jnp.concatenate([states_ref[k, :COLS, :] for k in (6, 7)], axis=1).astype(BF16)
-    for step in range(STEPS):
-        choose(ids_ref, step, pair, outs[step])
     for token in range(0, TOKENS, WIDE):
         tokens = slice(token, token + WIDE)
-        output = part_ref[:, tokens] + turned_product(weights, outs[0][tokens, :])
+        output = part_ref[:, tokens] + turned_product(weights, now_ref[tokens, :])
         store_output(out_ref, token, output)
+
+
+def rest_kernel(ids_ref, first_ref, second_ref, *later):
+    pair = pair_of(first_ref, second_ref)
+    for step in range(1, STEPS):
+        choose(ids_ref, step, pair, later[step - 1])
+
+
+def rest_rows(ids, first, second):
+    return pl.pallas_call(
+        rest_kernel,
+        in_specs=[pl.BlockSpec(memory_space=pltpu.VMEM)] * 3,
+        out_shape=[shaped(TOKENS, WIDE, dtype=BF16)] * (STEPS - 1),
+        cost_estimate=pl.CostEstimate(
+            flops=2 * STEPS * TOKENS * TABLE * WIDE, bytes_accessed=4 * MIB, transcendentals=0
+        ),
+        compiler_params=pltpu.CompilerParams(vmem_limit_bytes=12 * MIB),
+    )(ids, first, second)
 
 
 def error_kernel(step, parts_ref, target_ref, out_ref):
@@ -367,16 +382,16 @@
         targets,
         *[pair[0] for pair in pairs],
     )
-    *late, parts = kernel_call(
+    now, parts = kernel_call(
         late_kernel,
-        [shaped(TOKENS, WIDE, dtype=BF16)] * STEPS + [shaped(SIDE, COLS, LANES)],
+        [shaped(TOKENS, WIDE, dtype=BF16), shaped(SIDE, COLS, LANES)],
         ids,
         start,
         held,
         opposite,
         part,
     )
-    pairs.append(late)
+    pairs.append([now, *rest_rows(ids, held, opposite)])
     states = start
     for step in range(STEPS):
         parts = exchange(parts, CZY, SUM_GROUPS)

time: 238 us -> 245 us (1.029)
  blocking collectives: 154 us -> 145 us
  local copies, waits for them, and re-layouts: 3.2 us -> 10.5 us
  starting transfers between devices: 32.9 us -> 36.9 us
  Pallas kernels: 33.7 us -> 36.8 us
    all_to_all x12 -> x11, blocking collectives: 154 us -> 145 us  [exchange(): lax.all_to_all(blocks, axes, split_axis=0, concat_axis=0, tiled=True, axi...]
    unnamed x51 -> x69, local copies, waits for them, and re-layouts: 3.2 us -> 10.5 us
    pallas_call x0 -> x1, Pallas kernels: none -> 4.1 us  [rest_rows(): pl.pallas_call(rest_kernel, in_specs=[pl.BlockSpec(memory_space=pltpu.VME...]
    all_to_all x1 -> x2, starting transfers between devices: 4.18 us -> 8.19 us  [exchange(): lax.all_to_all(blocks, axes, split_axis=0, concat_axis=0, tiled=True, axi...]
  transfers between devices with their start and end apart: 8 -> 9, of which waited for: 3 -> 4; matrix products, arithmetic and copies ran while one was open for 0% -> 0% of each run, Pallas kernels for 9% -> 10%
where the time goes in v9:
time: 245 us; the launch traced here: 243 us
  blocking collectives  145 us (59%)
  starting transfers between devices  36.9 us (15%)
  Pallas kernels  36.8 us (15%)
  waiting for transfers between devices  13.1 us (5%)
  local copies, waits for them, and re-layouts  10.5 us (4%)
    all_to_all x11, blocking collectives, exchange(): lax.all_to_all(blocks, axes, split_axis=0, concat_axis=0, tiled=True, axi...  145 us
    ppermute x3, starting transfers between devices, on_device(): downward = lax.ppermute(downward, CZY, DOWN)  18 us
    pallas_call x3, Pallas kernels, chosen_rows(): pl.pallas_call(rows_kernel, in_specs=[pl.BlockSpec(memory_space=pltpu.VME...  17.6 us
    pallas_call x15, Pallas kernels, kernel_call(): pl.pallas_call(body, in_specs=in_specs, out_shape=out_shapes, compiler_pa...  13.2 us
    unnamed x69, local copies, waits for them, and re-layouts  10.5 us
    ppermute x3, starting transfers between devices, on_device(): upward = lax.ppermute(upward, CZY, UP)  8.65 us
    ppermute x3, waiting for transfers between devices, on_device(): upward = lax.ppermute(upward, CZY, UP)  8.48 us
    all_to_all x2, starting transfers between devices, exchange(): lax.all_to_all(blocks, axes, split_axis=0, concat_axis=0, tiled=True, axi...  8.19 us
  transfers between devices with their start and end apart: 9, of which 4 were waited for; matrix products, arithmetic and copies ran while one was open for 0% of the time, Pallas kernels for 10%

profile of v9, /device:TPU:1, one launch (start us, length us, event | category | flops | bytes accessed | tf_op | source)
XLA Modules:
  0.0 243.2 jit_solution(10637549489621289816)
XLA Ops:
  2.1 4.8 %collective-permute-start = (f32[1536,128]{1,0:T(8,128)S(1)}, f32[1536,128]{1,0:T(8,128)S(1)}, u32[]{:S(2)}, u32[]{:S(2)}) collective-permute-start(f32[1536,128]{1,0:T(8,128)S(1)} %shard_map.84.first_ref), channel_id=1, source_target_pairs={{0,1},{1,2},{2,3},{3,4},{4,5},{5,6},{6,7},{7,0},{8,9},{9,10},{10,1... | collective-permute-start | bytes 2359304 | tf_op jit(solution)/shard_map/ppermute | solution.py:366
  7.0 8.6 %collective-permute-start.3 = (f32[1536,128]{1,0:T(8,128)S(1)}, f32[1536,128]{1,0:T(8,128)S(1)}, u32[]{:S(2)}, u32[]{:S(2)}) collective-permute-start(f32[1536,128]{1,0:T(8,128)S(1)} %shard_map.84.first_ref), channel_id=1, source_target_pairs={{0,7},{1,0},{2,1},{3,2},{4,3},{5,4},{6,5},{7,6},{8,15},{9,8},{10,9... | collective-permute-start | bytes 2359304 | tf_op jit(solution)/shard_map/ppermute | solution.py:367
  15.6 7.7 %collective-permute-done.second_ref = f32[1536,128]{1,0:T(8,128)S(1)} collective-permute-done((f32[1536,128]{1,0:T(8,128)S(1)}, f32[1536,128]{1,0:T(8,128)S(1)}, u32[]{:S(2)}, u32[]{:S(2)}) %collective-permute-start) | collective-permute-done | bytes 786464 | tf_op jit(solution)/shard_map/ppermute | solution.py:366
  26.3 4.7 %collective-permute-start.4 = (f32[1536,128]{1,0:T(8,128)S(1)}, f32[1536,128]{1,0:T(8,128)}, u32[]{:S(2)}, u32[]{:S(2)}) collective-permute-start(f32[1536,128]{1,0:T(8,128)S(1)} %collective-permute-done.3.first_ref), channel_id=1, source_target_pairs={{0,7},{1,0},{2,1},{3,2},{4,3},{5,4},{6,5},{7,6},{8,15},{9,8},{10,9... | collective-permute-start | bytes 2359304 | tf_op jit(solution)/shard_map/ppermute | solution.py:367
  31.0 5.8 %shard_map.85 = (bf16[1024,256]{1,0:T(8,128)(2,1)}, bf16[1024,256]{1,0:T(8,128)(2,1)}, bf16[1024,256]{1,0:T(8,128)(2,1)}, bf16[1024,256]{1,0:T(8,128)(2,1)}) custom-call(f32[1024,4]{1,0:T(8,128)} %convert_bitcast_fusion.ids_ref, f32[1536,128]{1,0:T(8,128)} %copy-done.21, f32[1536,128]{1,0:T(8,128)} %copy-done.33), custom_call_target="tpu_custom_call" | custom-call | flops 3221225472 | bytes 4194304 | tf_op jit(solution)/shard_map/pallas_call | solution.py:173
  40.6 4.2 %all-to-all-start = ((f32[8,144,128]{2,1,0:T(8,128)}), f32[8,144,128]{2,1,0:T(8,128)S(1)}, u32[]{:S(2)}, u32[]{:S(2)}) async-start(f32[8,144,128]{2,1,0:T(8,128)} %shard_map.82), calls=%async_computation | async-start | bytes 1179648 | tf_op jit(solution)/shard_map/all_to_all | solution.py:53
  44.8 4.7 %collective-permute-start.5 = (f32[1536,128]{1,0:T(8,128)}, f32[1536,128]{1,0:T(8,128)}, u32[]{:S(2)}, u32[]{:S(2)}) collective-permute-start(f32[1536,128]{1,0:T(8,128)} %collective-permute-done.4.first_ref), channel_id=1, source_target_pairs={{0,7},{1,0},{2,1},{3,2},{4,3},{5,4},{6,5},{7,6},{8,15},{9,8},{10,9... | collective-permute-start | bytes 2359304 | tf_op jit(solution)/shard_map/ppermute | solution.py:367
  49.5 5.8 %shard_map.86 = (bf16[1024,256]{1,0:T(8,128)(2,1)}, bf16[1024,256]{1,0:T(8,128)(2,1)}, bf16[1024,256]{1,0:T(8,128)(2,1)}, bf16[1024,256]{1,0:T(8,128)(2,1)}) custom-call(f32[1024,4]{1,0:T(8,128)} %convert_bitcast_fusion.ids_ref, f32[1536,128]{1,0:T(8,128)} %copy-done.32, f32[1536,128]{1,0:T(8,128)} %collective-permute-done.1.second_ref), custom_call_target="tpu_custom_call" | custom-call | flops 3221225472 | bytes 4194304 | tf_op jit(solution)/shard_map/pallas_call | solution.py:173
  59.3 5.9 %shard_map.87 = (bf16[1024,256]{1,0:T(8,128)(2,1)}, bf16[1024,256]{1,0:T(8,128)(2,1)}, bf16[1024,256]{1,0:T(8,128)(2,1)}, bf16[1024,256]{1,0:T(8,128)(2,1)}) custom-call(f32[1024,4]{1,0:T(8,128)} %convert_bitcast_fusion.ids_ref, f32[1536,128]{1,0:T(8,128)} %collective-permute-done.4.first_ref, f32[1536,128]{1,0:T(8,128)} %collective-permute-done.2.second_ref), custom_call_target="tpu_custom_call" | custom-call | flops 3221225472 | bytes 4194304 | tf_op jit(solution)/shard_map/pallas_call | solution.py:173
  67.4 2.5 %collective-permute-done.6.second_ref = f32[1536,128]{1,0:T(8,128)} collective-permute-done((f32[1536,128]{1,0:T(8,128)}, f32[1536,128]{1,0:T(8,128)}, u32[]{:S(2)}, u32[]{:S(2)}) %collective-permute-start.6) | collective-permute-done | bytes 786464 | tf_op jit(solution)/shard_map/ppermute | solution.py:371
  69.9 2.5 %shard_map.89 = (bf16[1024,256]{1,0:T(8,128)(2,1)S(1)}, f32[8,48,128]{2,1,0:T(8,128)S(1)}) custom-call(f32[1024,4]{1,0:T(8,128)S(1)} %copy-done.1, f32[8,144,128]{2,1,0:T(8,128)S(1)} %get-tuple-element.52.states_ref.w_ref, f32[1536,128]{1,0:T(8,128)} %collective-permute-done.5.first_ref, f32[1536,128]{1,0:T(8,128)} %collective-permute-done.6.second_ref, ...), custom_call_target="tpu_custom_call" | custom-call | tf_op jit(solution)/shard_map/pallas_call | solution.py:63
  73.2 15.2 %all_to_all.65.parts_ref = f32[8,48,128]{2,1,0:T(8,128)S(1)} all-to-all(f32[8,48,128]{2,1,0:T(8,128)S(1)} %get-tuple-element.55), channel_id=1, replica_groups={{0,8,16,24,32,40,48,56},{1,9,17,25,33,41,49,57},{2,10,18,26,34,42,50,58..., dimensions={0} | all-to-all | bytes 393216 | tf_op jit(solution)/shard_map/all_to_all | solution.py:53
  89.2 4.0 %all-to-all-start.2 = ((f32[8,48,128]{2,1,0:T(8,128)}), f32[8,48,128]{2,1,0:T(8,128)}, u32[]{:S(2)}, u32[]{:S(2)}) async-start(f32[8,48,128]{2,1,0:T(8,128)} %shard_map.90), calls=%async_computation.2 | async-start | bytes 393216 | tf_op jit(solution)/shard_map/all_to_all | solution.py:53
  93.2 4.1 %shard_map.91 = (bf16[1024,256]{1,0:T(8,128)(2,1)S(1)}, bf16[1024,256]{1,0:T(8,128)(2,1)S(1)}, bf16[1024,256]{1,0:T(8,128)(2,1)S(1)}) custom-call(f32[1024,4]{1,0:T(8,128)S(1)} %copy-done.1, f32[1536,128]{1,0:T(8,128)} %collective-permute-done.5.first_ref, f32[1536,128]{1,0:T(8,128)} %collective-permute-done.6.second_ref), custom_call_target="tpu_custom_call" | custom-call | flops 3221225472 | bytes 4194304 | tf_op jit(solution)/shard_map/pallas_call | solution.py:218
  108.1 13.0 %all_to_all.66.parts_ref = f32[8,48,128]{2,1,0:T(8,128)S(1)} all-to-all(f32[8,48,128]{2,1,0:T(8,128)S(1)} %get-tuple-element.61), channel_id=1, replica_groups={{0,8,16,24,32,40,48,56},{1,9,17,25,33,41,49,57},{2,10,18,26,34,42,50,58..., dimensions={0} | all-to-all | bytes 393216 | tf_op jit(solution)/shard_map/all_to_all | solution.py:53
  121.2 11.2 %all_to_all.67.error_ref = f32[8,48,128]{2,1,0:T(8,128)S(1)} all-to-all(f32[8,48,128]{2,1,0:T(8,128)S(1)} %shard_map.93), channel_id=1, replica_groups={{0,8,16,24,32,40,48,56},{1,9,17,25,33,41,49,57},{2,10,18,26,34,42,50,58..., dimensions={0} | all-to-all | bytes 393216 | tf_op jit(solution)/shard_map/all_to_all | solution.py:53
  134.0 11.2 %all_to_all.68.parts_ref = f32[8,48,128]{2,1,0:T(8,128)S(1)} all-to-all(f32[8,48,128]{2,1,0:T(8,128)S(1)} %get-tuple-element.67), channel_id=1, replica_groups={{0,8,16,24,32,40,48,56},{1,9,17,25,33,41,49,57},{2,10,18,26,34,42,50,58..., dimensions={0} | all-to-all | bytes 393216 | tf_op jit(solution)/shard_map/all_to_all | solution.py:53
  145.2 11.2 %all_to_all.69.error_ref = f32[8,48,128]{2,1,0:T(8,128)S(1)} all-to-all(f32[8,48,128]{2,1,0:T(8,128)S(1)} %shard_map.95), channel_id=1, replica_groups={{0,8,16,24,32,40,48,56},{1,9,17,25,33,41,49,57},{2,10,18,26,34,42,50,58..., dimensions={0} | all-to-all | bytes 393216 | tf_op jit(solution)/shard_map/all_to_all | solution.py:53
  158.1 11.0 %all_to_all.70.parts_ref = f32[8,48,128]{2,1,0:T(8,128)S(1)} all-to-all(f32[8,48,128]{2,1,0:T(8,128)S(1)} %get-tuple-element.73), channel_id=1, replica_groups={{0,8,16,24,32,40,48,56},{1,9,17,25,33,41,49,57},{2,10,18,26,34,42,50,58..., dimensions={0} | all-to-all | bytes 393216 | tf_op jit(solution)/shard_map/all_to_all | solution.py:53
  169.1 11.3 %all_to_all.71.error_ref = f32[8,48,128]{2,1,0:T(8,128)S(1)} all-to-all(f32[8,48,128]{2,1,0:T(8,128)S(1)} %shard_map.97), channel_id=1, replica_groups={{0,8,16,24,32,40,48,56},{1,9,17,25,33,41,49,57},{2,10,18,26,34,42,50,58..., dimensions={0} | all-to-all | bytes 393216 | tf_op jit(solution)/shard_map/all_to_all | solution.py:53
  181.5 13.3 %all_to_all.72.parts_ref = f32[8,48,128]{2,1,0:T(8,128)S(1)} all-to-all(f32[8,48,128]{2,1,0:T(8,128)S(1)} %shard_map.98), channel_id=1, replica_groups={{0,1,2,3,4,5,6,7},{8,9,10,11,12,13,14,15},{16,17,18,19,20,21,22,23},{24..., dimensions={0} | all-to-all | bytes 393216 | tf_op jit(solution)/shard_map/all_to_all | solution.py:53
  195.0 24.7 %all_to_all.73.updates_ref = f32[8,16,384]{2,1,0:T(8,128)S(1)} all-to-all(f32[8,16,384]{2,1,0:T(8,128)S(1)} %shard_map.99), channel_id=1, replica_groups=mesh['x'=4,'core'=2,'z'=8,'y'=8] {'x','core'}, dimensions={0} | all-to-all | bytes 393216 | tf_op jit(solution)/shard_map/all_to_all | solution.py:53
  219.9 7.9 %all_to_all.74.parts_ref = f32[8,1,128]{2,1,0:T(1,128)S(1)} all-to-all(f32[8,1,128]{2,1,0:T(1,128)S(1)} %shard_map.100), channel_id=1, replica_groups=mesh['x'=4,'core'=2,'z'=8,'y'=8] {'x','core'}, dimensions={0} | all-to-all | bytes 8192 | tf_op jit(solution)/shard_map/all_to_all | solution.py:53
  227.8 14.6 %all_to_all.75.parts_ref = f32[64,1,128]{2,1,0:T(1,128)S(1)} all-to-all(f32[64,1,128]{2,1,0:T(1,128)S(1)} %shard_map.101), channel_id=1, replica_groups=mesh['x'=4,'core'=2,'z'=8,'y'=8] {'z','y'}, dimensions={0} | all-to-all | bytes 65536 | tf_op jit(solution)/shard_map/all_to_all | solution.py:53
  (97 shorter events, 32.8 us)
Async XLA Ops:
  1.9 23.4 %copy-start.31 = (s32[1,4,1024]{2,1,0:T(4,128)S(1)}, s32[1,4,1024]{2,1,0:T(4,128)}, u32[]{:S(2)}) copy-start(s32[1,4,1024]{2,1,0:T(4,128)} %param.11) | copy-start | bytes 49156
  2.1 24.2 %copy-start.21 = (f32[1536,128]{1,0:T(8,128)}, f32[1536,128]{1,0:T(8,128)S(1)}, u32[]{:S(2)}) copy-start(f32[1536,128]{1,0:T(8,128)S(1)} %shard_map.84.first_ref) | copy-start | bytes 2359300
  2.1 21.2 %collective-permute-start = (f32[1536,128]{1,0:T(8,128)S(1)}, f32[1536,128]{1,0:T(8,128)S(1)}, u32[]{:S(2)}, u32[]{:S(2)}) collective-permute-start(f32[1536,128]{1,0:T(8,128)S(1)} %shard_map.84.first_ref), channel_id=1, source_target_pairs={{0,1},{1,2},{2,3},{3,4},{4,5},{5,6},{6,7},{7,0},{8,9},{9,10},{10,1... | collective-permute-start | bytes 2359304 | tf_op jit(solution)/shard_map/ppermute | solution.py:366
  7.0 19.3 %collective-permute-start.3 = (f32[1536,128]{1,0:T(8,128)S(1)}, f32[1536,128]{1,0:T(8,128)S(1)}, u32[]{:S(2)}, u32[]{:S(2)}) collective-permute-start(f32[1536,128]{1,0:T(8,128)S(1)} %shard_map.84.first_ref), channel_id=1, source_target_pairs={{0,7},{1,0},{2,1},{3,2},{4,3},{5,4},{6,5},{7,6},{8,15},{9,8},{10,9... | collective-permute-start | bytes 2359304 | tf_op jit(solution)/shard_map/ppermute | solution.py:367
  23.3 14.3 %collective-permute-start.1 = (f32[1536,128]{1,0:T(8,128)S(1)}, f32[1536,128]{1,0:T(8,128)}, u32[]{:S(2)}, u32[]{:S(2)}) collective-permute-start(f32[1536,128]{1,0:T(8,128)S(1)} %collective-permute-done.second_ref), channel_id=1, source_target_pairs={{0,1},{1,2},{2,3},{3,4},{4,5},{5,6},{6,7},{7,0},{8,9},{9,10},{10,1... | collective-permute-start | bytes 2359304 | tf_op jit(solution)/shard_map/ppermute | solution.py:366
  26.3 13.3 %copy-start.28 = (bf16[128,384]{1,0:T(8,128)(2,1)S(1)}, bf16[128,384]{1,0:T(8,128)(2,1)}, u32[]{:S(2)}) copy-start(bf16[128,384]{1,0:T(8,128)(2,1)} %w_ref.1) | copy-start | bytes 294916
  26.3 13.3 %copy-start.29 = (bf16[1,128,384]{2,1,0:T(8,128)(2,1)S(1)}, bf16[1,128,384]{2,1,0:T(8,128)(2,1)}, u32[]{:S(2)}) copy-start(bf16[1,128,384]{2,1,0:T(8,128)(2,1)} %param.9) | copy-start | bytes 294916
  26.3 13.3 %copy-start.30 = (bf16[1,128,384]{2,1,0:T(8,128)(2,1)S(1)}, bf16[1,128,384]{2,1,0:T(8,128)(2,1)}, u32[]{:S(2)}) copy-start(bf16[1,128,384]{2,1,0:T(8,128)(2,1)} %param.10) | copy-start | bytes 294916
  26.3 18.5 %collective-permute-start.4 = (f32[1536,128]{1,0:T(8,128)S(1)}, f32[1536,128]{1,0:T(8,128)}, u32[]{:S(2)}, u32[]{:S(2)}) collective-permute-start(f32[1536,128]{1,0:T(8,128)S(1)} %collective-permute-done.3.first_ref), channel_id=1, source_target_pairs={{0,7},{1,0},{2,1},{3,2},{4,3},{5,4},{6,5},{7,6},{8,15},{9,8},{10,9... | collective-permute-start | bytes 2359304 | tf_op jit(solution)/shard_map/ppermute | solution.py:367
  37.6 17.7 %collective-permute-start.2 = (f32[1536,128]{1,0:T(8,128)}, f32[1536,128]{1,0:T(8,128)}, u32[]{:S(2)}, u32[]{:S(2)}) collective-permute-start(f32[1536,128]{1,0:T(8,128)} %collective-permute-done.1.second_ref), channel_id=1, source_target_pairs={{0,1},{1,2},{2,3},{3,4},{4,5},{5,6},{6,7},{7,0},{8,9},{9,10},{10,1... | collective-permute-start | bytes 2359304 | tf_op jit(solution)/shard_map/ppermute | solution.py:366
  40.6 24.6 %all-to-all-start = ((f32[8,144,128]{2,1,0:T(8,128)}), f32[8,144,128]{2,1,0:T(8,128)S(1)}, u32[]{:S(2)}, u32[]{:S(2)}) async-start(f32[8,144,128]{2,1,0:T(8,128)} %shard_map.82), calls=%async_computation | async-start | bytes 1179648 | tf_op jit(solution)/shard_map/all_to_all | solution.py:53
  44.8 12.8 %copy-start = (f32[1024,4]{1,0:T(8,128)S(1)}, f32[1024,4]{1,0:T(8,128)}, u32[]{:S(2)}) copy-start(f32[1024,4]{1,0:T(8,128)} %convert_bitcast_fusion.ids_ref) | copy-start | bytes 49156
  44.8 12.8 %copy-start.22 = (bf16[1024,384]{1,0:T(8,128)(2,1)S(1)}, bf16[1024,384]{1,0:T(8,128)(2,1)}, u32[]{:S(2)}) copy-start(bf16[1024,384]{1,0:T(8,128)(2,1)} %shared_ref.2) | copy-start | bytes 2359300
  44.8 12.8 %copy-start.25 = (bf16[1,512,384]{2,1,0:T(8,128)(2,1)S(1)}, bf16[1,512,384]{2,1,0:T(8,128)(2,1)}, u32[]{:S(2)}) copy-start(bf16[1,512,384]{2,1,0:T(8,128)(2,1)} %param.15) | copy-start | bytes 1179652
  44.8 22.6 %collective-permute-start.5 = (f32[1536,128]{1,0:T(8,128)}, f32[1536,128]{1,0:T(8,128)}, u32[]{:S(2)}, u32[]{:S(2)}) collective-permute-start(f32[1536,128]{1,0:T(8,128)} %collective-permute-done.4.first_ref), channel_id=1, source_target_pairs={{0,7},{1,0},{2,1},{3,2},{4,3},{5,4},{6,5},{7,6},{8,15},{9,8},{10,9... | collective-permute-start | bytes 2359304 | tf_op jit(solution)/shard_map/ppermute | solution.py:367
  55.4 14.6 %collective-permute-start.6 = (f32[1536,128]{1,0:T(8,128)}, f32[1536,128]{1,0:T(8,128)}, u32[]{:S(2)}, u32[]{:S(2)}) collective-permute-start(f32[1536,128]{1,0:T(8,128)} %collective-permute-done.2.second_ref), channel_id=1, source_target_pairs={{0,1},{1,2},{2,3},{3,4},{4,5},{5,6},{6,7},{7,0},{8,9},{9,10},{10,1... | collective-permute-start | bytes 2359304 | tf_op jit(solution)/shard_map/ppermute | solution.py:371
  89.2 12.6 %all-to-all-start.2 = ((f32[8,48,128]{2,1,0:T(8,128)}), f32[8,48,128]{2,1,0:T(8,128)}, u32[]{:S(2)}, u32[]{:S(2)}) async-start(f32[8,48,128]{2,1,0:T(8,128)} %shard_map.90), calls=%async_computation.2 | async-start | bytes 393216 | tf_op jit(solution)/shard_map/all_to_all | solution.py:53
  106.0 26.3 %copy-start.8 = (bf16[1024,256]{1,0:T(8,128)(2,1)S(1)}, bf16[1024,256]{1,0:T(8,128)(2,1)}, u32[]{:S(2)}) copy-start(bf16[1024,256]{1,0:T(8,128)(2,1)} %get-tuple-element.65.refs_6_.refs_2_) | copy-start | bytes 1572868
  106.0 26.3 %copy-start.13 = (bf16[1024,256]{1,0:T(8,128)(2,1)S(1)}, bf16[1024,256]{1,0:T(8,128)(2,1)}, u32[]{:S(2)}) copy-start(bf16[1024,256]{1,0:T(8,128)(2,1)} %copy-done.12) | copy-start | bytes 1572868
  108.1 24.2 %copy-start.4 = (bf16[1024,256]{1,0:T(8,128)(2,1)S(1)}, bf16[1024,256]{1,0:T(8,128)(2,1)}, u32[]{:S(2)}) copy-start(bf16[1024,256]{1,0:T(8,128)(2,1)} %get-tuple-element.64.refs_5_.refs_1_) | copy-start | bytes 1572868
  121.1 11.2 %copy-start.2 = (bf16[1024,256]{1,0:T(8,128)(2,1)S(1)}, bf16[1024,256]{1,0:T(8,128)(2,1)}, u32[]{:S(2)}) copy-start(bf16[1024,256]{1,0:T(8,128)(2,1)} %get-tuple-element.63.refs_4_.refs_0_) | copy-start | bytes 1572868
  132.3 24.0 %copy-start.18 = (bf16[1024,256]{1,0:T(8,128)(2,1)S(1)}, bf16[1024,256]{1,0:T(8,128)(2,1)}, u32[]{:S(2)}) copy-start(bf16[1024,256]{1,0:T(8,128)(2,1)} %get-tuple-element.71.refs_6_.refs_2_) | copy-start | bytes 1572868
  132.3 24.0 %copy-start.20 = (bf16[1024,256]{1,0:T(8,128)(2,1)S(1)}, bf16[1024,256]{1,0:T(8,128)(2,1)}, u32[]{:S(2)}) copy-start(bf16[1024,256]{1,0:T(8,128)(2,1)} %copy-done.19) | copy-start | bytes 1572868
  134.0 22.4 %copy-start.17 = (bf16[1024,256]{1,0:T(8,128)(2,1)S(1)}, bf16[1024,256]{1,0:T(8,128)(2,1)}, u32[]{:S(2)}) copy-start(bf16[1024,256]{1,0:T(8,128)(2,1)} %get-tuple-element.70.refs_5_.refs_1_) | copy-start | bytes 1572868
  (19 other events, 67.8 us)

commit v10 on v8

--- a/solution.py
+++ b/solution.py
@@ -156,32 +156,32 @@
     return jnp.concatenate([first_ref[...], second_ref[...]], axis=1).astype(BF16)
 
 
-def rows_kernel(ids_ref, first_ref, second_ref, now_ref, *refs):
-    later, (held, left) = refs[: STEPS - 1], refs[STEPS - 1 :]
+def rows_kernel(steps, ids_ref, first_ref, second_ref, *refs):
+    outs, (held, left) = refs[: len(steps)], refs[len(steps) :]
     pair = pair_of(first_ref, second_ref)
     copies = []
-    for step in range(1, STEPS):
-        choose(ids_ref, step, pair, held.at[step - 1])
-        copies.append(pltpu.make_async_copy(held.at[step - 1], later[step - 1], left.at[step - 1]))
+    for place, step in enumerate(steps):
+        choose(ids_ref, step, pair, held.at[place])
+        copies.append(pltpu.make_async_copy(held.at[place], outs[place], left.at[place]))
         copies[-1].start()
-    choose(ids_ref, 0, pair, now_ref)
     for copy in copies:
         copy.wait()
 
 
-def chosen_rows(ids, first, second):
+def chosen_rows(ids, first, second, steps):
     return pl.pallas_call(
-        rows_kernel,
+        functools.partial(rows_kernel, steps),
         in_specs=[pl.BlockSpec(memory_space=pltpu.VMEM)] * 3,
-        out_shape=[shaped(TOKENS, WIDE, dtype=BF16)] * STEPS,
-        out_specs=[pl.BlockSpec(memory_space=pltpu.VMEM)]
-        + [pl.BlockSpec(memory_space=pltpu.HBM)] * (STEPS - 1),
+        out_shape=[shaped(TOKENS, WIDE, dtype=BF16)] * len(steps),
+        out_specs=[pl.BlockSpec(memory_space=pltpu.HBM)] * len(steps),
         scratch_shapes=[
-            pltpu.VMEM((STEPS - 1, TOKENS, WIDE), BF16),
-            pltpu.SemaphoreType.DMA((STEPS - 1,)),
+            pltpu.VMEM((len(steps), TOKENS, WIDE), BF16),
+            pltpu.SemaphoreType.DMA((len(steps),)),
         ],
         cost_estimate=pl.CostEstimate(
-            flops=2 * STEPS * TOKENS * TABLE * WIDE, bytes_accessed=4 * MIB, transcendentals=0
+            flops=2 * len(steps) * TOKENS * TABLE * WIDE,
+            bytes_accessed=len(steps) * MIB,
+            transcendentals=0,
         ),
         compiler_params=pltpu.CompilerParams(vmem_limit_bytes=54 * MIB),
     )(ids, first, second)
@@ -350,10 +350,16 @@
             upward, pairs[hop - 2] = lax.optimization_barrier((upward, pairs[hop - 2]))
         upward = lax.ppermute(upward, CZY, UP)
         downward = lax.ppermute(downward, CZY, DOWN)
-        pairs.append(chosen_rows(ids, held, upward))
+        steps = range(STEPS // 2 if hop == 1 else STEPS)
+        pairs.append(chosen_rows(ids, held, upward, tuple(steps)))
+        if hop == 1:
+            second = (held, upward)
         held = downward
     upward, pairs[1] = lax.optimization_barrier((upward, pairs[1]))
     opposite = lax.ppermute(upward, CZY, UP)
+    rest = chosen_rows(ids, *second, tuple(range(STEPS // 2, STEPS)))
+    pairs[2], rest = lax.optimization_barrier((pairs[2], rest))
+    pairs[1] = [*pairs[1], *rest]
 
     start = kernel_call(
         states_kernel, shaped(SIDE, 3 * COLS, LANES), weight, first_moment[0], second_moment[0]

time: 238 us -> 239 us (level)
  Pallas kernels: 33.7 us -> 36.4 us
  waiting for transfers between devices: 11.3 us -> 8.78 us
    pallas_call x3 -> x4, Pallas kernels: 17.5 us -> 20.2 us  [chosen_rows(): pl.pallas_call(functools.partial(rows_kernel, steps), in_specs=[pl.BlockS...]
    ppermute x1, waiting for transfers between devices: 2.53 us -> 0.01 us  [on_device(): opposite = lax.ppermute(upward, CZY, UP)]
  transfers between devices with their start and end apart: 8 -> 8, of which waited for: 3 -> 2; matrix products, arithmetic and copies ran while one was open for 0% -> 0% of each run, Pallas kernels for 9% -> 10%
where the time goes in v10:
time: 239 us; the launch traced here: 238 us
  blocking collectives  155 us (65%)
  Pallas kernels  36.4 us (15%)
  starting transfers between devices  32.9 us (14%)
  waiting for transfers between devices  8.78 us (4%)
  local copies, waits for them, and re-layouts  3.25 us (1%)
    all_to_all x12, blocking collectives, exchange(): lax.all_to_all(blocks, axes, split_axis=0, concat_axis=0, tiled=True, axi...  155 us
    pallas_call x4, Pallas kernels, chosen_rows(): pl.pallas_call(functools.partial(rows_kernel, steps), in_specs=[pl.BlockS...  20.2 us
    ppermute x3, starting transfers between devices, on_device(): downward = lax.ppermute(downward, CZY, DOWN)  18 us
    pallas_call x15, Pallas kernels, kernel_call(): pl.pallas_call(body, in_specs=in_specs, out_shape=out_shapes, compiler_pa...  14.2 us
    ppermute x3, waiting for transfers between devices, on_device(): upward = lax.ppermute(upward, CZY, UP)  8.76 us
    ppermute x3, starting transfers between devices, on_device(): upward = lax.ppermute(upward, CZY, UP)  8.65 us
  transfers between devices with their start and end apart: 8, of which 2 were waited for; matrix products, arithmetic and copies ran while one was open for 0% of the time, Pallas kernels for 10%

profile of v10, /device:TPU:1, one launch (start us, length us, event | category | flops | bytes accessed | tf_op | source)
XLA Modules:
  0.0 238.2 jit_solution(13391330879508190643)
XLA Ops:
  2.1 4.8 %collective-permute-start = (f32[1536,128]{1,0:T(8,128)S(1)}, f32[1536,128]{1,0:T(8,128)}, u32[]{:S(2)}, u32[]{:S(2)}) collective-permute-start(f32[1536,128]{1,0:T(8,128)S(1)} %shard_map.84.first_ref), channel_id=1, source_target_pairs={{0,1},{1,2},{2,3},{3,4},{4,5},{5,6},{6,7},{7,0},{8,9},{9,10},{10,1... | collective-permute-start | bytes 2359304 | tf_op jit(solution)/shard_map/ppermute | solution.py:351
  7.0 8.6 %collective-permute-start.3 = (f32[1536,128]{1,0:T(8,128)S(1)}, f32[1536,128]{1,0:T(8,128)S(1)}, u32[]{:S(2)}, u32[]{:S(2)}) collective-permute-start(f32[1536,128]{1,0:T(8,128)S(1)} %shard_map.84.first_ref), channel_id=1, source_target_pairs={{0,7},{1,0},{2,1},{3,2},{4,3},{5,4},{6,5},{7,6},{8,15},{9,8},{10,9... | collective-permute-start | bytes 2359304 | tf_op jit(solution)/shard_map/ppermute | solution.py:352
  15.6 7.8 %collective-permute-done.second_ref = f32[1536,128]{1,0:T(8,128)} collective-permute-done((f32[1536,128]{1,0:T(8,128)S(1)}, f32[1536,128]{1,0:T(8,128)}, u32[]{:S(2)}, u32[]{:S(2)}) %collective-permute-start) | collective-permute-done | bytes 786464 | tf_op jit(solution)/shard_map/ppermute | solution.py:351
  26.4 4.7 %collective-permute-start.4 = (f32[1536,128]{1,0:T(8,128)S(1)}, f32[1536,128]{1,0:T(8,128)}, u32[]{:S(2)}, u32[]{:S(2)}) collective-permute-start(f32[1536,128]{1,0:T(8,128)S(1)} %collective-permute-done.3.first_ref), channel_id=1, source_target_pairs={{0,7},{1,0},{2,1},{3,2},{4,3},{5,4},{6,5},{7,6},{8,15},{9,8},{10,9... | collective-permute-start | bytes 2359304 | tf_op jit(solution)/shard_map/ppermute | solution.py:352
  31.2 5.8 %shard_map.85 = (bf16[1024,256]{1,0:T(8,128)(2,1)}, bf16[1024,256]{1,0:T(8,128)(2,1)}, bf16[1024,256]{1,0:T(8,128)(2,1)}, bf16[1024,256]{1,0:T(8,128)(2,1)}) custom-call(f32[1024,4]{1,0:T(8,128)} %convert_bitcast_fusion.ids_ref, f32[1536,128]{1,0:T(8,128)} %copy-done.15, f32[1536,128]{1,0:T(8,128)} %collective-permute-done.second_ref), custom_call_target="tpu_custom_call" | custom-call | flops 3221225472 | bytes 4194304 | tf_op jit(solution)/shard_map/pallas_call | solution.py:172
  40.9 4.2 %all-to-all-start = ((f32[8,144,128]{2,1,0:T(8,128)}), f32[8,144,128]{2,1,0:T(8,128)S(1)}, u32[]{:S(2)}, u32[]{:S(2)}) async-start(f32[8,144,128]{2,1,0:T(8,128)} %shard_map.82), calls=%async_computation | async-start | bytes 1179648 | tf_op jit(solution)/shard_map/all_to_all | solution.py:53
  45.1 4.7 %collective-permute-start.5 = (f32[1536,128]{1,0:T(8,128)}, f32[1536,128]{1,0:T(8,128)S(1)}, u32[]{:S(2)}, u32[]{:S(2)}) collective-permute-start(f32[1536,128]{1,0:T(8,128)} %collective-permute-done.4.first_ref), channel_id=1, source_target_pairs={{0,7},{1,0},{2,1},{3,2},{4,3},{5,4},{6,5},{7,6},{8,15},{9,8},{10,9... | collective-permute-start | bytes 2359304 | tf_op jit(solution)/shard_map/ppermute | solution.py:352
  49.8 4.2 %shard_map.86 = (bf16[1024,256]{1,0:T(8,128)(2,1)}, bf16[1024,256]{1,0:T(8,128)(2,1)}) custom-call(f32[1024,4]{1,0:T(8,128)} %convert_bitcast_fusion.ids_ref, f32[1536,128]{1,0:T(8,128)} %copy-done.24, f32[1536,128]{1,0:T(8,128)} %collective-permute-done.1.second_ref), custom_call_target="tpu_custom_call" | custom-call | flops 1610612736 | bytes 2097152 | tf_op jit(solution)/shard_map/pallas_call | solution.py:172
  54.1 2.1 collective-permute-start.6
  58.0 4.2 %shard_map.88 = (bf16[1024,256]{1,0:T(8,128)(2,1)}, bf16[1024,256]{1,0:T(8,128)(2,1)}) custom-call(f32[1024,4]{1,0:T(8,128)} %convert_bitcast_fusion.ids_ref, f32[1536,128]{1,0:T(8,128)} %copy-done.24, f32[1536,128]{1,0:T(8,128)} %collective-permute-done.1.second_ref), custom_call_target="tpu_custom_call" | custom-call | flops 1610612736 | bytes 2097152 | tf_op jit(solution)/shard_map/pallas_call | solution.py:172
  62.2 5.9 %shard_map.87 = (bf16[1024,256]{1,0:T(8,128)(2,1)}, bf16[1024,256]{1,0:T(8,128)(2,1)}, bf16[1024,256]{1,0:T(8,128)(2,1)}, bf16[1024,256]{1,0:T(8,128)(2,1)}) custom-call(f32[1024,4]{1,0:T(8,128)} %convert_bitcast_fusion.ids_ref, f32[1536,128]{1,0:T(8,128)} %collective-permute-done.4.first_ref, f32[1536,128]{1,0:T(8,128)} %collective-permute-done.2.second_ref), custom_call_target="tpu_custom_call" | custom-call | flops 3221225472 | bytes 4194304 | tf_op jit(solution)/shard_map/pallas_call | solution.py:172
  70.4 4.8 %shard_map.90 = (bf16[1024,256]{1,0:T(8,128)(2,1)S(1)}, bf16[1024,256]{1,0:T(8,128)(2,1)S(1)}, bf16[1024,256]{1,0:T(8,128)(2,1)S(1)}, bf16[1024,256]{1,0:T(8,128)(2,1)S(1)}, f32[8,48,128]{2,1,0:T(8,128)S(1)}) custom-call(f32[1024,4]{1,0:T(8,128)S(1)} %copy-done.1, f32[8,144,128]{2,1,0:T(8,128)S(1)} %get-tuple-element.60.states_ref.w_ref, ...), custom_call_target="tpu_custom_call" | custom-call | tf_op jit(solution)/shard_map/pallas_call | solution.py:63
  75.2 15.4 %all_to_all.65.parts_ref = f32[8,48,128]{2,1,0:T(8,128)S(1)} all-to-all(f32[8,48,128]{2,1,0:T(8,128)S(1)} %get-tuple-element.63), channel_id=1, replica_groups={{0,8,16,24,32,40,48,56},{1,9,17,25,33,41,49,57},{2,10,18,26,34,42,50,58..., dimensions={0} | all-to-all | bytes 393216 | tf_op jit(solution)/shard_map/all_to_all | solution.py:53
  90.6 11.2 %all_to_all.66.error_ref = f32[8,48,128]{2,1,0:T(8,128)S(1)} all-to-all(f32[8,48,128]{2,1,0:T(8,128)S(1)} %shard_map.91), channel_id=1, replica_groups={{0,8,16,24,32,40,48,56},{1,9,17,25,33,41,49,57},{2,10,18,26,34,42,50,58..., dimensions={0} | all-to-all | bytes 393216 | tf_op jit(solution)/shard_map/all_to_all | solution.py:53
  103.5 11.2 %all_to_all.67.parts_ref = f32[8,48,128]{2,1,0:T(8,128)S(1)} all-to-all(f32[8,48,128]{2,1,0:T(8,128)S(1)} %get-tuple-element.69), channel_id=1, replica_groups={{0,8,16,24,32,40,48,56},{1,9,17,25,33,41,49,57},{2,10,18,26,34,42,50,58..., dimensions={0} | all-to-all | bytes 393216 | tf_op jit(solution)/shard_map/all_to_all | solution.py:53
  114.7 11.2 %all_to_all.68.error_ref = f32[8,48,128]{2,1,0:T(8,128)S(1)} all-to-all(f32[8,48,128]{2,1,0:T(8,128)S(1)} %shard_map.93), channel_id=1, replica_groups={{0,8,16,24,32,40,48,56},{1,9,17,25,33,41,49,57},{2,10,18,26,34,42,50,58..., dimensions={0} | all-to-all | bytes 393216 | tf_op jit(solution)/shard_map/all_to_all | solution.py:53
  127.5 11.2 %all_to_all.69.parts_ref = f32[8,48,128]{2,1,0:T(8,128)S(1)} all-to-all(f32[8,48,128]{2,1,0:T(8,128)S(1)} %get-tuple-element.75), channel_id=1, replica_groups={{0,8,16,24,32,40,48,56},{1,9,17,25,33,41,49,57},{2,10,18,26,34,42,50,58..., dimensions={0} | all-to-all | bytes 393216 | tf_op jit(solution)/shard_map/all_to_all | solution.py:53
  138.7 11.2 %all_to_all.70.error_ref = f32[8,48,128]{2,1,0:T(8,128)S(1)} all-to-all(f32[8,48,128]{2,1,0:T(8,128)S(1)} %shard_map.95), channel_id=1, replica_groups={{0,8,16,24,32,40,48,56},{1,9,17,25,33,41,49,57},{2,10,18,26,34,42,50,58..., dimensions={0} | all-to-all | bytes 393216 | tf_op jit(solution)/shard_map/all_to_all | solution.py:53
  151.5 11.0 %all_to_all.71.parts_ref = f32[8,48,128]{2,1,0:T(8,128)S(1)} all-to-all(f32[8,48,128]{2,1,0:T(8,128)S(1)} %get-tuple-element.81), channel_id=1, replica_groups={{0,8,16,24,32,40,48,56},{1,9,17,25,33,41,49,57},{2,10,18,26,34,42,50,58..., dimensions={0} | all-to-all | bytes 393216 | tf_op jit(solution)/shard_map/all_to_all | solution.py:53
  162.6 11.3 %all_to_all.72.error_ref = f32[8,48,128]{2,1,0:T(8,128)S(1)} all-to-all(f32[8,48,128]{2,1,0:T(8,128)S(1)} %shard_map.97), channel_id=1, replica_groups={{0,8,16,24,32,40,48,56},{1,9,17,25,33,41,49,57},{2,10,18,26,34,42,50,58..., dimensions={0} | all-to-all | bytes 393216 | tf_op jit(solution)/shard_map/all_to_all | solution.py:53
  175.0 13.9 %all_to_all.73.parts_ref = f32[8,48,128]{2,1,0:T(8,128)S(1)} all-to-all(f32[8,48,128]{2,1,0:T(8,128)S(1)} %shard_map.98), channel_id=1, replica_groups={{0,1,2,3,4,5,6,7},{8,9,10,11,12,13,14,15},{16,17,18,19,20,21,22,23},{24..., dimensions={0} | all-to-all | bytes 393216 | tf_op jit(solution)/shard_map/all_to_all | solution.py:53
  189.0 25.6 %all_to_all.74.updates_ref = f32[8,16,384]{2,1,0:T(8,128)S(1)} all-to-all(f32[8,16,384]{2,1,0:T(8,128)S(1)} %shard_map.99), channel_id=1, replica_groups=mesh['x'=4,'core'=2,'z'=8,'y'=8] {'x','core'}, dimensions={0} | all-to-all | bytes 393216 | tf_op jit(solution)/shard_map/all_to_all | solution.py:53
  214.8 7.9 %all_to_all.75.parts_ref = f32[8,1,128]{2,1,0:T(1,128)S(1)} all-to-all(f32[8,1,128]{2,1,0:T(1,128)S(1)} %shard_map.100), channel_id=1, replica_groups=mesh['x'=4,'core'=2,'z'=8,'y'=8] {'x','core'}, dimensions={0} | all-to-all | bytes 8192 | tf_op jit(solution)/shard_map/all_to_all | solution.py:53
  222.7 14.6 %all_to_all.76.parts_ref = f32[64,1,128]{2,1,0:T(1,128)S(1)} all-to-all(f32[64,1,128]{2,1,0:T(1,128)S(1)} %shard_map.101), channel_id=1, replica_groups=mesh['x'=4,'core'=2,'z'=8,'y'=8] {'z','y'}, dimensions={0} | all-to-all | bytes 65536 | tf_op jit(solution)/shard_map/all_to_all | solution.py:53
  (78 shorter events, 20.4 us)
Async XLA Ops:
  1.9 23.5 %copy-start.23 = (s32[1,4,1024]{2,1,0:T(4,128)S(1)}, s32[1,4,1024]{2,1,0:T(4,128)}, u32[]{:S(2)}) copy-start(s32[1,4,1024]{2,1,0:T(4,128)} %param.11) | copy-start | bytes 49156
  2.1 24.3 %copy-start.15 = (f32[1536,128]{1,0:T(8,128)}, f32[1536,128]{1,0:T(8,128)S(1)}, u32[]{:S(2)}) copy-start(f32[1536,128]{1,0:T(8,128)S(1)} %shard_map.84.first_ref) | copy-start | bytes 2359300
  2.1 21.3 %collective-permute-start = (f32[1536,128]{1,0:T(8,128)S(1)}, f32[1536,128]{1,0:T(8,128)}, u32[]{:S(2)}, u32[]{:S(2)}) collective-permute-start(f32[1536,128]{1,0:T(8,128)S(1)} %shard_map.84.first_ref), channel_id=1, source_target_pairs={{0,1},{1,2},{2,3},{3,4},{4,5},{5,6},{6,7},{7,0},{8,9},{9,10},{10,1... | collective-permute-start | bytes 2359304 | tf_op jit(solution)/shard_map/ppermute | solution.py:351
  7.0 19.5 %collective-permute-start.3 = (f32[1536,128]{1,0:T(8,128)S(1)}, f32[1536,128]{1,0:T(8,128)S(1)}, u32[]{:S(2)}, u32[]{:S(2)}) collective-permute-start(f32[1536,128]{1,0:T(8,128)S(1)} %shard_map.84.first_ref), channel_id=1, source_target_pairs={{0,7},{1,0},{2,1},{3,2},{4,3},{5,4},{6,5},{7,6},{8,15},{9,8},{10,9... | collective-permute-start | bytes 2359304 | tf_op jit(solution)/shard_map/ppermute | solution.py:352
  23.4 14.5 %collective-permute-start.1 = (f32[1536,128]{1,0:T(8,128)}, f32[1536,128]{1,0:T(8,128)}, u32[]{:S(2)}, u32[]{:S(2)}) collective-permute-start(f32[1536,128]{1,0:T(8,128)} %collective-permute-done.second_ref), channel_id=1, source_target_pairs={{0,1},{1,2},{2,3},{3,4},{4,5},{5,6},{6,7},{7,0},{8,9},{9,10},{10,1... | collective-permute-start | bytes 2359304 | tf_op jit(solution)/shard_map/ppermute | solution.py:351
  26.4 13.5 %copy-start.20 = (bf16[128,384]{1,0:T(8,128)(2,1)S(1)}, bf16[128,384]{1,0:T(8,128)(2,1)}, u32[]{:S(2)}) copy-start(bf16[128,384]{1,0:T(8,128)(2,1)} %w_ref.1) | copy-start | bytes 294916
  26.4 13.5 %copy-start.21 = (bf16[1,128,384]{2,1,0:T(8,128)(2,1)S(1)}, bf16[1,128,384]{2,1,0:T(8,128)(2,1)}, u32[]{:S(2)}) copy-start(bf16[1,128,384]{2,1,0:T(8,128)(2,1)} %param.9) | copy-start | bytes 294916
  26.4 13.5 %copy-start.22 = (bf16[1,128,384]{2,1,0:T(8,128)(2,1)S(1)}, bf16[1,128,384]{2,1,0:T(8,128)(2,1)}, u32[]{:S(2)}) copy-start(bf16[1,128,384]{2,1,0:T(8,128)(2,1)} %param.10) | copy-start | bytes 294916
  26.4 18.7 %collective-permute-start.4 = (f32[1536,128]{1,0:T(8,128)S(1)}, f32[1536,128]{1,0:T(8,128)}, u32[]{:S(2)}, u32[]{:S(2)}) collective-permute-start(f32[1536,128]{1,0:T(8,128)S(1)} %collective-permute-done.3.first_ref), channel_id=1, source_target_pairs={{0,7},{1,0},{2,1},{3,2},{4,3},{5,4},{6,5},{7,6},{8,15},{9,8},{10,9... | collective-permute-start | bytes 2359304 | tf_op jit(solution)/shard_map/ppermute | solution.py:352
  37.9 16.1 %collective-permute-start.2 = (f32[1536,128]{1,0:T(8,128)}, f32[1536,128]{1,0:T(8,128)}, u32[]{:S(2)}, u32[]{:S(2)}) collective-permute-start(f32[1536,128]{1,0:T(8,128)} %collective-permute-done.1.second_ref), channel_id=1, source_target_pairs={{0,1},{1,2},{2,3},{3,4},{4,5},{5,6},{6,7},{7,0},{8,9},{9,10},{10,1... | collective-permute-start | bytes 2359304 | tf_op jit(solution)/shard_map/ppermute | solution.py:351
  40.9 27.2 %all-to-all-start = ((f32[8,144,128]{2,1,0:T(8,128)}), f32[8,144,128]{2,1,0:T(8,128)S(1)}, u32[]{:S(2)}, u32[]{:S(2)}) async-start(f32[8,144,128]{2,1,0:T(8,128)} %shard_map.82), calls=%async_computation | async-start | bytes 1179648 | tf_op jit(solution)/shard_map/all_to_all | solution.py:53
  45.1 11.2 %copy-start = (f32[1024,4]{1,0:T(8,128)S(1)}, f32[1024,4]{1,0:T(8,128)}, u32[]{:S(2)}) copy-start(f32[1024,4]{1,0:T(8,128)} %convert_bitcast_fusion.ids_ref) | copy-start | bytes 49156
  45.1 11.2 %copy-start.16 = (bf16[1024,384]{1,0:T(8,128)(2,1)S(1)}, bf16[1024,384]{1,0:T(8,128)(2,1)}, u32[]{:S(2)}) copy-start(bf16[1024,384]{1,0:T(8,128)(2,1)} %shared_ref.2) | copy-start | bytes 2359300
  45.1 25.3 %collective-permute-start.5 = (f32[1536,128]{1,0:T(8,128)}, f32[1536,128]{1,0:T(8,128)S(1)}, u32[]{:S(2)}, u32[]{:S(2)}) collective-permute-start(f32[1536,128]{1,0:T(8,128)} %collective-permute-done.4.first_ref), channel_id=1, source_target_pairs={{0,7},{1,0},{2,1},{3,2},{4,3},{5,4},{6,5},{7,6},{8,15},{9,8},{10,9... | collective-permute-start | bytes 2359304 | tf_op jit(solution)/shard_map/ppermute | solution.py:352
  54.1 16.3 %collective-permute-start.6 = (f32[1536,128]{1,0:T(8,128)}, f32[1536,128]{1,0:T(8,128)}, u32[]{:S(2)}, u32[]{:S(2)}) collective-permute-start(f32[1536,128]{1,0:T(8,128)} %collective-permute-done.2.second_ref), channel_id=1, source_target_pairs={{0,1},{1,2},{2,3},{3,4},{4,5},{5,6},{6,7},{7,0},{8,9},{9,10},{10,1... | collective-permute-start | bytes 2359304 | tf_op jit(solution)/shard_map/ppermute | solution.py:359
  70.4 31.4 %copy-start.9 = (bf16[1024,256]{1,0:T(8,128)(2,1)S(1)}, bf16[1024,256]{1,0:T(8,128)(2,1)}, u32[]{:S(2)}) copy-start(bf16[1024,256]{1,0:T(8,128)(2,1)} %get-tuple-element.67.refs_6_.refs_2_) | copy-start | bytes 1572868
  70.4 31.4 %copy-start.11 = (bf16[1024,256]{1,0:T(8,128)(2,1)S(1)}, bf16[1024,256]{1,0:T(8,128)(2,1)}, u32[]{:S(2)}) copy-start(bf16[1024,256]{1,0:T(8,128)(2,1)} %get-tuple-element.59.refs_2_) | copy-start | bytes 1572868
  75.2 26.6 %copy-start.5 = (bf16[1024,256]{1,0:T(8,128)(2,1)S(1)}, bf16[1024,256]{1,0:T(8,128)(2,1)}, u32[]{:S(2)}) copy-start(bf16[1024,256]{1,0:T(8,128)(2,1)} %get-tuple-element.66.refs_5_.refs_1_) | copy-start | bytes 1572868
  90.6 11.2 %copy-start.3 = (bf16[1024,256]{1,0:T(8,128)(2,1)S(1)}, bf16[1024,256]{1,0:T(8,128)(2,1)}, u32[]{:S(2)}) copy-start(bf16[1024,256]{1,0:T(8,128)(2,1)} %get-tuple-element.65.refs_4_.refs_0_) | copy-start | bytes 1572868
  101.8 24.0 %copy-start.8 = (bf16[1024,256]{1,0:T(8,128)(2,1)S(1)}, bf16[1024,256]{1,0:T(8,128)(2,1)}, u32[]{:S(2)}) copy-start(bf16[1024,256]{1,0:T(8,128)(2,1)} %get-tuple-element.73.refs_6_.refs_2_) | copy-start | bytes 1572868
  103.5 22.4 %copy-start.7 = (bf16[1024,256]{1,0:T(8,128)(2,1)S(1)}, bf16[1024,256]{1,0:T(8,128)(2,1)}, u32[]{:S(2)}) copy-start(bf16[1024,256]{1,0:T(8,128)(2,1)} %get-tuple-element.72.refs_5_.refs_1_) | copy-start | bytes 1572868
  114.6 11.2 %copy-start.2 = (bf16[1024,256]{1,0:T(8,128)(2,1)S(1)}, bf16[1024,256]{1,0:T(8,128)(2,1)}, u32[]{:S(2)}) copy-start(bf16[1024,256]{1,0:T(8,128)(2,1)} %get-tuple-element.71.refs_4_.refs_0_) | copy-start | bytes 1572868
  125.8 24.0 %copy-start.14 = (bf16[1024,256]{1,0:T(8,128)(2,1)S(1)}, bf16[1024,256]{1,0:T(8,128)(2,1)}, u32[]{:S(2)}) copy-start(bf16[1024,256]{1,0:T(8,128)(2,1)} %get-tuple-element.79.refs_6_.refs_2_) | copy-start | bytes 1572868
  127.5 22.4 %copy-start.13 = (bf16[1024,256]{1,0:T(8,128)(2,1)S(1)}, bf16[1024,256]{1,0:T(8,128)(2,1)}, u32[]{:S(2)}) copy-start(bf16[1024,256]{1,0:T(8,128)(2,1)} %get-tuple-element.78.refs_5_.refs_1_) | copy-start | bytes 1572868
  (9 other events, 50.1 us)
